TPU v7x, 32 devices: a whole 2x2x4 slice. The times are simulated.
32 devices in a mesh: dp: 4 (over y, core), tensor: 8 (over z, x).
Axes of the slice: x: 2, y: 2, z: 4, core: 2. Of those that a mesh axis runs over, the one named last changes fastest.
Arguments:
- hidden: bfloat16 [640, 16384], P(None, ('dp', 'tensor')), may hold values from -100 to 100
- gain: bfloat16 [1, 16384], P(None, ('dp', 'tensor')), may hold values from 0.5 to 2, as said below
- head_weight: bfloat16 [16384, 65536], P('dp', 'tensor'), may hold values from -3 to 3
- draft_probs: float32 [640, 65536], P(('dp', 'tensor')), may hold values from 0 to 1, as said below
- draft_ids: int32 [640], P('dp'), may hold values from 0 to 65535
- reject_at: int32 [128], P('dp'), may hold values from 0 to 4
Outputs:
- token_logprob: float32 [640], P('dp')
- residual: float32 [128, 65536], P('dp', 'tensor')
Inputs may be any that keep to these rules, and one draw needn't show every extreme that they name: `draft_probs`: every row is a probability distribution over the 65536 entries that sums to one. `gain`: positive.
All inputs are finite; a program needn't handle non-finite values.
Results may differ from a plain program's by a relative error of at most 0.0005.
The roundings to bfloat16 on the way count: a program that leaves them out, or rounds other values in their place, can miss the bound.
Values may be sent and summed in bfloat16 or wider, within the bound.
No kernel may reach another device: no remote copies, remote signals or barrier semaphores. Data moves between devices by JAX's collectives and lax.ppermute only.
A program may use at most 192 MiB of HBM per device.

v0:
```python
import jax
import jax.numpy as jnp
from jax import lax
from jax.sharding import PartitionSpec as P

D = 16384
VOCAB = 65536
POS = 5


EPS = 1e-05


def shards(hidden, gain, head_weight, draft_probs, draft_ids, reject_at):
    raw, gains = (
        lax.all_gather(hidden, "tensor", axis=1, tiled=True),
        lax.all_gather(gain, "tensor", axis=1, tiled=True),
    )
    values = raw.astype(jnp.float32)
    squares = lax.psum(jnp.sum(values * values, axis=1), "dp")
    normed = (values * lax.rsqrt(squares / D + EPS)[:, None] * gains.astype(jnp.float32)).astype(
        jnp.bfloat16
    )
    logits = lax.psum_scatter(
        jnp.dot(normed, head_weight, preferred_element_type=jnp.float32),
        "dp",
        scatter_dimension=0,
        tiled=True,
    )
    width = logits.shape[1]
    columns = lax.broadcasted_iota(jnp.int32, (1, width), 1) + lax.axis_index("tensor") * width
    local_max = jnp.max(logits, axis=1)
    local_pick = jnp.sum(jnp.where(columns == draft_ids[:, None], logits, 0.0), axis=1)
    top = lax.pmax(local_max, "tensor")
    local_total = jnp.sum(jnp.exp(logits - top[:, None]), axis=1)
    total, picked = lax.psum((local_total, local_pick), "tensor")
    logz = top + jnp.log(total)
    token_logprob = picked - logz
    requests = reject_at.shape[0]
    where_at = reject_at[:, None, None]
    chosen = jnp.take_along_axis(logits.reshape(requests, POS, width), where_at, axis=1)[:, 0]
    chosen_logz = jnp.take_along_axis(logz.reshape(requests, POS), reject_at[:, None], axis=1)[:, 0]
    moved = lax.all_to_all(draft_probs, "tensor", split_axis=1, concat_axis=0, tiled=True)
    drafts = jnp.take_along_axis(moved.reshape(requests, POS, width), where_at, axis=1)[:, 0]
    target = jnp.exp(chosen - chosen_logz[:, None])
    kept = jnp.maximum(target - drafts, 0.0)
    mass = lax.psum(jnp.sum(kept, axis=1), "tensor")
    residual = VOCAB * kept / mass[:, None]
    return (token_logprob, residual)


def solution(mesh):
    return jax.shard_map(
        shards,
        mesh=mesh,
        in_specs=(
            P(None, ("dp", "tensor")),
            P(None, ("dp", "tensor")),
            P("dp", "tensor"),
            P(("dp", "tensor"), None),
            P("dp"),
            P("dp"),
        ),
        out_specs=(P("dp"), P("dp", "tensor")),
        check_vma=False,
    )
```

profile of v0, /device:TPU:0, one launch (start us, length us, event | category | flops | bytes accessed | tf_op | source)
XLA Modules:
  0.0 426.0 jit_solution(10375910509984115631)
XLA Ops:
  7.2 0.7 all-gather.2.cloned.1.call-update
  7.9 28.2 %all_gather.7 = bf16[1,4096]{1,0:T(2,128)(2,1)S(1)} all-gather(bf16[1,512]{1,0:T(2,128)(2,1)} %param.9), channel_id=1, replica_groups=mesh['dp'=4,'tensor'=8] {'tensor'}, dimensions={1}, use_global_device_ids=true | all-gather | bytes 9216 | tf_op jit(solution)/shard_map/all_gather | solution.py:17
  36.2 63.9 %all-gather.2.cloned.1.call-done = bf16[640,4096]{1,0:T(8,128)(2,1)} async-done(((bf16[640,512]{1,0:T(8,128)(2,1)}), bf16[640,4096]{1,0:T(8,128)(2,1)}) %all-gather.2.cloned.1.call-update) | async-done | bytes 5242896 | tf_op jit(solution)/shard_map/all_gather | solution.py:16
  100.1 3.6 fusion
  103.7 6.2 %psum.28 = f32[640]{0:T(1024)S(1)} all-reduce(f32[640]{0:T(1024)S(1)} %fusion), channel_id=1, replica_groups=mesh['dp'=4,'tensor'=8] {'dp'}, use_global_device_ids=true, to_apply=%region_1.0 | all-reduce | flops 640 | bytes 5120 | tf_op jit(solution)/shard_map/psum | solution.py:20
  109.8 51.4 %fusion.3 = f32[640,8192]{1,0:T(8,128)} fusion(bf16[4096,8192]{1,0:T(8,128)(2,1)} %param.10, bf16[640,4096]{1,0:T(8,128)(2,1)} %all-gather.2.cloned.1.call-done, f32[4096]{0:T(1024)S(1)} %bitcast.62, f32[640]{0:T(1024)S(1)} %add_rsqrt_fusion), kind=kOutput, calls=%fused_computation.8 | convolution fusion | flops 42960158720 | bytes 93342208 | tf_op jit(solution)/shard_map/dot_general | solution.py:25
  161.3 6.4 %copy.12 = f32[3,8,8,8192]{3,2,1,0:T(8,128)S(1)} copy(f32[3,8,8,8192]{3,1,2,0:T(8,128)} %bitcast.61) | data formatting | bytes 12582912
  168.2 6.8 %copy.10 = f32[20,8,8192]{2,0,1:T(8,128)} copy(f32[20,8,8192]{2,1,0:T(8,128)S(1)} %slice.10) | data formatting | bytes 10485760 | tf_op jit(solution)/shard_map/all_to_all | solution.py:43
  175.0 5.2 %all-to-all-start = ((f32[20,8,8192]{2,0,1:T(8,128)}), f32[20,8,8192]{2,0,1:T(8,128)}, u32[]{:S(2)}, u32[]{:S(2)}) async-start(f32[20,8,8192]{2,0,1:T(8,128)} %copy.10), calls=%async_computation.1 | async-start | bytes 12582912 | tf_op jit(solution)/shard_map/all_to_all | solution.py:43
  180.3 137.7 %all-to-all-done = f32[20,8,8192]{2,0,1:T(8,128)} async-done(((f32[20,8,8192]{2,0,1:T(8,128)}), f32[20,8,8192]{2,0,1:T(8,128)}, u32[]{:S(2)}, u32[]{:S(2)}) %all-to-all-start) | async-done | bytes 5242912 | tf_op jit(solution)/shard_map/all_to_all | solution.py:43
  318.0 6.5 %reshape.95 = f32[32,5,8192]{2,1,0:T(8,128)} reshape(f32[8,20,8192]{2,1,0:T(8,128)} %bitcast.11) | data formatting | bytes 10485760 | tf_op jit(solution)/shard_map/reshape | solution.py:44
  324.5 8.7 %copy.11 = f32[32,5,8192]{2,0,1:T(8,128)} copy(f32[32,5,8192]{2,1,0:T(8,128)} %reshape.95) | data formatting | bytes 10485760 | tf_op jit(solution)/shard_map/reshape | solution.py:44
  333.3 2.5 gather_fusion.2
  335.8 2.8 reduce_max.9
  338.6 19.5 %pmax.7 = f32[160]{0:T(256)S(1)} all-reduce(f32[160]{0:T(256)S(1)} %reduce_max.9), channel_id=1, replica_groups=mesh['dp'=4,'tensor'=8] {'tensor'}, use_global_device_ids=true, to_apply=%region_6.7 | all-reduce | flops 160 | bytes 1280 | tf_op jit(solution)/shard_map/pmax | solution.py:34
  358.1 3.9 exponential_reduce_fusion
  362.0 17.1 %psum.30 = f32[160]{0:T(256)S(1)} all-reduce(f32[160]{0:T(256)S(1)} %get-tuple-element.3), channel_id=1, replica_groups=mesh['dp'=4,'tensor'=8] {'tensor'}, use_global_device_ids=true, to_apply=%region_8.9 | all-reduce | flops 160 | bytes 1280 | tf_op jit(solution)/shard_map/psum | solution.py:36
  379.3 0.7 gather_fusion
  380.0 6.4 %reshape.92 = f32[32,5,8192]{2,1,0:T(8,128)} reshape(f32[160,8192]{1,0:T(8,128)} %reduce-scatter.2.cloned.1.call-done) | data formatting | bytes 10485760 | tf_op jit(solution)/shard_map/reshape | solution.py:41
  386.4 8.8 %copy.9 = f32[32,5,8192]{2,0,1:T(8,128)} copy(f32[32,5,8192]{2,1,0:T(8,128)} %reshape.92) | data formatting | bytes 10485760 | tf_op jit(solution)/shard_map/reshape | solution.py:41
  395.2 2.5 gather_fusion.1
  398.1 19.1 %all-reduce = (f32[160]{0:T(256)S(1)}, f32[32]{0:T(128)S(1)}) all-reduce(f32[160]{0:T(256)S(1)} %get-tuple-element.4, f32[32]{0:T(128)S(1)} %fusion.12), channel_id=1, replica_groups=mesh['dp'=4,'tensor'=8] {'tensor'}, use_global_device_ids=true, to_apply=%region_4.5 | all-reduce | flops 192 | bytes 1536 | tf_op jit(solution)/shard_map/psum | solution.py:36
  417.3 1.4 multiply_divide_fusion
  418.6 0.6 sub.24
  (23 shorter events, 1.3 us)
Async XLA Ops:
  7.2 92.9 %all-gather.2.cloned.1.call-start = ((), (), s32[]{:S(2)}) async-start(), calls=%async_computation.2 | async-start | bytes 5898240 | tf_op jit(solution)/shard_map/all_gather | solution.py:16
  7.9 327.9 %reduce-scatter.2.cloned.1.call-start = ((), (), s32[]{:S(2)}) async-start(), calls=%async_computation.3 | async-start | bytes 26214400 | tf_op jit(solution)/shard_map/reduce_scatter | solution.py:24
  175.0 5.2 %copy-start.1 = (s32[32]{0:T(128)S(1)}, s32[32]{0:T(128)}, u32[]{:S(2)}) copy-start(s32[32]{0:T(128)} %param.13) | copy-start | bytes 388
  175.0 143.0 %all-to-all-start = ((f32[20,8,8192]{2,0,1:T(8,128)}), f32[20,8,8192]{2,0,1:T(8,128)}, u32[]{:S(2)}, u32[]{:S(2)}) async-start(f32[20,8,8192]{2,0,1:T(8,128)} %copy.10), calls=%async_computation.1 | async-start | bytes 12582912 | tf_op jit(solution)/shard_map/all_to_all | solution.py:43
  333.3 24.8 %copy-start = (s32[160]{0:T(256)S(1)}, s32[160]{0:T(256)}, u32[]{:S(2)}) copy-start(s32[160]{0:T(256)} %param.12) | copy-start | bytes 1924
Sparse Core Ops, SparseCore 0:
  10.0 90.0 all-gather.1
  161.4 151.0 reduce-scatter.1
where the time goes:
time: 427 us; the launch traced here: 426 us
  waiting for transfers between devices  202 us (47%)
  blocking collectives  90.1 us (21%)
  matrix products  51.4 us (12%)
  local copies, waits for them, and re-layouts  50 us (12%)
  between operations  14.2 us (3%)
  other arithmetic  12.8 us (3%)
  starting transfers between devices  5.27 us (1%)
    all_to_all x1, waiting for transfers between devices, shards(): lax.all_to_all(draft_probs, 'tensor', split_axis=1, concat_axis=0, tiled=...  138 us
    all_gather x1, waiting for transfers between devices, shards(): lax.all_gather(hidden, 'tensor', axis=1, tiled=True)  63.9 us
    dot_general x1, matrix products, shards(): jnp.dot(normed, head_weight, preferred_element_type=jnp.float32)  51.4 us
    psum x2, blocking collectives, shards(): total, picked = lax.psum((local_total, local_pick), 'tensor')  36.3 us
    all_gather x1, blocking collectives, shards(): lax.all_gather(gain, 'tensor', axis=1, tiled=True)  28.2 us
    pmax x1, blocking collectives, shards(): top = lax.pmax(local_max, 'tensor')  19.5 us
    reshape x2, local copies, waits for them, and re-layouts, shards(): moved.reshape(requests, POS, width)  15.2 us
    reshape x2, local copies, waits for them, and re-layouts, shards(): logits.reshape(requests, POS, width)  15.2 us
  transfers between devices with their start and end apart: 3, of which 2 were waited for; matrix products, arithmetic and copies ran while one was open for 7% of the time, Pallas kernels for 0%

commit v1 on v0

v1 whole, which is shorter than its diff:
```python
import functools

import jax
import jax.numpy as jnp
from jax import lax
from jax.experimental import pallas as pl
from jax.experimental.pallas import tpu as pltpu
from jax.sharding import PartitionSpec as P

EPS = 1e-05
CHUNKS = 2
PARTS = 2
TILE = 512
VMEM_LIMIT = 56 * 1024 * 1024
F32 = jnp.float32


def tree_sum(value, axis, count):
    bit = 1
    while bit < count:
        value = value + lax.ppermute(value, axis, [(i, i ^ bit) for i in range(count)])
        bit *= 2
    return value


def merge(first, second):
    top = jnp.maximum(first[0], second[0])
    total = first[1] * jnp.exp(first[0] - top) + second[1] * jnp.exp(second[0] - top)
    return jnp.stack([top, total, first[2] + second[2]])


def tree_merge(stats, axis, count):
    me = lax.axis_index(axis)
    bit = 1
    while bit < count:
        other = lax.ppermute(stats, axis, [(i, i ^ bit) for i in range(count)])
        upper = (me & bit) != 0
        stats = merge(jnp.where(upper, other, stats), jnp.where(upper, stats, other))
        bit *= 2
    return stats


def gather_pieces(piece, nz, nx):
    z = lax.axis_index("tensor") // nx

    def across(found, rows):
        out = [found]
        for k in range(1, nx):
            pairs = [(r * nx + x, r * nx + (x + k) % nx) for r in rows for x in range(nx)]
            out.append(lax.ppermute(found, "tensor", pairs))
        return out

    pieces = [(p, 0, k, z >= 0) for k, p in enumerate(across(piece, range(nz)))]
    up = down = piece
    for far in range(1, nz):
        up = lax.ppermute(
            up, "tensor", [(r * nx + x, (r + 1) * nx + x) for r in range(far - 1, nz - 1) for x in range(nx)]
        )
        down = lax.ppermute(
            down, "tensor", [(r * nx + x, (r - 1) * nx + x) for r in range(1, nz - far + 1) for x in range(nx)]
        )
        pieces += [(p, -far, k, z >= far) for k, p in enumerate(across(up, range(far, nz)))]
        pieces += [(p, far, k, z + far < nz) for k, p in enumerate(across(down, range(0, nz - far)))]
    return pieces


def prepare_kernel(count, holds, place, order, scale, gain, *refs):
    pieces, out = refs[:count], refs[count]
    rows = order.shape[0]
    width = pieces[0].shape[1]
    pick = (lax.broadcasted_iota(jnp.int32, (rows, rows), 1) == order[...]).astype(jnp.bfloat16)
    for n in range(count):

        @pl.when(holds[n] == 1)
        def _(n=n):
            at = place[n]
            normed = (pieces[n][...].astype(F32) * scale[...] * gain[pl.ds(at, 1), :]).astype(jnp.bfloat16)
            moved = jnp.dot(pick, normed, preferred_element_type=F32).astype(jnp.bfloat16)
            out[:, pl.ds(pl.multiple_of(at * width, width), width)] = moved


def prepare(pieces, holds, place, order, scale, gain, depth):
    rows = order.shape[0]
    smem = pl.BlockSpec(memory_space=pltpu.SMEM)
    vmem = pl.BlockSpec(memory_space=pltpu.VMEM)
    return pl.pallas_call(
        functools.partial(prepare_kernel, len(pieces)),
        out_shape=jax.ShapeDtypeStruct((rows, depth), jnp.bfloat16),
        in_specs=[smem, smem] + [vmem] * (3 + len(pieces)),
        out_specs=vmem,
        compiler_params=pltpu.CompilerParams(vmem_limit_bytes=VMEM_LIMIT),
        cost_estimate=pl.CostEstimate(
            flops=2 * rows * rows * depth, bytes_accessed=6 * rows * depth, transcendentals=0
        ),
        name="prepare",
    )(holds, place, order, scale, gain, *pieces)


def head_kernel(x, w, send, keep):
    half = send.shape[0]
    out = jnp.dot(x[...], w[...], preferred_element_type=F32)
    send[...] = out[:half]
    keep[...] = out[half:]


def head(normed, weight, first, width):
    rows, depth = normed.shape
    tile = min(TILE, width)
    half = jax.ShapeDtypeStruct((rows // 2, width), F32)
    spec = pl.BlockSpec((rows // 2, tile), lambda j: (0, j))
    return pl.pallas_call(
        head_kernel,
        out_shape=(half, half),
        grid=(width // tile,),
        in_specs=[
            pl.BlockSpec((rows, depth), lambda j: (0, 0)),
            pl.BlockSpec((depth, tile), lambda j: (0, first // tile + j)),
        ],
        out_specs=(spec, spec),
        compiler_params=pltpu.CompilerParams(vmem_limit_bytes=VMEM_LIMIT),
        cost_estimate=pl.CostEstimate(
            flops=2 * rows * depth * width,
            bytes_accessed=2 * depth * width + 2 * rows * depth + 4 * rows * width,
            transcendentals=0,
        ),
        name="head",
    )(normed, weight)


def encode_kernel(keep, came, coded, info):
    total = keep[...] + came[...]
    high = jnp.max(total, axis=1, keepdims=True)
    low = jnp.min(total, axis=1, keepdims=True)
    middle = 0.5 * high + 0.5 * low
    step = jnp.maximum((0.5 * high - 0.5 * low) * (1.0 / 32700.0), 1e-30)
    scaled = (total - middle) * (1.0 / step)
    coded[...] = jnp.floor(scaled + 0.5).astype(jnp.int32).astype(jnp.int16)
    lanes = lax.broadcasted_iota(jnp.int32, info.shape, 1)
    info[...] = jnp.where(lanes < info.shape[1] // 2, middle, step)


def encode(keep, came, first, count, block):
    width = keep.shape[1]
    source = pl.BlockSpec((block, width), lambda i: (first // block + i, 0))
    return pl.pallas_call(
        encode_kernel,
        out_shape=(
            jax.ShapeDtypeStruct((count, width), jnp.int16),
            jax.ShapeDtypeStruct((count, 128), F32),
        ),
        grid=(count // block,),
        in_specs=[source, source],
        out_specs=(
            pl.BlockSpec((block, width), lambda i: (i, 0)),
            pl.BlockSpec((block, 128), lambda i: (i, 0)),
        ),
        cost_estimate=pl.CostEstimate(
            flops=8 * count * width, bytes_accessed=10 * count * width, transcendentals=0
        ),
        name="encode",
    )(keep, came)


def finish_kernel(others, ids, keep, came, *refs):
    total = keep[...] + came[...]
    for n in range(others):
        info = refs[2 * n + 1][...]
        middle, step = info[:, :1], info[:, 127:]
        total = total + (refs[2 * n][...].astype(jnp.int32).astype(F32) * step + middle)
    stats = refs[2 * others]
    top = jnp.max(total, axis=1, keepdims=True)
    sums = jnp.sum(jnp.exp(total - top), axis=1, keepdims=True)
    columns = lax.broadcasted_iota(jnp.int32, total.shape, 1)
    picked = jnp.sum(jnp.where(columns == ids[...], total, 0.0), axis=1, keepdims=True)
    lanes = lax.broadcasted_iota(jnp.int32, stats.shape, 1)
    stats[...] = jnp.where(lanes == 0, top, jnp.where(lanes == 1, sums, picked))


def finish(ids, keep, came, arrived, first, block):
    count, width = ids.shape[0], keep.shape[1]
    own = pl.BlockSpec((block, width), lambda i: (first // block + i, 0))
    specs, args = [], []
    for coded, info in arrived:
        specs += [
            pl.BlockSpec((block, width), lambda i: (i, 0)),
            pl.BlockSpec((block, 128), lambda i: (i, 0)),
        ]
        args += [coded, info]
    return pl.pallas_call(
        functools.partial(finish_kernel, len(arrived)),
        out_shape=jax.ShapeDtypeStruct((count, 128), F32),
        grid=(count // block,),
        in_specs=[pl.BlockSpec((block, 1), lambda i: (i, 0)), own, own] + specs,
        out_specs=pl.BlockSpec((block, 128), lambda i: (i, 0)),
        cost_estimate=pl.CostEstimate(
            flops=12 * count * width, bytes_accessed=10 * count * width, transcendentals=count * width
        ),
        name="finish",
    )(ids, keep, came, *args)


def select_kernel(positions, at, drafts, out):
    for r in range(out.shape[1]):
        out[0, pl.ds(r, 1), :] = drafts[pl.ds(r * positions + at[r], 1), :]


def select_drafts(drafts, at, positions, count):
    rows, vocab = drafts.shape
    width = vocab // count
    return pl.pallas_call(
        functools.partial(select_kernel, positions),
        out_shape=jax.ShapeDtypeStruct((count, rows // positions, width), F32),
        grid=(count,),
        in_specs=[
            pl.BlockSpec(memory_space=pltpu.SMEM),
            pl.BlockSpec((rows, width), lambda j: (0, j)),
        ],
        out_specs=pl.BlockSpec((1, rows // positions, width), lambda j: (j, 0, 0)),
        cost_estimate=pl.CostEstimate(flops=0, bytes_accessed=5 * rows * vocab, transcendentals=0),
        name="select_drafts",
    )(at, drafts)


def shards(n_dp, n_tensor, hidden, gain, head_weight, draft_probs, draft_ids, reject_at):
    tokens, local = hidden.shape
    features = local * n_dp * n_tensor
    depth, width = head_weight.shape
    vocab = width * n_tensor
    requests = reject_at.shape[0]
    owned = draft_ids.shape[0]
    positions = owned // requests
    n_y = n_dp // 2
    nx = 1
    while nx * nx * 4 <= n_tensor:
        nx *= 2
    nz = n_tensor // nx
    d, t = lax.axis_index("dp"), lax.axis_index("tensor")
    y, c = d // 2, d % 2
    z, x = t // nx, t % nx

    values = hidden.astype(F32)
    squares = jnp.sum(values * values, axis=1)
    places = lax.dynamic_update_slice(jnp.zeros((n_dp * requests,), F32), reject_at.astype(F32), (d * requests,))
    small = jnp.concatenate([squares, places])
    short = -small.shape[0] % 1024
    small = tree_sum(jnp.pad(small, (0, short)).reshape(-1, 128), "dp", n_dp)
    flat = small.reshape(-1)
    every_at = flat[tokens : tokens + n_dp * requests].astype(jnp.int32).reshape(n_dp, requests)
    gains = lax.dynamic_update_slice(jnp.zeros((depth,), F32), gain[0].astype(F32), (t * local,))
    small = jnp.concatenate([flat[:tokens], gains])
    small = jnp.pad(small, (0, -small.shape[0] % 1024)).reshape(-1, 128)
    flat = tree_sum(small, "tensor", n_tensor).reshape(-1)
    scale = lax.rsqrt(flat[:tokens] / features + EPS)
    gains = flat[tokens : tokens + depth]

    rq = requests // CHUNKS
    rpo = rq * positions
    rows = n_dp * rpo
    by_owner = hidden.reshape(n_dp, owned, local)
    relayed = local % 128 == 0
    gathered = []
    for chunk in range(CHUNKS):
        piece = by_owner[:, chunk * rpo : (chunk + 1) * rpo].reshape(rows, local)
        if relayed:
            gathered.append(gather_pieces(piece, nz, nx))
        else:
            whole = lax.all_gather(piece, "tensor", axis=1, tiled=True)
            gathered.append([(whole, 0, 0, z >= 0)])
    piece_width = local if relayed else depth
    gains = gains.reshape(-1, piece_width)

    pad16 = rq
    rest = rpo - rq
    r_at = jnp.arange(rest) // (positions - 1)
    k_at = jnp.arange(rest) % (positions - 1)

    def rows_of(at):
        chosen = jnp.arange(rq) * positions + at
        there = at[r_at]
        return jnp.concatenate([chosen, r_at * positions + k_at + (k_at >= there)]).astype(jnp.int32)

    hops = [k % n_y for k in range(1, n_y + 1)]
    block = 16 if rest % 16 == 0 and rq % 16 == 0 else rq
    own_at = (n_y - 1) * rpo
    part = width // PARTS
    chosen_logits, chosen_stats, other_stats, own_rows = [], [], [], []
    far_chosen = {}
    core_pairs = [(i, i ^ 1) for i in range(n_dp)]

    def y_pairs(k):
        return [(i, ((i // 2 + k) % n_y) * 2 + i % 2) for i in range(n_dp)]

    for chunk in range(CHUNKS):
        order = []
        for core in (1 - c, c):
            for k in hops:
                owner = ((y + k) % n_y) * 2 + core
                at = lax.dynamic_slice(every_at, (owner, chunk * rq), (1, rq))[0]
                order.append(owner * rpo + rows_of(at))
        order = jnp.concatenate(order)[:, None].astype(jnp.int32)
        pieces = gathered[chunk]
        if relayed:
            place = jnp.stack([(z + dz) * nx + (x - k) % nx for _, dz, k, _ in pieces]).astype(jnp.int32)
        else:
            place = jnp.zeros((1,), jnp.int32)
        holds = jnp.stack([h for *_, h in pieces]).astype(jnp.int32)
        place = jnp.where(holds == 1, place, 0)
        chunk_scale = scale.reshape(n_dp, owned)[:, chunk * rpo : (chunk + 1) * rpo].reshape(rows, 1)
        normed = prepare([p for p, *_ in pieces], holds, place, order, chunk_scale, gains, depth)
        mine = rows_of(reject_at[chunk * rq : (chunk + 1) * rq])
        own_rows.append(mine + chunk * rpo)
        ids = draft_ids[chunk * rpo : (chunk + 1) * rpo][mine][:, None] - t * width
        for p in range(PARTS):
            send, keep = head(normed, head_weight, p * part, part)
            came = lax.ppermute(send, "dp", core_pairs)
            arrived, chosen_far = [], None
            for n, k in enumerate(hops[:-1]):
                at = n * rpo
                leaving = keep[at : at + rq] + came[at : at + rq]
                got = lax.ppermute(leaving, "dp", y_pairs(k))
                chosen_far = got if chosen_far is None else chosen_far + got
                coded, info = encode(keep, came, at + rq, rest, block)
                arrived.append(
                    (lax.ppermute(coded, "dp", y_pairs(k)), lax.ppermute(info, "dp", y_pairs(k)))
                )
            part_ids = ids - p * part
            logits = keep[own_at : own_at + rq] + came[own_at : own_at + rq]
            if chosen_far is not None:
                logits = logits + chosen_far
            chosen_logits.append(logits)
            top = jnp.max(logits, axis=1)
            sums = jnp.sum(jnp.exp(logits - top[:, None]), axis=1)
            columns = lax.broadcasted_iota(jnp.int32, (1, part), 1)
            picked = jnp.sum(jnp.where(columns == part_ids[:rq], logits, 0.0), axis=1)
            chosen_stats.append(jnp.stack([top, sums, picked]))
            stats = finish(part_ids[rq:], keep, came, arrived, own_at + rq, block)
            other_stats.append(stats[:, :3].T)

    def joined(stats):
        chunks = []
        for chunk in range(CHUNKS):
            merged = stats[chunk * PARTS]
            for p in range(1, PARTS):
                merged = merge(merged, stats[chunk * PARTS + p])
            chunks.append(merged)
        return jnp.concatenate(chunks, axis=1)

    of_chosen = tree_merge(joined(chosen_stats), "tensor", n_tensor)
    chosen_logz = of_chosen[0] + jnp.log(of_chosen[1])

    mine = requests // n_tensor
    at = lax.dynamic_slice(reject_at, (t * mine,), (mine,))
    drafts = select_drafts(draft_probs, at, positions, n_tensor)
    drafts, _ = lax.optimization_barrier((drafts, gathered[-1][-1][0]))
    drafts = lax.all_to_all(drafts, "tensor", split_axis=0, concat_axis=0, tiled=True).reshape(requests, width)

    logits = jnp.concatenate(
        [
            jnp.concatenate(chosen_logits[chunk * PARTS : (chunk + 1) * PARTS], axis=1)
            for chunk in range(CHUNKS)
        ]
    )
    kept = jnp.maximum(jnp.exp(logits - chosen_logz[:, None]) - drafts, 0.0)
    mass = tree_sum(jnp.sum(kept, axis=1), "tensor", n_tensor)
    residual = vocab * kept / mass[:, None]

    of_other = tree_merge(joined(other_stats), "tensor", n_tensor)
    chosen_logprob = of_chosen[2] - chosen_logz
    other_logprob = of_other[2] - (of_other[0] + jnp.log(of_other[1]))
    found = jnp.concatenate(
        [
            jnp.concatenate(
                [chosen_logprob[chunk * rq : (chunk + 1) * rq], other_logprob[chunk * rest : (chunk + 1) * rest]]
            )
            for chunk in range(CHUNKS)
        ]
    )
    where = jnp.concatenate(own_rows)
    token_logprob = jnp.sum(
        jnp.where(where[None, :] == jnp.arange(owned)[:, None], found[None, :], 0.0), axis=1
    )
    return (token_logprob, residual)


def solution(mesh):
    return jax.shard_map(
        functools.partial(shards, mesh.shape["dp"], mesh.shape["tensor"]),
        mesh=mesh,
        in_specs=(
            P(None, ("dp", "tensor")),
            P(None, ("dp", "tensor")),
            P("dp", "tensor"),
            P(("dp", "tensor"), None),
            P("dp"),
            P("dp"),
        ),
        out_specs=(P("dp"), P("dp", "tensor")),
        check_vma=False,
    )
```

time: 427 us -> 311 us (0.73)
  waiting for transfers between devices: 202 us -> 32.9 us
  Pallas kernels: 0 us -> 130 us
  blocking collectives: 90.1 us -> 0 us
  starting transfers between devices: 5.27 us -> 90.8 us
  matrix products: 51.4 us -> 0 us
  local copies, waits for them, and re-layouts: 50 us -> 31.2 us
  between operations: 14.2 us -> 1.54 us
  other arithmetic: 12.8 us -> 21.5 us
    all_to_all x1, waiting for transfers between devices: 138 us -> 0.01 us  [shards(): lax.all_to_all(drafts, 'tensor', split_axis=0, concat_axis=0, tiled=True)]
    pallas_call x0 -> x15, Pallas kernels: none -> 130 us  [the longest x4 77.1 us: head(): pl.pallas_call(head_kernel, out_shape=(half, half), grid=(width // tile,)...]
    ppermute x0 -> x56, starting transfers between devices: none -> 82.1 us  [the longest x14 25.6 us: across(): out.append(lax.ppermute(found, 'tensor', pairs))]
    all_gather x1 -> x0, waiting for transfers between devices: 63.9 us -> none  [shards(): lax.all_gather(hidden, 'tensor', axis=1, tiled=True)]
    dot_general x1 -> x0, matrix products: 51.4 us -> none  [shards(): jnp.dot(normed, head_weight, preferred_element_type=jnp.float32)]
    psum x3 -> x0, blocking collectives: 42.4 us -> none  [the longest x2 36.3 us: shards(): total, picked = lax.psum((local_total, local_pick), 'tensor')]
    ppermute x0 -> x56, waiting for transfers between devices: none -> 32.9 us  [the longest x4 13.4 us: shards(): got = lax.ppermute(leaving, 'dp', y_pairs(k))]
    all_gather x1 -> x0, blocking collectives: 28.2 us -> none  [shards(): lax.all_gather(gain, 'tensor', axis=1, tiled=True)]
  transfers between devices with their start and end apart: 3 -> 57, of which waited for: 2 -> 17; matrix products, arithmetic and copies ran while one was open for 7% -> 14% of each run, Pallas kernels for 0% -> 42%
where the time goes in v1:
time: 311 us; the launch traced here: 308 us
  Pallas kernels  130 us (42%)
  starting transfers between devices  90.8 us (29%)
  waiting for transfers between devices  32.9 us (11%)
  local copies, waits for them, and re-layouts  31.2 us (10%)
  other arithmetic  21.5 us (7%)
    pallas_call x4, Pallas kernels, head(): pl.pallas_call(head_kernel, out_shape=(half, half), grid=(width // tile,)...  77.1 us
    ppermute x14, starting transfers between devices, across(): out.append(lax.ppermute(found, 'tensor', pairs))  25.6 us
    pallas_call x4, Pallas kernels, finish(): pl.pallas_call(functools.partial(finish_kernel, len(arrived)), out_shape=...  16.4 us
    pallas_call x2, Pallas kernels, prepare(): pl.pallas_call(functools.partial(prepare_kernel, len(pieces)), out_shape=...  15.2 us
    pallas_call x4, Pallas kernels, encode(): pl.pallas_call(encode_kernel, out_shape=(jax.ShapeDtypeStruct((count, wid...  15.1 us
    ppermute x6, starting transfers between devices, gather_pieces(): lax.ppermute(up, 'tensor', [(r * nx + x, (r + 1) * nx + x) for r in range...  14.3 us
    ppermute x4, waiting for transfers between devices, shards(): got = lax.ppermute(leaving, 'dp', y_pairs(k))  13.4 us
    ppermute x8, starting transfers between devices, tree_sum(): lax.ppermute(value, axis, [(i, i ^ bit) for i in range(count)])  10.9 us
  transfers between devices with their start and end apart: 57, of which 17 were waited for; matrix products, arithmetic and copies ran while one was open for 14% of the time, Pallas kernels for 42%

profile of v1, /device:TPU:0, one launch (start us, length us, event | category | flops | bytes accessed | tf_op | source)
XLA Modules:
  0.0 308.1 jit_solution(17000074708170926903)
XLA Ops:
  3.1 5.6 %collective-permute-start.23 = (bf16[320,512]{1,0:T(8,128)(2,1)S(1)}, bf16[320,512]{1,0:T(8,128)(2,1)S(1)}, u32[]{:S(2)}, u32[]{:S(2)}) collective-permute-start(bf16[320,512]{1,0:T(8,128)(2,1)S(1)} %bitcast.229), channel_id=1, source_target_pairs={{0,2},{1,3},{2,4},{3,5},{4,6},{5,7},{8,10},{9,11},{10,12},{11,13},... | collective-permute-start | bytes 983048 | tf_op jit(solution)/shard_map/ppermute | solution.py:56
  10.0 4.6 %collective-permute-start.6 = (bf16[320,512]{1,0:T(8,128)(2,1)S(1)}, bf16[320,512]{1,0:T(8,128)(2,1)S(1)}, u32[]{:S(2)}, u32[]{:S(2)}) collective-permute-start(bf16[320,512]{1,0:T(8,128)(2,1)S(1)} %bitcast.233), channel_id=1, source_target_pairs={{0,2},{1,3},{2,4},{3,5},{4,6},{5,7},{8,10},{9,11},{10,12},{11,13},... | collective-permute-start | bytes 983048 | tf_op jit(solution)/shard_map/ppermute | solution.py:56
  26.2 6.4 %select_drafts.1 = f32[8,4,8192]{2,1,0:T(4,128)} custom-call(s32[4]{0:T(128)} %dynamic_slice.35.at, f32[20,65536]{1,0:T(8,128)} %drafts.1), custom_call_target="tpu_custom_call" | custom-call | bytes 6553600 | tf_op jit(solution)/shard_map/select_drafts/pallas_call | solution.py:210
  58.8 5.5 %collective-permute-done.29.refs_8_ = bf16[320,512]{1,0:T(8,128)(2,1)S(1)} collective-permute-done((bf16[320,512]{1,0:T(8,128)(2,1)S(1)}, bf16[320,512]{1,0:T(8,128)(2,1)S(1)}, u32[]{:S(2)}, u32[]{:S(2)}) %collective-permute-start.29) | collective-permute-done | bytes 327712 | tf_op jit(solution)/shard_map/ppermute | solution.py:59
  76.9 3.2 %collective-permute-start.17 = (bf16[320,512]{1,0:T(8,128)(2,1)}, bf16[320,512]{1,0:T(8,128)(2,1)}, u32[]{:S(2)}, u32[]{:S(2)}) collective-permute-start(bf16[320,512]{1,0:T(8,128)(2,1)} %collective-permute-done.16.refs_12_), channel_id=1, source_target_pairs={{0,1},{1,0},{8,9},{9,8},{16,17},{17,16},{24,25},{25,24}} | collective-permute-start | bytes 983048 | tf_op jit(solution)/shard_map/ppermute | solution.py:50
  92.1 3.2 %collective-permute-start.34 = (bf16[320,512]{1,0:T(8,128)(2,1)}, bf16[320,512]{1,0:T(8,128)(2,1)S(1)}, u32[]{:S(2)}, u32[]{:S(2)}) collective-permute-start(bf16[320,512]{1,0:T(8,128)(2,1)} %collective-permute-done.33.refs_12_), channel_id=1, source_target_pairs={{0,1},{1,0},{8,9},{9,8},{16,17},{17,16},{24,25},{25,24}} | collective-permute-start | bytes 983048 | tf_op jit(solution)/shard_map/ppermute | solution.py:50
  95.3 7.6 %prepare.2.x = bf16[320,4096]{1,0:T(8,128)(2,1)} custom-call(s32[14]{0:T(128)} %convert_element_type.83.holds, s32[14]{0:T(128)} %compare_select_fusion.3.place, s32[320,1]{1,0:T(8,128)} %broadcast_in_dim.67.order, f32[320,1]{1,0:T(8,128)} %reshape.570.scale, f32[8,512]{1,0:T(8,128)} %reshape.467.gain, bf16[320,512]{1,0:T(8,128)(2,1)} %bitcast.235, ...), custom_call_target="tpu_custom_call" | custom-call | flops 838860800 | bytes 7864320 | tf_op jit(solution)/shard_map/prepare/pallas_call | solution.py:86
  102.9 19.2 %head.4 = (f32[160,4096]{1,0:T(8,128)}, f32[160,4096]{1,0:T(8,128)}) custom-call(bf16[320,4096]{1,0:T(8,128)(2,1)} %prepare.2.x, bf16[4096,8192]{1,0:T(8,128)(2,1)} %w.7), custom_call_target="tpu_custom_call" | custom-call | flops 10737418240 | bytes 41418752 | tf_op jit(solution)/shard_map/head/pallas_call | solution.py:111
  127.0 19.3 %head.5 = (f32[160,4096]{1,0:T(8,128)}, f32[160,4096]{1,0:T(8,128)}) custom-call(bf16[320,4096]{1,0:T(8,128)(2,1)} %prepare.2.x, bf16[4096,8192]{1,0:T(8,128)(2,1)} %w.7), custom_call_target="tpu_custom_call" | custom-call | flops 10737418240 | bytes 41418752 | tf_op jit(solution)/shard_map/head/pallas_call | solution.py:111
  146.3 8.7 %all-to-all-start = ((f32[8,4,8192]{2,1,0:T(4,128)}), f32[8,4,8192]{2,1,0:T(4,128)}, u32[]{:S(2)}, u32[]{:S(2)}) async-start(f32[8,4,8192]{2,1,0:T(4,128)} %select_drafts.1), calls=%async_computation | async-start | bytes 2097152 | tf_op jit(solution)/shard_map/all_to_all | solution.py:355
  156.9 7.6 %prepare.3.x = bf16[320,4096]{1,0:T(8,128)(2,1)} custom-call(s32[14]{0:T(128)} %convert_element_type.83.holds, s32[14]{0:T(128)} %compare_select_fusion.3.place, s32[320,1]{1,0:T(8,128)} %broadcast_in_dim.68.order, f32[320,1]{1,0:T(8,128)} %reshape.571.scale, f32[8,512]{1,0:T(8,128)} %reshape.467.gain, bf16[320,512]{1,0:T(8,128)(2,1)} %bitcast.231, ...), custom_call_target="tpu_custom_call" | custom-call | flops 838860800 | bytes 7864320 | tf_op jit(solution)/shard_map/prepare/pallas_call | solution.py:86
  164.5 19.3 %head.6 = (f32[160,4096]{1,0:T(8,128)}, f32[160,4096]{1,0:T(8,128)}) custom-call(bf16[320,4096]{1,0:T(8,128)(2,1)} %prepare.3.x, bf16[4096,8192]{1,0:T(8,128)(2,1)} %w.7), custom_call_target="tpu_custom_call" | custom-call | flops 10737418240 | bytes 41418752 | tf_op jit(solution)/shard_map/head/pallas_call | solution.py:111
  184.0 19.3 %head.7 = (f32[160,4096]{1,0:T(8,128)}, f32[160,4096]{1,0:T(8,128)}) custom-call(bf16[320,4096]{1,0:T(8,128)(2,1)} %prepare.3.x, bf16[4096,8192]{1,0:T(8,128)(2,1)} %w.7), custom_call_target="tpu_custom_call" | custom-call | flops 10737418240 | bytes 41418752 | tf_op jit(solution)/shard_map/head/pallas_call | solution.py:111
  215.3 4.2 %collective-permute-done.21 = f32[16,4096]{1,0:T(8,128)S(1)} collective-permute-done((f32[16,4096]{1,0:T(8,128)S(1)}, f32[16,4096]{1,0:T(8,128)S(1)}, u32[]{:S(2)}, u32[]{:S(2)}) %collective-permute-start.21) | collective-permute-done | bytes 262176 | tf_op jit(solution)/shard_map/ppermute | solution.py:320
  220.8 4.2 %collective-permute-done.36 = f32[16,4096]{1,0:T(8,128)S(1)} collective-permute-done((f32[16,4096]{1,0:T(8,128)S(1)}, f32[16,4096]{1,0:T(8,128)S(1)}, u32[]{:S(2)}, u32[]{:S(2)}) %collective-permute-start.36) | collective-permute-done | bytes 262176 | tf_op jit(solution)/shard_map/ppermute | solution.py:320
  226.4 3.6 %collective-permute-done.38 = f32[16,4096]{1,0:T(8,128)S(1)} collective-permute-done((f32[16,4096]{1,0:T(8,128)S(1)}, f32[16,4096]{1,0:T(8,128)S(1)}, u32[]{:S(2)}, u32[]{:S(2)}) %collective-permute-start.38) | collective-permute-done | bytes 262176 | tf_op jit(solution)/shard_map/ppermute | solution.py:320
  234.2 3.8 %encode.4 = (s16[64,4096]{1,0:T(8,128)(2,1)}, f32[64,128]{1,0:T(8,128)}) custom-call(f32[160,4096]{1,0:T(8,128)} %get-tuple-element.19.keep, f32[160,4096]{1,0:T(8,128)} %collective-permute-done.18.came), custom_call_target="tpu_custom_call" | custom-call | flops 2097152 | bytes 2621440 | tf_op jit(solution)/shard_map/encode/pallas_call | solution.py:145
  241.6 3.8 %encode.5 = (s16[64,4096]{1,0:T(8,128)(2,1)}, f32[64,128]{1,0:T(8,128)}) custom-call(f32[160,4096]{1,0:T(8,128)} %get-tuple-element.21.keep, f32[160,4096]{1,0:T(8,128)} %copy-done.1), custom_call_target="tpu_custom_call" | custom-call | flops 2097152 | bytes 2621440 | tf_op jit(solution)/shard_map/encode/pallas_call | solution.py:145
  254.9 3.8 %encode.6 = (s16[64,4096]{1,0:T(8,128)(2,1)}, f32[64,128]{1,0:T(8,128)}) custom-call(f32[160,4096]{1,0:T(8,128)} %get-tuple-element.23.keep, f32[160,4096]{1,0:T(8,128)} %copy-done.2), custom_call_target="tpu_custom_call" | custom-call | flops 2097152 | bytes 2621440 | tf_op jit(solution)/shard_map/encode/pallas_call | solution.py:145
  263.8 3.8 %encode.7 = (s16[64,4096]{1,0:T(8,128)(2,1)}, f32[64,128]{1,0:T(8,128)}) custom-call(f32[160,4096]{1,0:T(8,128)} %get-tuple-element.25.keep, f32[160,4096]{1,0:T(8,128)} %copy-done), custom_call_target="tpu_custom_call" | custom-call | flops 2097152 | bytes 2621440 | tf_op jit(solution)/shard_map/encode/pallas_call | solution.py:145
  269.7 4.1 %finish.4 = f32[64,128]{1,0:T(8,128)} custom-call(s32[64,1]{1,0:T(8,128)} %copy.52.ids, f32[160,4096]{1,0:T(8,128)} %get-tuple-element.19.keep, f32[160,4096]{1,0:T(8,128)} %collective-permute-done.18.came, s16[64,4096]{1,0:T(8,128)(2,1)} %collective-permute-done.42.refs_0_, f32[64,128]{1,0:T(8,128)} %copy-done.28), custom_call_target="tpu_custom_call" | custom-call | flops 3145728 | bytes 2621440 | tf_op jit(solution)/shard_map/finish/pallas_call | solution.py:189
  276.2 4.1 %finish.5 = f32[64,128]{1,0:T(8,128)} custom-call(s32[64,1]{1,0:T(8,128)} %copy.53.ids, f32[160,4096]{1,0:T(8,128)} %get-tuple-element.21.keep, f32[160,4096]{1,0:T(8,128)} %copy-done.1, s16[64,4096]{1,0:T(8,128)(2,1)} %copy-done.7, f32[64,128]{1,0:T(8,128)} %copy-done.29), custom_call_target="tpu_custom_call" | custom-call | flops 3145728 | bytes 2621440 | tf_op jit(solution)/shard_map/finish/pallas_call | solution.py:189
  282.5 4.1 %finish.6 = f32[64,128]{1,0:T(8,128)} custom-call(s32[64,1]{1,0:T(8,128)} %copy.57.ids, f32[160,4096]{1,0:T(8,128)} %get-tuple-element.23.keep, f32[160,4096]{1,0:T(8,128)} %copy-done.2, s16[64,4096]{1,0:T(8,128)(2,1)} %copy-done.8, f32[64,128]{1,0:T(8,128)} %copy-done.31), custom_call_target="tpu_custom_call" | custom-call | flops 3145728 | bytes 2621440 | tf_op jit(solution)/shard_map/finish/pallas_call | solution.py:189
  289.1 4.1 %finish.7 = f32[64,128]{1,0:T(8,128)} custom-call(s32[64,1]{1,0:T(8,128)} %copy.58.ids, f32[160,4096]{1,0:T(8,128)} %get-tuple-element.25.keep, f32[160,4096]{1,0:T(8,128)} %copy-done, s16[64,4096]{1,0:T(8,128)(2,1)} %copy-done.9, f32[64,128]{1,0:T(8,128)} %copy-done.30), custom_call_target="tpu_custom_call" | custom-call | flops 3145728 | bytes 2621440 | tf_op jit(solution)/shard_map/finish/pallas_call | solution.py:189
  (322 shorter events, 133.7 us)
Async XLA Ops:
  1.8 50.1 %collective-permute-start.25 = (bf16[320,512]{1,0:T(8,128)(2,1)S(1)}, bf16[320,512]{1,0:T(8,128)(2,1)S(1)}, u32[]{:S(2)}, u32[]{:S(2)}) collective-permute-start(bf16[320,512]{1,0:T(8,128)(2,1)S(1)} %bitcast.228), channel_id=1, source_target_pairs={{2,0},{3,1},{4,2},{5,3},{6,4},{7,5},{10,8},{11,9},{12,10},{13,11},... | collective-permute-start | bytes 983048 | tf_op jit(solution)/shard_map/ppermute | solution.py:59
  3.1 52.2 %collective-permute-start.23 = (bf16[320,512]{1,0:T(8,128)(2,1)S(1)}, bf16[320,512]{1,0:T(8,128)(2,1)S(1)}, u32[]{:S(2)}, u32[]{:S(2)}) collective-permute-start(bf16[320,512]{1,0:T(8,128)(2,1)S(1)} %bitcast.229), channel_id=1, source_target_pairs={{0,2},{1,3},{2,4},{3,5},{4,6},{5,7},{8,10},{9,11},{10,12},{11,13},... | collective-permute-start | bytes 983048 | tf_op jit(solution)/shard_map/ppermute | solution.py:56
  8.7 44.5 %collective-permute-start.8 = (bf16[320,512]{1,0:T(8,128)(2,1)S(1)}, bf16[320,512]{1,0:T(8,128)(2,1)S(1)}, u32[]{:S(2)}, u32[]{:S(2)}) collective-permute-start(bf16[320,512]{1,0:T(8,128)(2,1)S(1)} %bitcast.232), channel_id=1, source_target_pairs={{2,0},{3,1},{4,2},{5,3},{6,4},{7,5},{10,8},{11,9},{12,10},{13,11},... | collective-permute-start | bytes 983048 | tf_op jit(solution)/shard_map/ppermute | solution.py:59
  10.0 44.6 %collective-permute-start.6 = (bf16[320,512]{1,0:T(8,128)(2,1)S(1)}, bf16[320,512]{1,0:T(8,128)(2,1)S(1)}, u32[]{:S(2)}, u32[]{:S(2)}) collective-permute-start(bf16[320,512]{1,0:T(8,128)(2,1)S(1)} %bitcast.233), channel_id=1, source_target_pairs={{0,2},{1,3},{2,4},{3,5},{4,6},{5,7},{8,10},{9,11},{10,12},{11,13},... | collective-permute-start | bytes 983048 | tf_op jit(solution)/shard_map/ppermute | solution.py:56
  55.4 18.6 %collective-permute-start.9 = (bf16[320,512]{1,0:T(8,128)(2,1)S(1)}, bf16[320,512]{1,0:T(8,128)(2,1)S(1)}, u32[]{:S(2)}, u32[]{:S(2)}) collective-permute-start(bf16[320,512]{1,0:T(8,128)(2,1)S(1)} %collective-permute-done.8.refs_4_), channel_id=1, source_target_pairs={{0,1},{1,0},{2,3},{3,2},{4,5},{5,4},{8,9},{9,8},{10,11},{11,10},{1... | collective-permute-start | bytes 983048 | tf_op jit(solution)/shard_map/ppermute | solution.py:50
  85.1 37.1 %collective-permute-start.22 = (bf16[320,512]{1,0:T(8,128)(2,1)S(1)}, bf16[320,512]{1,0:T(8,128)(2,1)S(1)}, u32[]{:S(2)}, u32[]{:S(2)}) collective-permute-start(bf16[320,512]{1,0:T(8,128)(2,1)S(1)} %bitcast.230), channel_id=1, source_target_pairs={{0,1},{1,0},{2,3},{3,2},{4,5},{5,4},{6,7},{7,6},{8,9},{9,8},{10,11... | collective-permute-start | bytes 983048 | tf_op jit(solution)/shard_map/ppermute | solution.py:50
  86.6 38.2 %collective-permute-start.26 = (bf16[320,512]{1,0:T(8,128)(2,1)S(1)}, bf16[320,512]{1,0:T(8,128)(2,1)S(1)}, u32[]{:S(2)}, u32[]{:S(2)}) collective-permute-start(bf16[320,512]{1,0:T(8,128)(2,1)S(1)} %collective-permute-done.25.refs_4_), channel_id=1, source_target_pairs={{0,1},{1,0},{2,3},{3,2},{4,5},{5,4},{8,9},{9,8},{10,11},{11,10},{1... | collective-permute-start | bytes 983048 | tf_op jit(solution)/shard_map/ppermute | solution.py:50
  89.1 66.0 %collective-permute-start.24 = (bf16[320,512]{1,0:T(8,128)(2,1)S(1)}, bf16[320,512]{1,0:T(8,128)(2,1)}, u32[]{:S(2)}, u32[]{:S(2)}) collective-permute-start(bf16[320,512]{1,0:T(8,128)(2,1)S(1)} %collective-permute-done.23.refs_2_), channel_id=1, source_target_pairs={{2,3},{3,2},{4,5},{5,4},{6,7},{7,6},{10,11},{11,10},{12,13},{13,12... | collective-permute-start | bytes 983048 | tf_op jit(solution)/shard_map/ppermute | solution.py:50
  90.7 34.9 %collective-permute-start.31 = (bf16[320,512]{1,0:T(8,128)(2,1)S(1)}, bf16[320,512]{1,0:T(8,128)(2,1)}, u32[]{:S(2)}, u32[]{:S(2)}) collective-permute-start(bf16[320,512]{1,0:T(8,128)(2,1)S(1)} %collective-permute-done.27.refs_6_), channel_id=1, source_target_pairs={{4,6},{5,7},{12,14},{13,15},{20,22},{21,23},{28,30},{29,31}} | collective-permute-start | bytes 983048 | tf_op jit(solution)/shard_map/ppermute | solution.py:56
  92.1 34.2 %collective-permute-start.34 = (bf16[320,512]{1,0:T(8,128)(2,1)}, bf16[320,512]{1,0:T(8,128)(2,1)S(1)}, u32[]{:S(2)}, u32[]{:S(2)}) collective-permute-start(bf16[320,512]{1,0:T(8,128)(2,1)} %collective-permute-done.33.refs_12_), channel_id=1, source_target_pairs={{0,1},{1,0},{8,9},{9,8},{16,17},{17,16},{24,25},{25,24}} | collective-permute-start | bytes 983048 | tf_op jit(solution)/shard_map/ppermute | solution.py:50
  122.2 33.1 %collective-permute-start.30 = (bf16[320,512]{1,0:T(8,128)(2,1)S(1)}, bf16[320,512]{1,0:T(8,128)(2,1)S(1)}, u32[]{:S(2)}, u32[]{:S(2)}) collective-permute-start(bf16[320,512]{1,0:T(8,128)(2,1)S(1)} %collective-permute-done.29.refs_8_), channel_id=1, source_target_pairs={{0,1},{1,0},{2,3},{3,2},{8,9},{9,8},{10,11},{11,10},{16,17},{17,16... | collective-permute-start | bytes 983048 | tf_op jit(solution)/shard_map/ppermute | solution.py:50
  124.9 30.5 %collective-permute-start.28 = (bf16[320,512]{1,0:T(8,128)(2,1)S(1)}, bf16[320,512]{1,0:T(8,128)(2,1)S(1)}, u32[]{:S(2)}, u32[]{:S(2)}) collective-permute-start(bf16[320,512]{1,0:T(8,128)(2,1)S(1)} %collective-permute-done.27.refs_6_), channel_id=1, source_target_pairs={{4,5},{5,4},{6,7},{7,6},{12,13},{13,12},{14,15},{15,14},{20,21},{2... | collective-permute-start | bytes 983048 | tf_op jit(solution)/shard_map/ppermute | solution.py:50
  125.6 29.8 %collective-permute-start.32 = (bf16[320,512]{1,0:T(8,128)(2,1)}, bf16[320,512]{1,0:T(8,128)(2,1)S(1)}, u32[]{:S(2)}, u32[]{:S(2)}) collective-permute-start(bf16[320,512]{1,0:T(8,128)(2,1)} %collective-permute-done.31.refs_10_), channel_id=1, source_target_pairs={{6,7},{7,6},{14,15},{15,14},{22,23},{23,22},{30,31},{31,30}} | collective-permute-start | bytes 983048 | tf_op jit(solution)/shard_map/ppermute | solution.py:50
  127.0 76.5 %collective-permute-start.18 = (f32[160,4096]{1,0:T(8,128)}, f32[160,4096]{1,0:T(8,128)}, u32[]{:S(2)}, u32[]{:S(2)}) collective-permute-start(f32[160,4096]{1,0:T(8,128)} %get-tuple-element.20), channel_id=1, source_target_pairs={{0,8},{8,0},{16,24},{24,16},{1,9},{9,1},{17,25},{25,17},{2,10},{10... | collective-permute-start | bytes 7864328 | tf_op jit(solution)/shard_map/ppermute | solution.py:315
  146.3 106.1 %all-to-all-start = ((f32[8,4,8192]{2,1,0:T(4,128)}), f32[8,4,8192]{2,1,0:T(4,128)}, u32[]{:S(2)}, u32[]{:S(2)}) async-start(f32[8,4,8192]{2,1,0:T(4,128)} %select_drafts.1), calls=%async_computation | async-start | bytes 2097152 | tf_op jit(solution)/shard_map/all_to_all | solution.py:355
  155.0 50.2 %collective-permute-start.20 = (f32[160,4096]{1,0:T(8,128)}, f32[160,4096]{1,0:T(8,128)S(1)}, u32[]{:S(2)}, u32[]{:S(2)}) collective-permute-start(f32[160,4096]{1,0:T(8,128)} %get-tuple-element.22), channel_id=1, source_target_pairs={{0,8},{8,0},{16,24},{24,16},{1,9},{9,1},{17,25},{25,17},{2,10},{10... | collective-permute-start | bytes 7864328 | tf_op jit(solution)/shard_map/ppermute | solution.py:315
  183.8 24.2 %collective-permute-start.35 = (f32[160,4096]{1,0:T(8,128)}, f32[160,4096]{1,0:T(8,128)S(1)}, u32[]{:S(2)}, u32[]{:S(2)}) collective-permute-start(f32[160,4096]{1,0:T(8,128)} %get-tuple-element.24), channel_id=1, source_target_pairs={{0,8},{8,0},{16,24},{24,16},{1,9},{9,1},{17,25},{25,17},{2,10},{10... | collective-permute-start | bytes 7864328 | tf_op jit(solution)/shard_map/ppermute | solution.py:315
  210.8 19.2 %collective-permute-start.38 = (f32[16,4096]{1,0:T(8,128)S(1)}, f32[16,4096]{1,0:T(8,128)S(1)}, u32[]{:S(2)}, u32[]{:S(2)}) collective-permute-start(f32[16,4096]{1,0:T(8,128)S(1)} %slice_add_fusion), channel_id=1, source_target_pairs={{0,16},{8,24},{16,0},{24,8},{1,17},{9,25},{17,1},{25,9},{2,18},{10... | collective-permute-start | bytes 786440 | tf_op jit(solution)/shard_map/ppermute | solution.py:320
  237.9 29.6 %collective-permute-start.43 = (f32[64,128]{1,0:T(8,128)}, f32[64,128]{1,0:T(8,128)S(1)}, u32[]{:S(2)}, u32[]{:S(2)}) collective-permute-start(f32[64,128]{1,0:T(8,128)} %get-tuple-element.28), channel_id=1, source_target_pairs={{0,16},{8,24},{16,0},{24,8},{1,17},{9,25},{17,1},{25,9},{2,18},{10... | collective-permute-start | bytes 98312 | tf_op jit(solution)/shard_map/ppermute | solution.py:324
  238.5 30.7 %collective-permute-start.42 = (s16[64,4096]{1,0:T(8,128)(2,1)}, s16[64,4096]{1,0:T(8,128)(2,1)}, u32[]{:S(2)}, u32[]{:S(2)}) collective-permute-start(s16[64,4096]{1,0:T(8,128)(2,1)} %get-tuple-element.27), channel_id=1, source_target_pairs={{0,16},{8,24},{16,0},{24,8},{1,17},{9,25},{17,1},{25,9},{2,18},{10... | collective-permute-start | bytes 1572872 | tf_op jit(solution)/shard_map/ppermute | solution.py:324
  245.4 28.4 %collective-permute-start.45 = (f32[64,128]{1,0:T(8,128)}, f32[64,128]{1,0:T(8,128)S(1)}, u32[]{:S(2)}, u32[]{:S(2)}) collective-permute-start(f32[64,128]{1,0:T(8,128)} %get-tuple-element.30), channel_id=1, source_target_pairs={{0,16},{8,24},{16,0},{24,8},{1,17},{9,25},{17,1},{25,9},{2,18},{10... | collective-permute-start | bytes 98312 | tf_op jit(solution)/shard_map/ppermute | solution.py:324
  245.9 29.5 %collective-permute-start.44 = (s16[64,4096]{1,0:T(8,128)(2,1)}, s16[64,4096]{1,0:T(8,128)(2,1)S(1)}, u32[]{:S(2)}, u32[]{:S(2)}) collective-permute-start(s16[64,4096]{1,0:T(8,128)(2,1)} %get-tuple-element.29), channel_id=1, source_target_pairs={{0,16},{8,24},{16,0},{24,8},{1,17},{9,25},{17,1},{25,9},{2,18},{10... | collective-permute-start | bytes 1572872 | tf_op jit(solution)/shard_map/ppermute | solution.py:324
  258.7 22.3 %collective-permute-start.46 = (s16[64,4096]{1,0:T(8,128)(2,1)}, s16[64,4096]{1,0:T(8,128)(2,1)S(1)}, u32[]{:S(2)}, u32[]{:S(2)}) collective-permute-start(s16[64,4096]{1,0:T(8,128)(2,1)} %get-tuple-element.31), channel_id=1, source_target_pairs={{0,16},{8,24},{16,0},{24,8},{1,17},{9,25},{17,1},{25,9},{2,18},{10... | collective-permute-start | bytes 1572872 | tf_op jit(solution)/shard_map/ppermute | solution.py:324
  275.4 20.5 %collective-permute-start.54 = (f32[32]{0:T(128)S(1)}, f32[32]{0:T(128)}, u32[]{:S(2)}, u32[]{:S(2)}) collective-permute-start(f32[32]{0:T(128)S(1)} %add.890), channel_id=1, source_target_pairs={{0,2},{1,3},{2,0},{3,1},{4,6},{5,7},{6,4},{7,5},{8,10},{9,11},{10,... | collective-permute-start | bytes 392 | tf_op jit(solution)/shard_map/ppermute | solution.py:21
  (68 other events, 1035.7 us)

commit v2 on v0

v2 whole, which is shorter than its diff:
```python
import functools

import jax
import jax.numpy as jnp
from jax import lax
from jax.experimental import pallas as pl
from jax.experimental.pallas import tpu as pltpu
from jax.sharding import PartitionSpec as P

EPS = 1e-05
FIRST_PARTS = (2, 2)
REST_PARTS = (2, 1, 1)
ROWS = 32
TILES = 1024, 512
VMEM_LIMIT = 56 * 1024 * 1024
F32 = jnp.float32
COST = pl.CostEstimate(flops=1024, bytes_accessed=1024, transcendentals=0)


def tree_sum(value, axis, count):
    bit = 1
    while bit < count:
        value = value + lax.ppermute(value, axis, [(i, i ^ bit) for i in range(count)])
        bit *= 2
    return value


def merge(first, second):
    top = jnp.maximum(first[0], second[0])
    total = first[1] * jnp.exp(first[0] - top) + second[1] * jnp.exp(second[0] - top)
    return jnp.stack([top, total, first[2] + second[2]])


def tree_merge(stats, axis, count):
    me = lax.axis_index(axis)
    bit = 1
    while bit < count:
        other = lax.ppermute(stats, axis, [(i, i ^ bit) for i in range(count)])
        upper = (me & bit) != 0
        stats = merge(jnp.where(upper, other, stats), jnp.where(upper, stats, other))
        bit *= 2
    return stats


def held_after(value, *earlier):
    if not earlier:
        return value
    return lax.optimization_barrier((value,) + earlier)[0]


def gather_pieces(piece, nz, nx, during=()):
    count = nz * nx

    def step(value, bits):
        return lax.ppermute(value, "tensor", [(i, i ^ bits) for i in range(count)])

    along = {0: piece}
    bit = nz // 2
    while bit:
        for offset in sorted(along):
            along[offset | bit] = step(held_after(along[offset], *during) if offset else piece, bit * nx)
        bit //= 2
    pieces = {(offset, 0): value for offset, value in along.items()}
    for k in range(1, nx):
        first = step(along[0], k)
        pieces[0, k] = first
        for offset in range(1, nz):
            pieces[offset, k] = step(along[offset], k)
    return pieces


def prepare_kernel(count, place, order, scale, gain, *refs):
    pieces, out = refs[:count], refs[count]
    rows, width = pieces[0].shape
    pick = (lax.broadcasted_iota(jnp.int32, (order.shape[0], rows), 1) == order[...]).astype(jnp.bfloat16)
    for n in range(count):
        at = place[n]
        normed = (pieces[n][...].astype(F32) * scale[...] * gain[pl.ds(at, 1), :]).astype(jnp.bfloat16)
        moved = jnp.dot(pick, normed, preferred_element_type=F32).astype(jnp.bfloat16)
        out[:, pl.ds(pl.multiple_of(at * width, width), width)] = moved


def prepare(pieces, place, order, scale, gain, depth):
    rows = order.shape[0]
    smem = pl.BlockSpec(memory_space=pltpu.SMEM)
    vmem = pl.BlockSpec(memory_space=pltpu.VMEM)
    return pl.pallas_call(
        functools.partial(prepare_kernel, len(pieces)),
        out_shape=jax.ShapeDtypeStruct((rows, depth), jnp.bfloat16),
        in_specs=[smem] + [vmem] * (3 + len(pieces)),
        out_specs=vmem,
        compiler_params=pltpu.CompilerParams(vmem_limit_bytes=VMEM_LIMIT),
        cost_estimate=COST,
        name="prepare",
    )(place, order, scale, gain, *pieces)


def head_kernel(x, w, send, keep):
    half = send.shape[0]
    out = jnp.dot(x[...], w[...], preferred_element_type=F32)
    send[...] = out[:half]
    keep[...] = out[half:]


def head(normed, weight, first, width, tile):
    rows, depth = normed.shape
    tile = min(tile, width)
    half = jax.ShapeDtypeStruct((rows // 2, width), F32)
    spec = pl.BlockSpec((rows // 2, tile), lambda j: (0, j))
    return pl.pallas_call(
        head_kernel,
        out_shape=(half, half),
        grid=(width // tile,),
        in_specs=[
            pl.BlockSpec((rows, depth), lambda j: (0, 0)),
            pl.BlockSpec((depth, tile), lambda j: (0, first // tile + j)),
        ],
        out_specs=(spec, spec),
        compiler_params=pltpu.CompilerParams(vmem_limit_bytes=VMEM_LIMIT),
        cost_estimate=pl.CostEstimate(
            flops=16 * rows * depth * width, bytes_accessed=2 * depth * width, transcendentals=0
        ),
        name="head",
    )(normed, weight)


def exponent(value):
    return jnp.floor(jnp.log2(jnp.maximum(value * 1.001, 1e-20))) + 1.0


def encode_kernel(keep, came, coded):
    rows, width = keep.shape
    lanes = lax.broadcasted_iota(jnp.int32, (rows, 128), 1)
    total = keep[...] + came[...]
    high = jnp.max(total, axis=1, keepdims=True)
    low = jnp.min(total, axis=1, keepdims=True)
    middle = 0.5 * high + 0.5 * low
    shift = exponent(jnp.abs(middle))
    unit = jnp.floor(middle * jnp.exp2(15.0 - shift) + 0.5)
    middle = unit * jnp.exp2(shift - 15.0)
    size = exponent(jnp.maximum(high - middle, middle - low))
    scaled = (total - middle) * jnp.exp2(15.0 - size)
    coded[:, :width] = jnp.floor(scaled + 0.5).astype(jnp.int32).astype(jnp.int16)
    info = jnp.where(lanes == 0, unit, jnp.where(lanes == 1, shift, size))
    coded[:, width:] = info.astype(jnp.int32).astype(jnp.int16)


def encode(keep, came, group, count):
    width = keep.shape[1]
    steps = count // ROWS
    source = pl.BlockSpec((ROWS, width), lambda i: (group * steps + i, 0))
    return pl.pallas_call(
        encode_kernel,
        out_shape=jax.ShapeDtypeStruct((count, width + 128), jnp.int16),
        grid=(steps,),
        in_specs=[source, source],
        out_specs=pl.BlockSpec((ROWS, width + 128), lambda i: (i, 0)),
        compiler_params=pltpu.CompilerParams(vmem_limit_bytes=VMEM_LIMIT),
        cost_estimate=COST,
        name="encode",
    )(keep, came)


def row_stats(total, ids):
    top = jnp.max(total, axis=1, keepdims=True)
    sums = jnp.sum(jnp.exp(total - top), axis=1, keepdims=True)
    columns = lax.broadcasted_iota(jnp.int32, total.shape, 1)
    picked = jnp.sum(jnp.where(columns == ids, total, 0.0), axis=1, keepdims=True)
    lanes = lax.broadcasted_iota(jnp.int32, (total.shape[0], 128), 1)
    return jnp.where(lanes == 0, top, jnp.where(lanes == 1, sums, picked))


def finish_chosen_kernel(far, ids, keep, came, *refs):
    total = keep[...] + came[...]
    for wide in refs[:far]:
        total = total + wide[:, : total.shape[1]]
    logits, stats = refs[far:]
    logits[...] = total
    stats[...] = row_stats(total, ids[...])


def finish_others_kernel(far, ids, keep, came, *refs):
    width = keep.shape[1]
    total = keep[...] + came[...]
    for coded in refs[:far]:
        info = coded[:, width:].astype(jnp.int32).astype(F32)
        middle = info[:, :1] * jnp.exp2(info[:, 1:2] - 15.0)
        step = jnp.exp2(info[:, 2:3] - 15.0)
        total = total + (coded[:, :width].astype(jnp.int32).astype(F32) * step + middle)
    refs[far][...] = row_stats(total, ids[...])


def finish_chosen(ids, keep, came, wides, first):
    count, width = ids.shape[0], keep.shape[1]
    own = pl.BlockSpec((count, width), lambda i: (first // count, 0))
    return pl.pallas_call(
        functools.partial(finish_chosen_kernel, len(wides)),
        out_shape=(jax.ShapeDtypeStruct((count, width), F32), jax.ShapeDtypeStruct((count, 128), F32)),
        grid=(1,),
        in_specs=[pl.BlockSpec((count, 1), lambda i: (0, 0)), own, own]
        + [pl.BlockSpec((count, width), lambda i: (0, 0)) for _ in wides],
        out_specs=(
            pl.BlockSpec((count, width), lambda i: (0, 0)),
            pl.BlockSpec((count, 128), lambda i: (0, 0)),
        ),
        cost_estimate=COST,
        name="finish_chosen",
    )(ids, keep, came, *wides)


def finish_others(ids, keep, came, codeds, group):
    count, width = ids.shape[0], keep.shape[1]
    steps = count // ROWS
    own = pl.BlockSpec((ROWS, width), lambda i: (group * steps + i, 0))
    return pl.pallas_call(
        functools.partial(finish_others_kernel, len(codeds)),
        out_shape=jax.ShapeDtypeStruct((count, 128), F32),
        grid=(steps,),
        in_specs=[pl.BlockSpec((ROWS, 1), lambda i: (i, 0)), own, own]
        + [pl.BlockSpec((ROWS, width + 128), lambda i: (i, 0)) for _ in codeds],
        out_specs=pl.BlockSpec((ROWS, 128), lambda i: (i, 0)),
        compiler_params=pltpu.CompilerParams(vmem_limit_bytes=VMEM_LIMIT),
        cost_estimate=COST,
        name="finish_others",
    )(ids, keep, came, *codeds)


def select_kernel(positions, at, drafts, out):
    for r in range(out.shape[1]):
        out[0, pl.ds(r, 1), :] = drafts[pl.ds(r * positions + at[r], 1), :]


def select_drafts(drafts, at, positions, count):
    rows, vocab = drafts.shape
    width = vocab // count
    return pl.pallas_call(
        functools.partial(select_kernel, positions),
        out_shape=jax.ShapeDtypeStruct((count, rows // positions, width), F32),
        grid=(count,),
        in_specs=[
            pl.BlockSpec(memory_space=pltpu.SMEM),
            pl.BlockSpec((rows, width), lambda j: (0, j)),
        ],
        out_specs=pl.BlockSpec((1, rows // positions, width), lambda j: (j, 0, 0)),
        cost_estimate=COST,
        name="select_drafts",
    )(at, drafts)


def shards(n_dp, n_tensor, hidden, gain, head_weight, draft_probs, draft_ids, reject_at):
    tokens, local = hidden.shape
    features = local * n_dp * n_tensor
    depth, width = head_weight.shape
    vocab = width * n_tensor
    requests = reject_at.shape[0]
    owned = draft_ids.shape[0]
    positions = owned // requests
    n_y = n_dp // 2
    nx = 1
    while nx * nx * 4 <= n_tensor:
        nx *= 2
    nz = n_tensor // nx
    d, t = lax.axis_index("dp"), lax.axis_index("tensor")
    y, c = d // 2, d % 2
    z, x = t // nx, t % nx

    relayed = local % 128 == 0
    if relayed:
        whole = gather_pieces(hidden, nz, nx)
    else:
        whole = {(0, 0): lax.all_gather(hidden, "tensor", axis=1, tiled=True)}
    offsets = list(whole)

    values = hidden.astype(F32)
    squares = jnp.sum(values * values, axis=1)
    places = lax.dynamic_update_slice(jnp.zeros((n_dp * requests,), F32), reject_at.astype(F32), (d * requests,))
    small = jnp.concatenate([squares, places])
    short = -small.shape[0] % 1024
    small = tree_sum(jnp.pad(small, (0, short)).reshape(-1, 128), "dp", n_dp)
    flat = small.reshape(-1)
    every_at = flat[tokens : tokens + n_dp * requests].astype(jnp.int32).reshape(n_dp, requests)
    gains = lax.dynamic_update_slice(jnp.zeros((depth,), F32), gain[0].astype(F32), (t * local,))
    small = jnp.concatenate([flat[:tokens], gains])
    small = jnp.pad(small, (0, -small.shape[0] % 1024)).reshape(-1, 128)
    flat = tree_sum(small, "tensor", n_tensor).reshape(-1)
    scale = lax.rsqrt(flat[:tokens] / features + EPS)
    gains = flat[tokens : tokens + depth]

    turn = []

    def next_turn(value):
        return held_after(value, turn[-1]) if turn else value

    mine = requests // n_tensor
    at = lax.dynamic_slice(reject_at, (t * mine,), (mine,))
    drafts = select_drafts(draft_probs, at, positions, n_tensor)

    rest = owned - requests
    starts = jnp.arange(requests, dtype=jnp.int32) * positions
    steps = jnp.arange(positions - 1, dtype=jnp.int32)

    def chosen_of(at):
        return starts + at

    def others_of(at):
        return (starts[:, None] + steps + (steps >= at[..., None])).reshape(at.shape[:-1] + (rest,))

    owners = jnp.arange(n_dp, dtype=jnp.int32)[:, None]
    chosen_tokens = (owners * owned + chosen_of(every_at)).reshape(-1)
    is_chosen = chosen_tokens[:, None] == jnp.arange(tokens)
    piece = jnp.dot(is_chosen.astype(jnp.bfloat16), hidden, preferred_element_type=F32).astype(jnp.bfloat16)
    chosen_scale = jnp.sum(jnp.where(is_chosen, scale, 0.0), axis=1)
    if relayed:
        gathered = gather_pieces(piece, nz, nx, (drafts,))
    else:
        gathered = {(0, 0): lax.all_gather(piece, "tensor", axis=1, tiled=True)}

    hops = [k % n_y for k in range(1, n_y + 1)]
    groups = jnp.stack([((y + k) % n_y) * 2 + core for core in (1 - c, c) for k in hops])
    is_group = (groups[:, None] == jnp.arange(n_dp))[:, :, None]

    def grouped(of_owner):
        return jnp.sum(jnp.where(is_group, of_owner, 0), axis=1).reshape(-1, 1).astype(jnp.int32)

    core_pairs = [(i, i ^ 1) for i in range(n_dp)]

    def y_pairs(k):
        return [(i, ((i // 2 + k) % n_y) * 2 + i % 2) for i in range(n_dp)]

    where = jnp.concatenate([chosen_of(reject_at), others_of(reject_at)])
    ids = jnp.sum(jnp.where(where[:, None] == jnp.arange(owned), draft_ids, 0), axis=1) - t * width
    ids = ids[:, None]

    def span(parts, p):
        quarter = width // sum(parts)
        return sum(parts[:p]) * quarter, parts[p] * quarter

    def do_head(normed, p, parts, tile):
        send, keep = head(next_turn(normed), head_weight, *span(parts, p), tile)
        turn.append(keep)
        return keep, lax.ppermute(send, "dp", core_pairs)

    place = jnp.stack([((z ^ dz) * nx + (x ^ k)) if relayed else 0 * z for dz, k in offsets]).astype(jnp.int32)
    order = grouped(owners * requests + jnp.arange(requests, dtype=jnp.int32))
    by_piece = gains.reshape(-1, local if relayed else depth)

    def met(*at):
        return tuple(whole[o] for o in at) if relayed and nz > 2 and nx == 2 else ()

    normed = prepare(
        [gathered[o] for o in offsets],
        place,
        held_after(next_turn(order), *met((1, 0), (2, 0), (0, 1), (1, 1))),
        chosen_scale[:, None],
        by_piece,
        depth,
    )
    turn.append(normed)
    first_heads = [do_head(normed, 0, FIRST_PARTS, TILES[0])]
    normed = held_after(normed, *met((3, 0), (2, 1)))
    for p in range(1, len(FIRST_PARTS)):
        first_heads.append(do_head(normed, p, FIRST_PARTS, TILES[0]))
    chosen_far = []

    def send_chosen(p):
        keep, came = first_heads[p]
        keep = next_turn(keep)
        leaving = [
            keep[n * requests : (n + 1) * requests] + came[n * requests : (n + 1) * requests]
            for n in range(n_y - 1)
        ]
        chosen_far.append([lax.ppermute(v, "dp", y_pairs(k)) for k, v in zip(hops, leaving)])
        turn.extend(leaving[-1:])

    chosen_logits, chosen_stats = [], []

    def do_chosen(p):
        keep, came = first_heads[p]
        part_ids = next_turn(ids[:requests] - span(FIRST_PARTS, p)[0])
        logits, stats = finish_chosen(part_ids, keep, came, chosen_far[p], (n_y - 1) * requests)
        chosen_logits.append(logits)
        chosen_stats.append(stats)
        turn.append(stats)

    for p in range(len(FIRST_PARTS) - 1):
        send_chosen(p)

    order = grouped(owners * owned + others_of(every_at))
    normed = prepare([whole[o] for o in offsets], place, next_turn(order), scale[:, None], by_piece, depth)
    turn.append(normed)
    send_chosen(len(FIRST_PARTS) - 1)
    drafts = held_after(drafts, normed)
    drafts = lax.all_to_all(drafts, "tensor", split_axis=0, concat_axis=0, tiled=True)
    rest_heads, coded_far, other_stats = [], [], []

    def send_others(p):
        keep, came = rest_heads[p]
        far = []
        for n, k in enumerate(hops[:-1]):
            coded = encode(next_turn(keep), came, n, rest)
            turn.append(coded)
            far.append(lax.ppermute(coded, "dp", y_pairs(k)))
        coded_far.append(far)

    def do_others(p):
        keep, came = rest_heads[p]
        part_ids = next_turn(ids[requests:] - span(REST_PARTS, p)[0])
        other_stats.append(finish_others(part_ids, keep, came, coded_far[p], n_y - 1))
        turn.append(other_stats[-1])

    for p in range(len(REST_PARTS)):
        rest_heads.append(do_head(normed, p, REST_PARTS, TILES[1]))
        if p == 0:
            turn.append(drafts)
            for q in range(len(FIRST_PARTS)):
                do_chosen(q)
        else:
            send_others(p - 1)
    for p in range(len(REST_PARTS) - 2):
        do_others(p)
    send_others(len(REST_PARTS) - 1)
    sent_last = turn[-1]
    for p in range(max(len(REST_PARTS) - 2, 0), len(REST_PARTS)):
        do_others(p)

    def joined(stats):
        merged = stats[0][:, :3].T
        for other in stats[1:]:
            merged = merge(merged, other[:, :3].T)
        return merged

    of_chosen = tree_merge(joined(chosen_stats), "tensor", n_tensor)
    chosen_logz = of_chosen[0] + jnp.log(of_chosen[1])
    logits = held_after(jnp.concatenate(chosen_logits, axis=1), sent_last)
    kept = jnp.maximum(jnp.exp(logits - chosen_logz[:, None]) - drafts.reshape(requests, width), 0.0)
    mass = jnp.sum(kept, axis=1)
    zero = jnp.zeros_like(mass)
    of_other = jnp.concatenate([joined(other_stats), jnp.stack([zero, mass, zero])], axis=1)
    of_other = tree_merge(of_other, "tensor", n_tensor)
    mass = of_other[1, rest:]
    of_other = of_other[:, :rest]
    residual = vocab * kept / mass[:, None]
    found = jnp.concatenate(
        [of_chosen[2] - chosen_logz, of_other[2] - (of_other[0] + jnp.log(of_other[1]))]
    )
    token_logprob = jnp.sum(
        jnp.where(where[None, :] == jnp.arange(owned)[:, None], found[None, :], 0.0), axis=1
    )
    return (token_logprob, residual)


def solution(mesh):
    return jax.shard_map(
        functools.partial(shards, mesh.shape["dp"], mesh.shape["tensor"]),
        mesh=mesh,
        in_specs=(
            P(None, ("dp", "tensor")),
            P(None, ("dp", "tensor")),
            P("dp", "tensor"),
            P(("dp", "tensor"), None),
            P("dp"),
            P("dp"),
        ),
        out_specs=(P("dp"), P("dp", "tensor")),
        check_vma=False,
    )
```

time: 427 us -> 272 us (0.64)
  waiting for transfers between devices: 202 us -> 62.2 us
  Pallas kernels: 0 us -> 127 us
  blocking collectives: 90.1 us -> 0 us
  matrix products: 51.4 us -> 1.4 us
  starting transfers between devices: 5.27 us -> 43.4 us
  local copies, waits for them, and re-layouts: 50 us -> 22 us
  between operations: 14.2 us -> 1.15 us
    all_to_all x1, waiting for transfers between devices: 138 us -> 1.09 us  [shards(): lax.all_to_all(drafts, 'tensor', split_axis=0, concat_axis=0, tiled=True)]
    pallas_call x0 -> x16, Pallas kernels: none -> 127 us  [the longest x5 79.1 us: head(): pl.pallas_call(head_kernel, out_shape=(half, half), grid=(width // tile,)...]
    all_gather x1 -> x0, waiting for transfers between devices: 63.9 us -> none  [shards(): lax.all_gather(hidden, 'tensor', axis=1, tiled=True)]
    ppermute x0 -> x35, waiting for transfers between devices: none -> 61.1 us  [the longest x14 28.1 us: step(): return lax.ppermute(value, 'tensor', [(i, i ^ bits) for i in range(count)])]
    dot_general x1, matrix products: 51.4 us -> 1.4 us  [shards(): jnp.dot(is_chosen.astype(jnp.bfloat16), hidden, preferred_element_type=F32)]
    psum x3 -> x0, blocking collectives: 42.4 us -> none  [the longest x2 36.3 us: shards(): total, picked = lax.psum((local_total, local_pick), 'tensor')]
    ppermute x0 -> x35, starting transfers between devices: none -> 38.5 us  [the longest x14 18.7 us: step(): return lax.ppermute(value, 'tensor', [(i, i ^ bits) for i in range(count)])]
    reshape x5 -> x3, local copies, waits for them, and re-layouts: 30.5 us -> 1.65 us  [the longest x1 0.67 us: grouped(): jnp.sum(jnp.where(is_group, of_owner, 0), axis=1).reshape(-1, 1)]
  transfers between devices with their start and end apart: 3 -> 36, of which waited for: 2 -> 15; matrix products, arithmetic and copies ran while one was open for 7% -> 11% of each run, Pallas kernels for 0% -> 40%
where the time goes in v2:
time: 272 us; the launch traced here: 270 us
  Pallas kernels  127 us (47%)
  waiting for transfers between devices  62.2 us (23%)
  starting transfers between devices  43.4 us (16%)
  local copies, waits for them, and re-layouts  22 us (8%)
  other arithmetic  12.9 us (5%)
    pallas_call x5, Pallas kernels, head(): pl.pallas_call(head_kernel, out_shape=(half, half), grid=(width // tile,)...  79.1 us
    ppermute x14, waiting for transfers between devices, step(): return lax.ppermute(value, 'tensor', [(i, i ^ bits) for i in range(count)])  28.1 us
    ppermute x14, starting transfers between devices, step(): return lax.ppermute(value, 'tensor', [(i, i ^ bits) for i in range(count)])  18.7 us
    ppermute x5, waiting for transfers between devices, tree_sum(): lax.ppermute(value, axis, [(i, i ^ bit) for i in range(count)])  18.2 us
    pallas_call x3, Pallas kernels, finish_others(): pl.pallas_call(functools.partial(finish_others_kernel, len(codeds)), out_...  13.2 us
    pallas_call x3, Pallas kernels, encode(): pl.pallas_call(encode_kernel, out_shape=jax.ShapeDtypeStruct((count, widt...  12.3 us
    pallas_call x2, Pallas kernels, prepare(): pl.pallas_call(functools.partial(prepare_kernel, len(pieces)), out_shape=...  11.5 us
    ppermute x6, starting transfers between devices, tree_merge(): other = lax.ppermute(stats, axis, [(i, i ^ bit) for i in range(count)])  9.09 us
  transfers between devices with their start and end apart: 36, of which 15 were waited for; matrix products, arithmetic and copies ran while one was open for 11% of the time, Pallas kernels for 40%

profile of v2, /device:TPU:0, one launch (start us, length us, event | category | flops | bytes accessed | tf_op | source)
XLA Modules:
  0.0 270.0 jit_solution(15902343672119381546)
XLA Ops:
  0.6 3.0 %collective-permute-start.4 = (bf16[640,512]{1,0:T(8,128)(2,1)}, bf16[640,512]{1,0:T(8,128)(2,1)S(1)}, u32[]{:S(2)}, u32[]{:S(2)}) collective-permute-start(bf16[640,512]{1,0:T(8,128)(2,1)} %refs_0_.1), channel_id=1, source_target_pairs={{0,1},{1,0},{2,3},{3,2},{4,5},{5,4},{6,7},{7,6},{8,9},{9,8},{10,11... | collective-permute-start | bytes 1966088 | tf_op jit(solution)/shard_map/ppermute | solution.py:55
  19.4 2.9 %collective-permute-done.6 = f32[40,128]{1,0:T(8,128)S(1)} collective-permute-done((f32[40,128]{1,0:T(8,128)S(1)}, f32[40,128]{1,0:T(8,128)S(1)}, u32[]{:S(2)}, u32[]{:S(2)}) %collective-permute-start.6) | collective-permute-done | bytes 20512 | tf_op jit(solution)/shard_map/ppermute | solution.py:23
  22.8 12.9 %collective-permute-done.7 = f32[40,128]{1,0:T(8,128)S(1)} collective-permute-done((f32[40,128]{1,0:T(8,128)S(1)}, f32[40,128]{1,0:T(8,128)S(1)}, u32[]{:S(2)}, u32[]{:S(2)}) %collective-permute-start.7) | collective-permute-done | bytes 20512 | tf_op jit(solution)/shard_map/ppermute | solution.py:23
  49.2 6.4 %select_drafts.1 = f32[8,4,8192]{2,1,0:T(4,128)} custom-call(s32[4]{0:T(128)} %dynamic_slice.3.at, f32[20,65536]{1,0:T(8,128)} %drafts.1), custom_call_target="tpu_custom_call" | custom-call | flops 1024 | bytes 1024 | tf_op jit(solution)/shard_map/select_drafts/pallas_call | solution.py:236
  62.4 8.3 %collective-permute-done.11.refs_3_ = bf16[128,512]{1,0:T(8,128)(2,1)S(1)} collective-permute-done((bf16[128,512]{1,0:T(8,128)(2,1)}, bf16[128,512]{1,0:T(8,128)(2,1)S(1)}, u32[]{:S(2)}, u32[]{:S(2)}) %collective-permute-start.11) | collective-permute-done | bytes 131104 | tf_op jit(solution)/shard_map/ppermute | solution.py:55
  80.8 2.9 %prepare.2.x = bf16[128,4096]{1,0:T(8,128)(2,1)} custom-call(s32[8]{0:T(128)} %stack.96.place, s32[128,1]{1,0:T(8,128)} %copy.72.order, f32[128,1]{1,0:T(8,128)} %copy.73.scale, f32[8,512]{1,0:T(8,128)} %reshape.202.gain, bf16[128,512]{1,0:T(8,128)(2,1)} %copy-done.12, bf16[128,512]{1,0:T(8,128)(2,1)} %copy-done.16, ...), custom_call_target="tpu_custom_call" | custom-call | flops 1024 | bytes 1024 | tf_op jit(solution)/shard_map/prepare/pallas_call | solution.py:87
  83.7 13.9 %head.5 = (f32[64,4096]{1,0:T(8,128)}, f32[64,4096]{1,0:T(8,128)}) custom-call(bf16[128,4096]{1,0:T(8,128)(2,1)} %prepare.2.x, bf16[4096,8192]{1,0:T(8,128)(2,1)} %w.9), custom_call_target="tpu_custom_call" | custom-call | flops 34359738368 | bytes 33554432 | tf_op jit(solution)/shard_map/head/pallas_call | solution.py:110
  97.7 13.6 %head.6 = (f32[64,4096]{1,0:T(8,128)}, f32[64,4096]{1,0:T(8,128)}) custom-call(bf16[128,4096]{1,0:T(8,128)(2,1)} %prepare.2.x, bf16[4096,8192]{1,0:T(8,128)(2,1)} %w.9), custom_call_target="tpu_custom_call" | custom-call | flops 34359738368 | bytes 33554432 | tf_op jit(solution)/shard_map/head/pallas_call | solution.py:110
  115.2 14.7 %collective-permute-done.19.refs_7_ = bf16[640,512]{1,0:T(8,128)(2,1)} collective-permute-done((bf16[640,512]{1,0:T(8,128)(2,1)}, bf16[640,512]{1,0:T(8,128)(2,1)}, u32[]{:S(2)}, u32[]{:S(2)}) %collective-permute-start.19) | collective-permute-done | bytes 655392 | tf_op jit(solution)/shard_map/ppermute | solution.py:55
  129.9 8.6 %prepare.3.x = bf16[512,4096]{1,0:T(8,128)(2,1)} custom-call(s32[8]{0:T(128)} %stack.96.place, s32[512,1]{1,0:T(8,128)} %copy.74.order, f32[640,1]{1,0:T(8,128)} %bitcast.105, f32[8,512]{1,0:T(8,128)} %reshape.202.gain, bf16[640,512]{1,0:T(8,128)(2,1)} %refs_0_.1, bf16[640,512]{1,0:T(8,128)(2,1)} %copy-done.5, bf16[640,512]{1,0:T(8,128)(2,1)} %copy-done.6, ...), custom_call_target="tpu_custom_call" | custom-call | flops 1024 | bytes 1024 | tf_op jit(solution)/shard_map/prepare/pallas_call | solution.py:87
  140.6 4.8 %all-to-all-start = ((f32[8,4,8192]{2,1,0:T(4,128)}), f32[8,4,8192]{2,1,0:T(4,128)S(1)}, u32[]{:S(2)}, u32[]{:S(2)}) async-start(f32[8,4,8192]{2,1,0:T(4,128)} %select_drafts.1), calls=%async_computation | async-start | bytes 2097152 | tf_op jit(solution)/shard_map/all_to_all | solution.py:393
  145.5 23.7 %head.8 = (f32[256,4096]{1,0:T(8,128)}, f32[256,4096]{1,0:T(8,128)}) custom-call(bf16[512,4096]{1,0:T(8,128)(2,1)} %prepare.3.x, bf16[4096,8192]{1,0:T(8,128)(2,1)} %w.9), custom_call_target="tpu_custom_call" | custom-call | flops 137438953472 | bytes 33554432 | tf_op jit(solution)/shard_map/head/pallas_call | solution.py:110
  179.4 13.9 %head.7 = (f32[256,2048]{1,0:T(8,128)}, f32[256,2048]{1,0:T(8,128)}) custom-call(bf16[512,4096]{1,0:T(8,128)(2,1)} %prepare.3.x, bf16[4096,8192]{1,0:T(8,128)(2,1)} %w.9), custom_call_target="tpu_custom_call" | custom-call | flops 68719476736 | bytes 16777216 | tf_op jit(solution)/shard_map/head/pallas_call | solution.py:110
  194.9 4.6 %encode.3 = s16[128,4224]{1,0:T(8,128)(2,1)} custom-call(f32[256,4096]{1,0:T(8,128)} %get-tuple-element.58.keep, f32[256,4096]{1,0:T(8,128)} %collective-permute-done.26.came), custom_call_target="tpu_custom_call" | custom-call | flops 1024 | bytes 1024 | tf_op jit(solution)/shard_map/encode/pallas_call | solution.py:152
  201.0 14.0 %head.9 = (f32[256,2048]{1,0:T(8,128)}, f32[256,2048]{1,0:T(8,128)}) custom-call(bf16[512,4096]{1,0:T(8,128)(2,1)} %prepare.3.x, bf16[4096,8192]{1,0:T(8,128)(2,1)} %w.9), custom_call_target="tpu_custom_call" | custom-call | flops 68719476736 | bytes 16777216 | tf_op jit(solution)/shard_map/head/pallas_call | solution.py:110
  218.0 3.8 %encode.4 = s16[128,2176]{1,0:T(8,128)(2,1)} custom-call(f32[256,2048]{1,0:T(8,128)} %get-tuple-element.62.keep, f32[256,2048]{1,0:T(8,128)} %collective-permute-done.27.came), custom_call_target="tpu_custom_call" | custom-call | flops 1024 | bytes 1024 | tf_op jit(solution)/shard_map/encode/pallas_call | solution.py:152
  223.1 3.1 %collective-permute-done.28.refs_0_ = s16[128,4224]{1,0:T(8,128)(2,1)} collective-permute-done((s16[128,4224]{1,0:T(8,128)(2,1)}, s16[128,4224]{1,0:T(8,128)(2,1)}, u32[]{:S(2)}, u32[]{:S(2)}) %collective-permute-start.28) | collective-permute-done | bytes 1081376 | tf_op jit(solution)/shard_map/ppermute | solution.py:402
  226.2 4.8 %finish_others.3 = f32[128,128]{1,0:T(8,128)} custom-call(s32[128,1]{1,0:T(8,128)} %copy.81.ids, f32[256,4096]{1,0:T(8,128)} %get-tuple-element.58.keep, f32[256,4096]{1,0:T(8,128)} %collective-permute-done.26.came, s16[128,4224]{1,0:T(8,128)(2,1)} %collective-permute-done.28.refs_0_), custom_call_target="tpu_custom_call" | custom-call | flops 1024 | bytes 1024 | tf_op jit(solution)/shard_map/finish_others/pallas_call | solution.py:215
  231.9 3.8 %encode.5 = s16[128,2176]{1,0:T(8,128)(2,1)} custom-call(f32[256,2048]{1,0:T(8,128)} %get-tuple-element.65.keep, f32[256,2048]{1,0:T(8,128)} %collective-permute-done.29.came), custom_call_target="tpu_custom_call" | custom-call | flops 1024 | bytes 1024 | tf_op jit(solution)/shard_map/encode/pallas_call | solution.py:152
  239.1 4.2 %finish_others.4 = f32[128,128]{1,0:T(8,128)} custom-call(s32[128,1]{1,0:T(8,128)} %copy.82.ids, f32[256,2048]{1,0:T(8,128)} %get-tuple-element.62.keep, f32[256,2048]{1,0:T(8,128)} %collective-permute-done.27.came, s16[128,2176]{1,0:T(8,128)(2,1)} %copy-done.9), custom_call_target="tpu_custom_call" | custom-call | flops 1024 | bytes 1024 | tf_op jit(solution)/shard_map/finish_others/pallas_call | solution.py:215
  245.8 3.6 %collective-permute-done.31.refs_0_ = s16[128,2176]{1,0:T(8,128)(2,1)S(1)} collective-permute-done((s16[128,2176]{1,0:T(8,128)(2,1)}, s16[128,2176]{1,0:T(8,128)(2,1)S(1)}, u32[]{:S(2)}, u32[]{:S(2)}) %collective-permute-start.31) | collective-permute-done | bytes 557088 | tf_op jit(solution)/shard_map/ppermute | solution.py:402
  250.2 4.2 %finish_others.5 = f32[128,128]{1,0:T(8,128)} custom-call(s32[128,1]{1,0:T(8,128)} %copy.83.ids, f32[256,2048]{1,0:T(8,128)} %get-tuple-element.65.keep, f32[256,2048]{1,0:T(8,128)} %collective-permute-done.29.came, s16[128,2176]{1,0:T(8,128)(2,1)} %copy-done.10), custom_call_target="tpu_custom_call" | custom-call | flops 1024 | bytes 1024 | tf_op jit(solution)/shard_map/finish_others/pallas_call | solution.py:215
  256.5 3.0 %collective-permute-done.32 = f32[3,160]{1,0:T(4,128)S(1)} collective-permute-done((f32[3,160]{1,0:T(4,128)S(1)}, f32[3,160]{1,0:T(4,128)S(1)}, u32[]{:S(2)}, u32[]{:S(2)}) %collective-permute-start.32) | collective-permute-done | bytes 1952 | tf_op jit(solution)/shard_map/ppermute | solution.py:38
  260.5 2.8 %collective-permute-done.33 = f32[3,160]{1,0:T(4,128)S(1)} collective-permute-done((f32[3,160]{1,0:T(4,128)S(1)}, f32[3,160]{1,0:T(4,128)S(1)}, u32[]{:S(2)}, u32[]{:S(2)}) %collective-permute-start.33) | collective-permute-done | bytes 1952 | tf_op jit(solution)/shard_map/ppermute | solution.py:38
  (247 shorter events, 87.2 us)
Async XLA Ops:
  0.6 71.6 %collective-permute-start.4 = (bf16[640,512]{1,0:T(8,128)(2,1)}, bf16[640,512]{1,0:T(8,128)(2,1)S(1)}, u32[]{:S(2)}, u32[]{:S(2)}) collective-permute-start(bf16[640,512]{1,0:T(8,128)(2,1)} %refs_0_.1), channel_id=1, source_target_pairs={{0,1},{1,0},{2,3},{3,2},{4,5},{5,4},{6,7},{7,6},{8,9},{9,8},{10,11... | collective-permute-start | bytes 1966088 | tf_op jit(solution)/shard_map/ppermute | solution.py:55
  3.6 53.3 %collective-permute-start.3 = (bf16[640,512]{1,0:T(8,128)(2,1)}, bf16[640,512]{1,0:T(8,128)(2,1)S(1)}, u32[]{:S(2)}, u32[]{:S(2)}) collective-permute-start(bf16[640,512]{1,0:T(8,128)(2,1)} %refs_0_.1), channel_id=1, source_target_pairs={{0,4},{1,5},{2,6},{3,7},{4,0},{5,1},{6,2},{7,3},{8,12},{9,13},{10,... | collective-permute-start | bytes 1966088 | tf_op jit(solution)/shard_map/ppermute | solution.py:55
  6.2 35.6 %collective-permute-start.2 = (bf16[640,512]{1,0:T(8,128)(2,1)}, bf16[640,512]{1,0:T(8,128)(2,1)S(1)}, u32[]{:S(2)}, u32[]{:S(2)}) collective-permute-start(bf16[640,512]{1,0:T(8,128)(2,1)} %refs_0_.1), channel_id=1, source_target_pairs={{0,2},{1,3},{2,0},{3,1},{4,6},{5,7},{6,4},{7,5},{8,10},{9,11},{10,... | collective-permute-start | bytes 1966088 | tf_op jit(solution)/shard_map/ppermute | solution.py:55
  22.3 13.4 %collective-permute-start.7 = (f32[40,128]{1,0:T(8,128)S(1)}, f32[40,128]{1,0:T(8,128)S(1)}, u32[]{:S(2)}, u32[]{:S(2)}) collective-permute-start(f32[40,128]{1,0:T(8,128)S(1)} %fusion.24), channel_id=1, source_target_pairs={{0,2},{1,3},{2,0},{3,1},{4,6},{5,7},{6,4},{7,5},{8,10},{9,11},{10,... | collective-permute-start | bytes 61448 | tf_op jit(solution)/shard_map/ppermute | solution.py:23
  40.5 16.9 %collective-permute-start.9 = (bf16[128,512]{1,0:T(8,128)(2,1)S(1)}, bf16[128,512]{1,0:T(8,128)(2,1)S(1)}, u32[]{:S(2)}, u32[]{:S(2)}) collective-permute-start(bf16[128,512]{1,0:T(8,128)(2,1)S(1)} %convolution_convert_fusion.refs_0_), channel_id=1, source_target_pairs={{0,4},{1,5},{2,6},{3,7},{4,0},{5,1},{6,2},{7,3},{8,12},{9,13},{10,... | collective-permute-start | bytes 393224 | tf_op jit(solution)/shard_map/ppermute | solution.py:55
  41.9 30.8 %collective-permute-start.5 = (bf16[640,512]{1,0:T(8,128)(2,1)S(1)}, bf16[640,512]{1,0:T(8,128)(2,1)S(1)}, u32[]{:S(2)}, u32[]{:S(2)}) collective-permute-start(bf16[640,512]{1,0:T(8,128)(2,1)S(1)} %collective-permute-done.2.refs_2_), channel_id=1, source_target_pairs={{0,1},{1,0},{2,3},{3,2},{4,5},{5,4},{6,7},{7,6},{8,9},{9,8},{10,11... | collective-permute-start | bytes 1966088 | tf_op jit(solution)/shard_map/ppermute | solution.py:55
  45.4 13.6 %collective-permute-start.10 = (bf16[128,512]{1,0:T(8,128)(2,1)S(1)}, bf16[128,512]{1,0:T(8,128)(2,1)}, u32[]{:S(2)}, u32[]{:S(2)}) collective-permute-start(bf16[128,512]{1,0:T(8,128)(2,1)S(1)} %convolution_convert_fusion.refs_0_), channel_id=1, source_target_pairs={{0,2},{1,3},{2,0},{3,1},{4,6},{5,7},{6,4},{7,5},{8,10},{9,11},{10,... | collective-permute-start | bytes 393224 | tf_op jit(solution)/shard_map/ppermute | solution.py:55
  57.0 26.7 %collective-permute-start.17 = (bf16[640,512]{1,0:T(8,128)(2,1)S(1)}, bf16[640,512]{1,0:T(8,128)(2,1)S(1)}, u32[]{:S(2)}, u32[]{:S(2)}) collective-permute-start(bf16[640,512]{1,0:T(8,128)(2,1)S(1)} %collective-permute-done.3.refs_1_), channel_id=1, source_target_pairs={{0,1},{1,0},{2,3},{3,2},{4,5},{5,4},{6,7},{7,6},{8,9},{9,8},{10,11... | collective-permute-start | bytes 1966088 | tf_op jit(solution)/shard_map/ppermute | solution.py:55
  57.4 26.3 %collective-permute-start.16 = (bf16[640,512]{1,0:T(8,128)(2,1)S(1)}, bf16[640,512]{1,0:T(8,128)(2,1)}, u32[]{:S(2)}, u32[]{:S(2)}) collective-permute-start(bf16[640,512]{1,0:T(8,128)(2,1)S(1)} %collective-permute-done.3.refs_1_), channel_id=1, source_target_pairs={{0,2},{1,3},{2,0},{3,1},{4,6},{5,7},{6,4},{7,5},{8,10},{9,11},{10,... | collective-permute-start | bytes 1966088 | tf_op jit(solution)/shard_map/ppermute | solution.py:55
  58.9 11.7 %collective-permute-start.11 = (bf16[128,512]{1,0:T(8,128)(2,1)}, bf16[128,512]{1,0:T(8,128)(2,1)S(1)}, u32[]{:S(2)}, u32[]{:S(2)}) collective-permute-start(bf16[128,512]{1,0:T(8,128)(2,1)} %copy-done.16), channel_id=1, source_target_pairs={{0,2},{1,3},{2,0},{3,1},{4,6},{5,7},{6,4},{7,5},{8,10},{9,11},{10,... | collective-permute-start | bytes 393224 | tf_op jit(solution)/shard_map/ppermute | solution.py:55
  97.6 15.7 %collective-permute-start.18 = (f32[64,4096]{1,0:T(8,128)}, f32[64,4096]{1,0:T(8,128)S(1)}, u32[]{:S(2)}, u32[]{:S(2)}) collective-permute-start(f32[64,4096]{1,0:T(8,128)} %get-tuple-element.45), channel_id=1, source_target_pairs={{0,8},{8,0},{16,24},{24,16},{1,9},{9,1},{17,25},{25,17},{2,10},{10... | collective-permute-start | bytes 3145736 | tf_op jit(solution)/shard_map/ppermute | solution.py:341
  111.4 27.1 %collective-permute-start.21 = (f32[64,4096]{1,0:T(8,128)}, f32[64,4096]{1,0:T(8,128)S(1)}, u32[]{:S(2)}, u32[]{:S(2)}) collective-permute-start(f32[64,4096]{1,0:T(8,128)} %get-tuple-element.51), channel_id=1, source_target_pairs={{0,8},{8,0},{16,24},{24,16},{1,9},{9,1},{17,25},{25,17},{2,10},{10... | collective-permute-start | bytes 3145736 | tf_op jit(solution)/shard_map/ppermute | solution.py:341
  112.8 17.1 %collective-permute-start.19 = (bf16[640,512]{1,0:T(8,128)(2,1)}, bf16[640,512]{1,0:T(8,128)(2,1)}, u32[]{:S(2)}, u32[]{:S(2)}) collective-permute-start(bf16[640,512]{1,0:T(8,128)(2,1)} %collective-permute-done.16.refs_3_), channel_id=1, source_target_pairs={{0,1},{1,0},{2,3},{3,2},{4,5},{5,4},{6,7},{7,6},{8,9},{9,8},{10,11... | collective-permute-start | bytes 1966088 | tf_op jit(solution)/shard_map/ppermute | solution.py:55
  138.5 35.5 %collective-permute-start.22 = (f32[32,4096]{1,0:T(8,128)S(1)}, f32[32,4096]{1,0:T(8,128)S(1)}, u32[]{:S(2)}, u32[]{:S(2)}) collective-permute-start(f32[32,4096]{1,0:T(8,128)S(1)} %slice_add_fusion), channel_id=1, source_target_pairs={{0,16},{8,24},{16,0},{24,8},{1,17},{9,25},{17,1},{25,9},{2,18},{10... | collective-permute-start | bytes 1572872 | tf_op jit(solution)/shard_map/ppermute | solution.py:372
  140.1 30.9 %collective-permute-start.20 = (f32[32,4096]{1,0:T(8,128)}, f32[32,4096]{1,0:T(8,128)}, u32[]{:S(2)}, u32[]{:S(2)}) collective-permute-start(f32[32,4096]{1,0:T(8,128)} %slice_add_fusion.1), channel_id=1, source_target_pairs={{0,16},{8,24},{16,0},{24,8},{1,17},{9,25},{17,1},{25,9},{2,18},{10... | collective-permute-start | bytes 1572872 | tf_op jit(solution)/shard_map/ppermute | solution.py:372
  140.6 29.7 %all-to-all-start = ((f32[8,4,8192]{2,1,0:T(4,128)}), f32[8,4,8192]{2,1,0:T(4,128)S(1)}, u32[]{:S(2)}, u32[]{:S(2)}) async-start(f32[8,4,8192]{2,1,0:T(4,128)} %select_drafts.1), calls=%async_computation | async-start | bytes 2097152 | tf_op jit(solution)/shard_map/all_to_all | solution.py:393
  169.2 25.7 %collective-permute-start.26 = (f32[256,4096]{1,0:T(8,128)}, f32[256,4096]{1,0:T(8,128)}, u32[]{:S(2)}, u32[]{:S(2)}) collective-permute-start(f32[256,4096]{1,0:T(8,128)} %get-tuple-element.59), channel_id=1, source_target_pairs={{0,8},{8,0},{16,24},{24,16},{1,9},{9,1},{17,25},{25,17},{2,10},{10... | collective-permute-start | bytes 12582920 | tf_op jit(solution)/shard_map/ppermute | solution.py:341
  178.1 15.2 %collective-permute-start.23 = (f32[3,32]{1,0:T(4,128)S(1)}, f32[3,32]{1,0:T(4,128)S(1)}, u32[]{:S(2)}, u32[]{:S(2)}) collective-permute-start(f32[3,32]{1,0:T(4,128)S(1)} %pad_maximum_fusion.3), channel_id=1, source_target_pairs={{0,1},{1,0},{2,3},{3,2},{4,5},{5,4},{6,7},{7,6},{8,9},{9,8},{10,11... | collective-permute-start | bytes 1160 | tf_op jit(solution)/shard_map/ppermute | solution.py:38
  193.3 24.6 %collective-permute-start.27 = (f32[256,2048]{1,0:T(8,128)}, f32[256,2048]{1,0:T(8,128)}, u32[]{:S(2)}, u32[]{:S(2)}) collective-permute-start(f32[256,2048]{1,0:T(8,128)} %get-tuple-element.63), channel_id=1, source_target_pairs={{0,8},{8,0},{16,24},{24,16},{1,9},{9,1},{17,25},{25,17},{2,10},{10... | collective-permute-start | bytes 6291464 | tf_op jit(solution)/shard_map/ppermute | solution.py:341
  193.4 22.1 %collective-permute-start.24 = (f32[3,32]{1,0:T(4,128)S(1)}, f32[3,32]{1,0:T(4,128)S(1)}, u32[]{:S(2)}, u32[]{:S(2)}) collective-permute-start(f32[3,32]{1,0:T(4,128)S(1)} %pad_maximum_fusion.4), channel_id=1, source_target_pairs={{0,2},{1,3},{2,0},{3,1},{4,6},{5,7},{6,4},{7,5},{8,10},{9,11},{10,... | collective-permute-start | bytes 1160 | tf_op jit(solution)/shard_map/ppermute | solution.py:38
  199.5 26.7 %collective-permute-start.28 = (s16[128,4224]{1,0:T(8,128)(2,1)}, s16[128,4224]{1,0:T(8,128)(2,1)}, u32[]{:S(2)}, u32[]{:S(2)}) collective-permute-start(s16[128,4224]{1,0:T(8,128)(2,1)} %encode.3), channel_id=1, source_target_pairs={{0,16},{8,24},{16,0},{24,8},{1,17},{9,25},{17,1},{25,9},{2,18},{10... | collective-permute-start | bytes 3244040 | tf_op jit(solution)/shard_map/ppermute | solution.py:402
  215.0 16.9 %collective-permute-start.29 = (f32[256,2048]{1,0:T(8,128)}, f32[256,2048]{1,0:T(8,128)}, u32[]{:S(2)}, u32[]{:S(2)}) collective-permute-start(f32[256,2048]{1,0:T(8,128)} %get-tuple-element.66), channel_id=1, source_target_pairs={{0,8},{8,0},{16,24},{24,16},{1,9},{9,1},{17,25},{25,17},{2,10},{10... | collective-permute-start | bytes 6291464 | tf_op jit(solution)/shard_map/ppermute | solution.py:341
  221.8 16.5 %collective-permute-start.30 = (s16[128,2176]{1,0:T(8,128)(2,1)}, s16[128,2176]{1,0:T(8,128)(2,1)S(1)}, u32[]{:S(2)}, u32[]{:S(2)}) collective-permute-start(s16[128,2176]{1,0:T(8,128)(2,1)} %encode.4), channel_id=1, source_target_pairs={{0,16},{8,24},{16,0},{24,8},{1,17},{9,25},{17,1},{25,9},{2,18},{10... | collective-permute-start | bytes 1671176 | tf_op jit(solution)/shard_map/ppermute | solution.py:402
  235.8 13.6 %collective-permute-start.31 = (s16[128,2176]{1,0:T(8,128)(2,1)}, s16[128,2176]{1,0:T(8,128)(2,1)S(1)}, u32[]{:S(2)}, u32[]{:S(2)}) collective-permute-start(s16[128,2176]{1,0:T(8,128)(2,1)} %encode.5), channel_id=1, source_target_pairs={{0,16},{8,24},{16,0},{24,8},{1,17},{9,25},{17,1},{25,9},{2,18},{10... | collective-permute-start | bytes 1671176 | tf_op jit(solution)/shard_map/ppermute | solution.py:402
  (45 other events, 457.9 us)

commit v3 on v2

--- a/solution.py
+++ b/solution.py
@@ -48,47 +48,58 @@
     return lax.optimization_barrier((value,) + earlier)[0]
 
 
-def gather_pieces(piece, nz, nx, during=()):
+def gather_pieces(piece, nz, nx, first, during):
     count = nz * nx
 
     def step(value, bits):
         return lax.ppermute(value, "tensor", [(i, i ^ bits) for i in range(count)])
 
-    along = {0: piece}
+    pieces = {(0, 0): piece}
     bit = nz // 2
     while bit:
-        for offset in sorted(along):
-            along[offset | bit] = step(held_after(along[offset], *during) if offset else piece, bit * nx)
+        pieces[bit, 0] = step(piece, bit * nx)
         bit //= 2
-    pieces = {(offset, 0): value for offset, value in along.items()}
     for k in range(1, nx):
-        first = step(along[0], k)
-        pieces[0, k] = first
-        for offset in range(1, nz):
-            pieces[offset, k] = step(along[offset], k)
+        pieces[0, k] = step(held_after(piece, first), k)
+        pieces[1, k] = step(held_after(pieces[1, 0], pieces[0, k]), k)
+    done = [0, 1]
+    for offset in range(2, nz):
+        near = offset & -offset
+        if (offset, 0) not in pieces:
+            before = [pieces[o, k] for o in done for k in range(1, nx)] + [during]
+            pieces[offset, 0] = step(held_after(pieces[offset - near, 0], *before), near * nx)
+        for k in range(1, nx):
+            ahead = (pieces[offset - 1, k],) if offset > 2 else ()
+            pieces[offset, k] = step(held_after(pieces[offset, 0], *ahead), k)
     return pieces
 
 
 def prepare_kernel(count, place, order, scale, gain, *refs):
-    pieces, out = refs[:count], refs[count]
+    pieces, (chosen, others) = refs[:count], refs[count:]
+    first = chosen.shape[0]
     rows, width = pieces[0].shape
     pick = (lax.broadcasted_iota(jnp.int32, (order.shape[0], rows), 1) == order[...]).astype(jnp.bfloat16)
     for n in range(count):
         at = place[n]
         normed = (pieces[n][...].astype(F32) * scale[...] * gain[pl.ds(at, 1), :]).astype(jnp.bfloat16)
         moved = jnp.dot(pick, normed, preferred_element_type=F32).astype(jnp.bfloat16)
-        out[:, pl.ds(pl.multiple_of(at * width, width), width)] = moved
-
-
-def prepare(pieces, place, order, scale, gain, depth):
+        columns = pl.ds(pl.multiple_of(at * width, width), width)
+        chosen[:, columns] = moved[:first]
+        others[:, columns] = moved[first:]
+
+
+def prepare(pieces, place, order, scale, gain, depth, first):
     rows = order.shape[0]
     smem = pl.BlockSpec(memory_space=pltpu.SMEM)
     vmem = pl.BlockSpec(memory_space=pltpu.VMEM)
     return pl.pallas_call(
         functools.partial(prepare_kernel, len(pieces)),
-        out_shape=jax.ShapeDtypeStruct((rows, depth), jnp.bfloat16),
+        out_shape=(
+            jax.ShapeDtypeStruct((first, depth), jnp.bfloat16),
+            jax.ShapeDtypeStruct((rows - first, depth), jnp.bfloat16),
+        ),
         in_specs=[smem] + [vmem] * (3 + len(pieces)),
-        out_specs=vmem,
+        out_specs=(vmem, vmem),
         compiler_params=pltpu.CompilerParams(vmem_limit_bytes=VMEM_LIMIT),
         cost_estimate=COST,
         name="prepare",
@@ -264,27 +275,37 @@
     y, c = d // 2, d % 2
     z, x = t // nx, t % nx
 
+    mine = requests // n_tensor
+    at = lax.dynamic_slice(reject_at, (t * mine,), (mine,))
+    drafts = select_drafts(draft_probs, at, positions, n_tensor)
+
+    values = hidden.astype(F32)
+    squares = jnp.sum(values * values, axis=1)
+    gains = lax.dynamic_update_slice(jnp.zeros((depth,), F32), gain[0].astype(F32), (t * local,))
+    small = jnp.concatenate([squares, gains])
+    small = jnp.pad(small, (0, -small.shape[0] % 1024)).reshape(-1, 128)
+    if n_tensor > 1:
+        small = small + lax.ppermute(small, "tensor", [(i, i ^ 1) for i in range(n_tensor)])
     relayed = local % 128 == 0
     if relayed:
-        whole = gather_pieces(hidden, nz, nx)
+        whole = gather_pieces(hidden, nz, nx, small, drafts)
     else:
         whole = {(0, 0): lax.all_gather(hidden, "tensor", axis=1, tiled=True)}
     offsets = list(whole)
-
-    values = hidden.astype(F32)
-    squares = jnp.sum(values * values, axis=1)
+    bit = 2
+    while bit < n_tensor:
+        if relayed and bit == 4:
+            small = held_after(small, whole[nz // 2, 0])
+        small = small + lax.ppermute(small, "tensor", [(i, i ^ bit) for i in range(n_tensor)])
+        bit *= 2
+    flat = small.reshape(-1)
+    gains = flat[tokens : tokens + depth]
+
     places = lax.dynamic_update_slice(jnp.zeros((n_dp * requests,), F32), reject_at.astype(F32), (d * requests,))
-    small = jnp.concatenate([squares, places])
-    short = -small.shape[0] % 1024
-    small = tree_sum(jnp.pad(small, (0, short)).reshape(-1, 128), "dp", n_dp)
-    flat = small.reshape(-1)
+    small = jnp.concatenate([flat[:tokens], places])
+    flat = tree_sum(jnp.pad(small, (0, -small.shape[0] % 1024)).reshape(-1, 128), "dp", n_dp).reshape(-1)
     every_at = flat[tokens : tokens + n_dp * requests].astype(jnp.int32).reshape(n_dp, requests)
-    gains = lax.dynamic_update_slice(jnp.zeros((depth,), F32), gain[0].astype(F32), (t * local,))
-    small = jnp.concatenate([flat[:tokens], gains])
-    small = jnp.pad(small, (0, -small.shape[0] % 1024)).reshape(-1, 128)
-    flat = tree_sum(small, "tensor", n_tensor).reshape(-1)
     scale = lax.rsqrt(flat[:tokens] / features + EPS)
-    gains = flat[tokens : tokens + depth]
 
     turn = []
 
@@ -306,14 +327,6 @@
         return (starts[:, None] + steps + (steps >= at[..., None])).reshape(at.shape[:-1] + (rest,))
 
     owners = jnp.arange(n_dp, dtype=jnp.int32)[:, None]
-    chosen_tokens = (owners * owned + chosen_of(every_at)).reshape(-1)
-    is_chosen = chosen_tokens[:, None] == jnp.arange(tokens)
-    piece = jnp.dot(is_chosen.astype(jnp.bfloat16), hidden, preferred_element_type=F32).astype(jnp.bfloat16)
-    chosen_scale = jnp.sum(jnp.where(is_chosen, scale, 0.0), axis=1)
-    if relayed:
-        gathered = gather_pieces(piece, nz, nx, (drafts,))
-    else:
-        gathered = {(0, 0): lax.all_gather(piece, "tensor", axis=1, tiled=True)}
 
     hops = [k % n_y for k in range(1, n_y + 1)]
     groups = jnp.stack([((y + k) % n_y) * 2 + core for core in (1 - c, c) for k in hops])
@@ -341,25 +354,22 @@
         return keep, lax.ppermute(send, "dp", core_pairs)
 
     place = jnp.stack([((z ^ dz) * nx + (x ^ k)) if relayed else 0 * z for dz, k in offsets]).astype(jnp.int32)
-    order = grouped(owners * requests + jnp.arange(requests, dtype=jnp.int32))
-    by_piece = gains.reshape(-1, local if relayed else depth)
-
-    def met(*at):
-        return tuple(whole[o] for o in at) if relayed and nz > 2 and nx == 2 else ()
-
-    normed = prepare(
-        [gathered[o] for o in offsets],
+    order = jnp.concatenate(
+        [grouped(owners * owned + chosen_of(every_at)), grouped(owners * owned + others_of(every_at))]
+    )
+    chosen_normed, normed = prepare(
+        [whole[o] for o in offsets],
         place,
-        held_after(next_turn(order), *met((1, 0), (2, 0), (0, 1), (1, 1))),
-        chosen_scale[:, None],
-        by_piece,
+        held_after(order, drafts),
+        scale[:, None],
+        gains.reshape(-1, local if relayed else depth),
         depth,
+        n_dp * requests,
     )
-    turn.append(normed)
-    first_heads = [do_head(normed, 0, FIRST_PARTS, TILES[0])]
-    normed = held_after(normed, *met((3, 0), (2, 1)))
-    for p in range(1, len(FIRST_PARTS)):
-        first_heads.append(do_head(normed, p, FIRST_PARTS, TILES[0]))
+    drafts = held_after(drafts, normed)
+    drafts = lax.all_to_all(drafts, "tensor", split_axis=0, concat_axis=0, tiled=True)
+
+    first_heads = [do_head(chosen_normed, p, FIRST_PARTS, TILES[0]) for p in range(len(FIRST_PARTS))]
     chosen_far = []
 
     def send_chosen(p):
@@ -376,7 +386,7 @@
 
     def do_chosen(p):
         keep, came = first_heads[p]
-        part_ids = next_turn(ids[:requests] - span(FIRST_PARTS, p)[0])
+        part_ids = held_after(next_turn(ids[:requests] - span(FIRST_PARTS, p)[0]), drafts)
         logits, stats = finish_chosen(part_ids, keep, came, chosen_far[p], (n_y - 1) * requests)
         chosen_logits.append(logits)
         chosen_stats.append(stats)
@@ -385,12 +395,6 @@
     for p in range(len(FIRST_PARTS) - 1):
         send_chosen(p)
 
-    order = grouped(owners * owned + others_of(every_at))
-    normed = prepare([whole[o] for o in offsets], place, next_turn(order), scale[:, None], by_piece, depth)
-    turn.append(normed)
-    send_chosen(len(FIRST_PARTS) - 1)
-    drafts = held_after(drafts, normed)
-    drafts = lax.all_to_all(drafts, "tensor", split_axis=0, concat_axis=0, tiled=True)
     rest_heads, coded_far, other_stats = [], [], []
 
     def send_others(p):
@@ -411,16 +415,14 @@
     for p in range(len(REST_PARTS)):
         rest_heads.append(do_head(normed, p, REST_PARTS, TILES[1]))
         if p == 0:
-            turn.append(drafts)
-            for q in range(len(FIRST_PARTS)):
-                do_chosen(q)
+            send_chosen(len(FIRST_PARTS) - 1)
         else:
             send_others(p - 1)
-    for p in range(len(REST_PARTS) - 2):
-        do_others(p)
+        if p < len(FIRST_PARTS):
+            do_chosen(p)
     send_others(len(REST_PARTS) - 1)
     sent_last = turn[-1]
-    for p in range(max(len(REST_PARTS) - 2, 0), len(REST_PARTS)):
+    for p in range(len(REST_PARTS)):
         do_others(p)
 
     def joined(stats):

time: 272 us -> 258 us (0.949)
  starting transfers between devices: 43.4 us -> 37.7 us
  waiting for transfers between devices: 62.2 us -> 59.2 us
    ppermute x0 -> x3, waiting for transfers between devices: none -> 21.6 us  [the longest x2 21.6 us: shards(): lax.ppermute(small, 'tensor', [(i, i ^ bit) for i in range(n_tensor)])]
    ppermute x5 -> x2, waiting for transfers between devices: 18.2 us -> 1.09 us  [tree_sum(): lax.ppermute(value, axis, [(i, i ^ bit) for i in range(count)])]
    ppermute x14 -> x7, starting transfers between devices: 18.7 us -> 12 us  [step(): return lax.ppermute(value, 'tensor', [(i, i ^ bits) for i in range(count)])]
    ppermute x3, waiting for transfers between devices: 6.74 us -> 1.25 us  [send_others(): far.append(lax.ppermute(coded, 'dp', y_pairs(k)))]
    ppermute x0 -> x3, starting transfers between devices: none -> 3.51 us  [the longest x2 1.96 us: shards(): lax.ppermute(small, 'tensor', [(i, i ^ bit) for i in range(n_tensor)])]
    ppermute x14 -> x7, waiting for transfers between devices: 28.1 us -> 24.9 us  [step(): return lax.ppermute(value, 'tensor', [(i, i ^ bits) for i in range(count)])]
    unnamed x68 -> x56, local copies, waits for them, and re-layouts: 4.81 us -> 6.89 us
    pallas_call x2 -> x1, Pallas kernels: 11.5 us -> 9.66 us  [prepare(): pl.pallas_call(functools.partial(prepare_kernel, len(pieces)), out_shape=...]
  transfers between devices with their start and end apart: 36 -> 29, of which waited for: 15 -> 12; matrix products, arithmetic and copies ran while one was open for 11% -> 9% of each run, Pallas kernels for 40% -> 38%
where the time goes in v3:
time: 258 us; the launch traced here: 256 us
  Pallas kernels  125 us (48%)
  waiting for transfers between devices  59.2 us (23%)
  starting transfers between devices  37.7 us (15%)
  local copies, waits for them, and re-layouts  20.9 us (8%)
  other arithmetic  12.1 us (5%)
    pallas_call x5, Pallas kernels, head(): pl.pallas_call(head_kernel, out_shape=(half, half), grid=(width // tile,)...  78.9 us
    ppermute x7, waiting for transfers between devices, step(): return lax.ppermute(value, 'tensor', [(i, i ^ bits) for i in range(count)])  24.9 us
    ppermute x2, waiting for transfers between devices, shards(): lax.ppermute(small, 'tensor', [(i, i ^ bit) for i in range(n_tensor)])  21.6 us
    pallas_call x3, Pallas kernels, finish_others(): pl.pallas_call(functools.partial(finish_others_kernel, len(codeds)), out_...  13.1 us
    pallas_call x3, Pallas kernels, encode(): pl.pallas_call(encode_kernel, out_shape=jax.ShapeDtypeStruct((count, widt...  12.3 us
    ppermute x7, starting transfers between devices, step(): return lax.ppermute(value, 'tensor', [(i, i ^ bits) for i in range(count)])  12 us
    ppermute x6, waiting for transfers between devices, tree_merge(): other = lax.ppermute(stats, axis, [(i, i ^ bit) for i in range(count)])  10.3 us
    ppermute x6, starting transfers between devices, tree_merge(): other = lax.ppermute(stats, axis, [(i, i ^ bit) for i in range(count)])  9.73 us
  transfers between devices with their start and end apart: 29, of which 12 were waited for; matrix products, arithmetic and copies ran while one was open for 9% of the time, Pallas kernels for 38%

profile of v3, /device:TPU:0, one launch (start us, length us, event | category | flops | bytes accessed | tf_op | source)
XLA Modules:
  0.0 255.9 jit_solution(5995607908615672588)
XLA Ops:
  0.6 4.1 %collective-permute-start.2 = (bf16[640,512]{1,0:T(8,128)(2,1)}, bf16[640,512]{1,0:T(8,128)(2,1)S(1)}, u32[]{:S(2)}, u32[]{:S(2)}) collective-permute-start(bf16[640,512]{1,0:T(8,128)(2,1)} %refs_0_.1), channel_id=1, source_target_pairs={{0,4},{1,5},{2,6},{3,7},{4,0},{5,1},{6,2},{7,3},{8,12},{9,13},{10,... | collective-permute-start | bytes 1966088 | tf_op jit(solution)/shard_map/ppermute | solution.py:55
  16.1 18.4 %collective-permute-done.1 = f32[40,128]{1,0:T(8,128)S(1)} collective-permute-done((f32[40,128]{1,0:T(8,128)S(1)}, f32[40,128]{1,0:T(8,128)S(1)}, u32[]{:S(2)}, u32[]{:S(2)}) %collective-permute-start.1) | collective-permute-done | bytes 20512 | tf_op jit(solution)/shard_map/ppermute | solution.py:299
  36.0 3.2 %collective-permute-done.3 = f32[40,128]{1,0:T(8,128)S(1)} collective-permute-done((f32[40,128]{1,0:T(8,128)S(1)}, f32[40,128]{1,0:T(8,128)S(1)}, u32[]{:S(2)}, u32[]{:S(2)}) %collective-permute-start.3) | collective-permute-done | bytes 20512 | tf_op jit(solution)/shard_map/ppermute | solution.py:299
  44.9 6.4 %select_drafts.1 = f32[8,4,8192]{2,1,0:T(4,128)} custom-call(s32[4]{0:T(128)} %dynamic_slice.4.at, f32[20,65536]{1,0:T(8,128)} %drafts.1), custom_call_target="tpu_custom_call" | custom-call | flops 1024 | bytes 1024 | tf_op jit(solution)/shard_map/select_drafts/pallas_call | solution.py:247
  56.0 12.3 %collective-permute-done.9.refs_5_ = bf16[640,512]{1,0:T(8,128)(2,1)S(1)} collective-permute-done((bf16[640,512]{1,0:T(8,128)(2,1)S(1)}, bf16[640,512]{1,0:T(8,128)(2,1)S(1)}, u32[]{:S(2)}, u32[]{:S(2)}) %collective-permute-start.9) | collective-permute-done | bytes 655392 | tf_op jit(solution)/shard_map/ppermute | solution.py:55
  72.8 11.4 %collective-permute-done.11.refs_7_ = bf16[640,512]{1,0:T(8,128)(2,1)S(1)} collective-permute-done((bf16[640,512]{1,0:T(8,128)(2,1)S(1)}, bf16[640,512]{1,0:T(8,128)(2,1)S(1)}, u32[]{:S(2)}, u32[]{:S(2)}) %collective-permute-start.11) | collective-permute-done | bytes 655392 | tf_op jit(solution)/shard_map/ppermute | solution.py:55
  85.0 9.7 %prepare.1 = (bf16[128,4096]{1,0:T(8,128)(2,1)}, bf16[512,4096]{1,0:T(8,128)(2,1)}) custom-call(s32[8]{0:T(128)} %stack.96.place, s32[640,1]{1,0:T(8,128)} %copy.66.order, f32[640,1]{1,0:T(8,128)} %bitcast.97, f32[8,512]{1,0:T(8,128)} %reshape.172.gain, bf16[640,512]{1,0:T(8,128)(2,1)} %refs_0_.1, bf16[640,512]{1,0:T(8,128)(2,1)} %copy-done.6, ...), custom_call_target="tpu_custom_call" | custom-call | flops 1024 | bytes 1024 | tf_op jit(solution)/shard_map/prepare/pallas_call | solution.py:95
  94.7 13.6 %head.5 = (f32[64,4096]{1,0:T(8,128)}, f32[64,4096]{1,0:T(8,128)}) custom-call(bf16[128,4096]{1,0:T(8,128)(2,1)} %get-tuple-element.50.x, bf16[4096,8192]{1,0:T(8,128)(2,1)} %w.9), custom_call_target="tpu_custom_call" | custom-call | flops 34359738368 | bytes 33554432 | tf_op jit(solution)/shard_map/head/pallas_call | solution.py:121
  108.3 13.6 %head.6 = (f32[64,4096]{1,0:T(8,128)}, f32[64,4096]{1,0:T(8,128)}) custom-call(bf16[128,4096]{1,0:T(8,128)(2,1)} %get-tuple-element.50.x, bf16[4096,8192]{1,0:T(8,128)(2,1)} %w.9), custom_call_target="tpu_custom_call" | custom-call | flops 34359738368 | bytes 33554432 | tf_op jit(solution)/shard_map/head/pallas_call | solution.py:121
  122.4 5.0 %all-to-all-start = ((f32[8,4,8192]{2,1,0:T(4,128)}), f32[8,4,8192]{2,1,0:T(4,128)S(1)}, u32[]{:S(2)}, u32[]{:S(2)}) async-start(f32[8,4,8192]{2,1,0:T(4,128)} %select_drafts.1), calls=%async_computation | async-start | bytes 2097152 | tf_op jit(solution)/shard_map/all_to_all | solution.py:370
  130.1 23.7 %head.7 = (f32[256,4096]{1,0:T(8,128)}, f32[256,4096]{1,0:T(8,128)}) custom-call(bf16[512,4096]{1,0:T(8,128)(2,1)} %get-tuple-element.70.x, bf16[4096,8192]{1,0:T(8,128)(2,1)} %w.9), custom_call_target="tpu_custom_call" | custom-call | flops 137438953472 | bytes 33554432 | tf_op jit(solution)/shard_map/head/pallas_call | solution.py:121
  157.6 2.3 finish_chosen.2
  159.9 14.0 %head.8 = (f32[256,2048]{1,0:T(8,128)}, f32[256,2048]{1,0:T(8,128)}) custom-call(bf16[512,4096]{1,0:T(8,128)(2,1)} %get-tuple-element.70.x, bf16[4096,8192]{1,0:T(8,128)(2,1)} %w.9), custom_call_target="tpu_custom_call" | custom-call | flops 68719476736 | bytes 16777216 | tf_op jit(solution)/shard_map/head/pallas_call | solution.py:121
  176.0 4.6 %encode.3 = s16[128,4224]{1,0:T(8,128)(2,1)} custom-call(f32[256,4096]{1,0:T(8,128)} %get-tuple-element.65.keep, f32[256,4096]{1,0:T(8,128)} %collective-permute-done.15.came), custom_call_target="tpu_custom_call" | custom-call | flops 1024 | bytes 1024 | tf_op jit(solution)/shard_map/encode/pallas_call | solution.py:163
  187.6 14.0 %head.9 = (f32[256,2048]{1,0:T(8,128)}, f32[256,2048]{1,0:T(8,128)}) custom-call(bf16[512,4096]{1,0:T(8,128)(2,1)} %get-tuple-element.70.x, bf16[4096,8192]{1,0:T(8,128)(2,1)} %w.9), custom_call_target="tpu_custom_call" | custom-call | flops 68719476736 | bytes 16777216 | tf_op jit(solution)/shard_map/head/pallas_call | solution.py:121
  204.5 3.8 %encode.4 = s16[128,2176]{1,0:T(8,128)(2,1)} custom-call(f32[256,2048]{1,0:T(8,128)} %get-tuple-element.72.keep, f32[256,2048]{1,0:T(8,128)} %copy-done), custom_call_target="tpu_custom_call" | custom-call | flops 1024 | bytes 1024 | tf_op jit(solution)/shard_map/encode/pallas_call | solution.py:163
  209.6 2.4 collective-permute-start.19
  215.5 3.8 %encode.5 = s16[128,2176]{1,0:T(8,128)(2,1)} custom-call(f32[256,2048]{1,0:T(8,128)} %get-tuple-element.74.keep, f32[256,2048]{1,0:T(8,128)} %copy-done.1), custom_call_target="tpu_custom_call" | custom-call | flops 1024 | bytes 1024 | tf_op jit(solution)/shard_map/encode/pallas_call | solution.py:163
  220.9 4.8 %finish_others.3 = f32[128,128]{1,0:T(8,128)} custom-call(s32[128,1]{1,0:T(8,128)} %copy.73.ids, f32[256,4096]{1,0:T(8,128)} %get-tuple-element.65.keep, f32[256,4096]{1,0:T(8,128)} %collective-permute-done.15.came, s16[128,4224]{1,0:T(8,128)(2,1)} %collective-permute-done.22.refs_0_), custom_call_target="tpu_custom_call" | custom-call | flops 1024 | bytes 1024 | tf_op jit(solution)/shard_map/finish_others/pallas_call | solution.py:226
  227.3 4.2 %finish_others.4 = f32[128,128]{1,0:T(8,128)} custom-call(s32[128,1]{1,0:T(8,128)} %copy.74.ids, f32[256,2048]{1,0:T(8,128)} %get-tuple-element.72.keep, f32[256,2048]{1,0:T(8,128)} %copy-done, s16[128,2176]{1,0:T(8,128)(2,1)} %copy-done.13), custom_call_target="tpu_custom_call" | custom-call | flops 1024 | bytes 1024 | tf_op jit(solution)/shard_map/finish_others/pallas_call | solution.py:226
  236.1 4.2 %finish_others.5 = f32[128,128]{1,0:T(8,128)} custom-call(s32[128,1]{1,0:T(8,128)} %copy.75.ids, f32[256,2048]{1,0:T(8,128)} %get-tuple-element.74.keep, f32[256,2048]{1,0:T(8,128)} %copy-done.1, s16[128,2176]{1,0:T(8,128)(2,1)} %copy-done.14), custom_call_target="tpu_custom_call" | custom-call | flops 1024 | bytes 1024 | tf_op jit(solution)/shard_map/finish_others/pallas_call | solution.py:226
  242.3 3.0 %collective-permute-done.25 = f32[3,160]{1,0:T(4,128)S(1)} collective-permute-done((f32[3,160]{1,0:T(4,128)S(1)}, f32[3,160]{1,0:T(4,128)S(1)}, u32[]{:S(2)}, u32[]{:S(2)}) %collective-permute-start.25) | collective-permute-done | bytes 1952 | tf_op jit(solution)/shard_map/ppermute | solution.py:38
  246.1 3.0 %collective-permute-done.26 = f32[3,160]{1,0:T(4,128)S(1)} collective-permute-done((f32[3,160]{1,0:T(4,128)S(1)}, f32[3,160]{1,0:T(4,128)S(1)}, u32[]{:S(2)}, u32[]{:S(2)}) %collective-permute-start.26) | collective-permute-done | bytes 1952 | tf_op jit(solution)/shard_map/ppermute | solution.py:38
  249.2 2.4 collective-permute-start.27
  (211 shorter events, 66.8 us)
Async XLA Ops:
  0.6 33.8 %collective-permute-start.2 = (bf16[640,512]{1,0:T(8,128)(2,1)}, bf16[640,512]{1,0:T(8,128)(2,1)S(1)}, u32[]{:S(2)}, u32[]{:S(2)}) collective-permute-start(bf16[640,512]{1,0:T(8,128)(2,1)} %refs_0_.1), channel_id=1, source_target_pairs={{0,4},{1,5},{2,6},{3,7},{4,0},{5,1},{6,2},{7,3},{8,12},{9,13},{10,... | collective-permute-start | bytes 1966088 | tf_op jit(solution)/shard_map/ppermute | solution.py:55
  4.7 34.5 %collective-permute-start.6 = (bf16[640,512]{1,0:T(8,128)(2,1)}, bf16[640,512]{1,0:T(8,128)(2,1)S(1)}, u32[]{:S(2)}, u32[]{:S(2)}) collective-permute-start(bf16[640,512]{1,0:T(8,128)(2,1)} %refs_0_.1), channel_id=1, source_target_pairs={{0,2},{1,3},{2,0},{3,1},{4,6},{5,7},{6,4},{7,5},{8,10},{9,11},{10,... | collective-permute-start | bytes 1966088 | tf_op jit(solution)/shard_map/ppermute | solution.py:55
  8.5 5.7 %collective-permute-start = (f32[40,128]{1,0:T(8,128)S(1)}, f32[40,128]{1,0:T(8,128)S(1)}, u32[]{:S(2)}, u32[]{:S(2)}) collective-permute-start(f32[40,128]{1,0:T(8,128)S(1)} %fusion.1), channel_id=1, source_target_pairs={{0,1},{1,0},{2,3},{3,2},{4,5},{5,4},{6,7},{7,6},{8,9},{9,8},{10,11... | collective-permute-start | bytes 61448 | tf_op jit(solution)/shard_map/ppermute | solution.py:288
  14.3 20.2 %collective-permute-start.1 = (f32[40,128]{1,0:T(8,128)S(1)}, f32[40,128]{1,0:T(8,128)S(1)}, u32[]{:S(2)}, u32[]{:S(2)}) collective-permute-start(f32[40,128]{1,0:T(8,128)S(1)} %fusion.18), channel_id=1, source_target_pairs={{0,2},{1,3},{2,0},{3,1},{4,6},{5,7},{6,4},{7,5},{8,10},{9,11},{10,... | collective-permute-start | bytes 61448 | tf_op jit(solution)/shard_map/ppermute | solution.py:299
  14.8 24.5 %collective-permute-start.7 = (bf16[640,512]{1,0:T(8,128)(2,1)}, bf16[640,512]{1,0:T(8,128)(2,1)S(1)}, u32[]{:S(2)}, u32[]{:S(2)}) collective-permute-start(bf16[640,512]{1,0:T(8,128)(2,1)} %refs_0_.1), channel_id=1, source_target_pairs={{0,1},{1,0},{2,3},{3,2},{4,5},{5,4},{6,7},{7,6},{8,9},{9,8},{10,11... | collective-permute-start | bytes 1966088 | tf_op jit(solution)/shard_map/ppermute | solution.py:55
  34.5 4.7 %collective-permute-start.3 = (f32[40,128]{1,0:T(8,128)S(1)}, f32[40,128]{1,0:T(8,128)S(1)}, u32[]{:S(2)}, u32[]{:S(2)}) collective-permute-start(f32[40,128]{1,0:T(8,128)S(1)} %fusion.23), channel_id=1, source_target_pairs={{0,4},{1,5},{2,6},{3,7},{4,0},{5,1},{6,2},{7,3},{8,12},{9,13},{10,... | collective-permute-start | bytes 61448 | tf_op jit(solution)/shard_map/ppermute | solution.py:299
  39.3 14.1 %collective-permute-start.8 = (bf16[640,512]{1,0:T(8,128)(2,1)S(1)}, bf16[640,512]{1,0:T(8,128)(2,1)S(1)}, u32[]{:S(2)}, u32[]{:S(2)}) collective-permute-start(bf16[640,512]{1,0:T(8,128)(2,1)S(1)} %collective-permute-done.6.refs_2_), channel_id=1, source_target_pairs={{0,1},{1,0},{2,3},{3,2},{4,5},{5,4},{6,7},{7,6},{8,9},{9,8},{10,11... | collective-permute-start | bytes 1966088 | tf_op jit(solution)/shard_map/ppermute | solution.py:55
  42.1 13.4 %collective-permute-start.5 = (f32[8,128]{1,0:T(8,128)S(1)}, f32[8,128]{1,0:T(8,128)S(1)}, u32[]{:S(2)}, u32[]{:S(2)}) collective-permute-start(f32[8,128]{1,0:T(8,128)S(1)} %fusion.22), channel_id=1, source_target_pairs={{0,16},{8,24},{16,0},{24,8},{1,17},{9,25},{17,1},{25,9},{2,18},{10... | collective-permute-start | bytes 12296 | tf_op jit(solution)/shard_map/ppermute | solution.py:23
  51.9 16.5 %collective-permute-start.9 = (bf16[640,512]{1,0:T(8,128)(2,1)S(1)}, bf16[640,512]{1,0:T(8,128)(2,1)S(1)}, u32[]{:S(2)}, u32[]{:S(2)}) collective-permute-start(bf16[640,512]{1,0:T(8,128)(2,1)S(1)} %collective-permute-done.2.refs_1_), channel_id=1, source_target_pairs={{0,1},{1,0},{2,3},{3,2},{4,5},{5,4},{6,7},{7,6},{8,9},{9,8},{10,11... | collective-permute-start | bytes 1966088 | tf_op jit(solution)/shard_map/ppermute | solution.py:55
  53.3 15.9 %collective-permute-start.10 = (bf16[640,512]{1,0:T(8,128)(2,1)S(1)}, bf16[640,512]{1,0:T(8,128)(2,1)S(1)}, u32[]{:S(2)}, u32[]{:S(2)}) collective-permute-start(bf16[640,512]{1,0:T(8,128)(2,1)S(1)} %collective-permute-done.2.refs_1_), channel_id=1, source_target_pairs={{0,2},{1,3},{2,0},{3,1},{4,6},{5,7},{6,4},{7,5},{8,10},{9,11},{10,... | collective-permute-start | bytes 1966088 | tf_op jit(solution)/shard_map/ppermute | solution.py:55
  69.3 14.9 %collective-permute-start.11 = (bf16[640,512]{1,0:T(8,128)(2,1)S(1)}, bf16[640,512]{1,0:T(8,128)(2,1)S(1)}, u32[]{:S(2)}, u32[]{:S(2)}) collective-permute-start(bf16[640,512]{1,0:T(8,128)(2,1)S(1)} %collective-permute-done.10.refs_6_), channel_id=1, source_target_pairs={{0,1},{1,0},{2,3},{3,2},{4,5},{5,4},{6,7},{7,6},{8,9},{9,8},{10,11... | collective-permute-start | bytes 1966088 | tf_op jit(solution)/shard_map/ppermute | solution.py:55
  108.3 19.1 %collective-permute-start.12 = (f32[64,4096]{1,0:T(8,128)}, f32[64,4096]{1,0:T(8,128)}, u32[]{:S(2)}, u32[]{:S(2)}) collective-permute-start(f32[64,4096]{1,0:T(8,128)} %get-tuple-element.54), channel_id=1, source_target_pairs={{0,8},{8,0},{16,24},{24,16},{1,9},{9,1},{17,25},{25,17},{2,10},{10... | collective-permute-start | bytes 3145736 | tf_op jit(solution)/shard_map/ppermute | solution.py:354
  121.9 31.9 %collective-permute-start.13 = (f32[64,4096]{1,0:T(8,128)}, f32[64,4096]{1,0:T(8,128)S(1)}, u32[]{:S(2)}, u32[]{:S(2)}) collective-permute-start(f32[64,4096]{1,0:T(8,128)} %get-tuple-element.58), channel_id=1, source_target_pairs={{0,8},{8,0},{16,24},{24,16},{1,9},{9,1},{17,25},{25,17},{2,10},{10... | collective-permute-start | bytes 3145736 | tf_op jit(solution)/shard_map/ppermute | solution.py:354
  122.4 33.6 %all-to-all-start = ((f32[8,4,8192]{2,1,0:T(4,128)}), f32[8,4,8192]{2,1,0:T(4,128)S(1)}, u32[]{:S(2)}, u32[]{:S(2)}) async-start(f32[8,4,8192]{2,1,0:T(4,128)} %select_drafts.1), calls=%async_computation | async-start | bytes 2097152 | tf_op jit(solution)/shard_map/all_to_all | solution.py:370
  129.3 27.5 %collective-permute-start.14 = (f32[32,4096]{1,0:T(8,128)}, f32[32,4096]{1,0:T(8,128)S(1)}, u32[]{:S(2)}, u32[]{:S(2)}) collective-permute-start(f32[32,4096]{1,0:T(8,128)} %slice_add_fusion.1), channel_id=1, source_target_pairs={{0,16},{8,24},{16,0},{24,8},{1,17},{9,25},{17,1},{25,9},{2,18},{10... | collective-permute-start | bytes 1572872 | tf_op jit(solution)/shard_map/ppermute | solution.py:382
  154.8 27.4 %collective-permute-start.16 = (f32[32,4096]{1,0:T(8,128)}, f32[32,4096]{1,0:T(8,128)}, u32[]{:S(2)}, u32[]{:S(2)}) collective-permute-start(f32[32,4096]{1,0:T(8,128)} %slice_add_fusion), channel_id=1, source_target_pairs={{0,16},{8,24},{16,0},{24,8},{1,17},{9,25},{17,1},{25,9},{2,18},{10... | collective-permute-start | bytes 1572872 | tf_op jit(solution)/shard_map/ppermute | solution.py:382
  156.0 20.0 %collective-permute-start.15 = (f32[256,4096]{1,0:T(8,128)}, f32[256,4096]{1,0:T(8,128)}, u32[]{:S(2)}, u32[]{:S(2)}) collective-permute-start(f32[256,4096]{1,0:T(8,128)} %get-tuple-element.66), channel_id=1, source_target_pairs={{0,8},{8,0},{16,24},{24,16},{1,9},{9,1},{17,25},{25,17},{2,10},{10... | collective-permute-start | bytes 12582920 | tf_op jit(solution)/shard_map/ppermute | solution.py:354
  173.9 29.3 %collective-permute-start.20 = (f32[256,2048]{1,0:T(8,128)}, f32[256,2048]{1,0:T(8,128)S(1)}, u32[]{:S(2)}, u32[]{:S(2)}) collective-permute-start(f32[256,2048]{1,0:T(8,128)} %get-tuple-element.73), channel_id=1, source_target_pairs={{0,8},{8,0},{16,24},{24,16},{1,9},{9,1},{17,25},{25,17},{2,10},{10... | collective-permute-start | bytes 6291464 | tf_op jit(solution)/shard_map/ppermute | solution.py:354
  180.6 40.3 %collective-permute-start.22 = (s16[128,4224]{1,0:T(8,128)(2,1)}, s16[128,4224]{1,0:T(8,128)(2,1)}, u32[]{:S(2)}, u32[]{:S(2)}) collective-permute-start(s16[128,4224]{1,0:T(8,128)(2,1)} %encode.3), channel_id=1, source_target_pairs={{0,16},{8,24},{16,0},{24,8},{1,17},{9,25},{17,1},{25,9},{2,18},{10... | collective-permute-start | bytes 3244040 | tf_op jit(solution)/shard_map/ppermute | solution.py:406
  185.5 16.1 %collective-permute-start.17 = (f32[3,32]{1,0:T(4,128)S(1)}, f32[3,32]{1,0:T(4,128)S(1)}, u32[]{:S(2)}, u32[]{:S(2)}) collective-permute-start(f32[3,32]{1,0:T(4,128)S(1)} %pad_maximum_fusion.3), channel_id=1, source_target_pairs={{0,1},{1,0},{2,3},{3,2},{4,5},{5,4},{6,7},{7,6},{8,9},{9,8},{10,11... | collective-permute-start | bytes 1160 | tf_op jit(solution)/shard_map/ppermute | solution.py:38
  201.6 12.6 %collective-permute-start.21 = (f32[256,2048]{1,0:T(8,128)}, f32[256,2048]{1,0:T(8,128)S(1)}, u32[]{:S(2)}, u32[]{:S(2)}) collective-permute-start(f32[256,2048]{1,0:T(8,128)} %get-tuple-element.75), channel_id=1, source_target_pairs={{0,8},{8,0},{16,24},{24,16},{1,9},{9,1},{17,25},{25,17},{2,10},{10... | collective-permute-start | bytes 6291464 | tf_op jit(solution)/shard_map/ppermute | solution.py:354
  201.7 7.9 %collective-permute-start.18 = (f32[3,32]{1,0:T(4,128)S(1)}, f32[3,32]{1,0:T(4,128)S(1)}, u32[]{:S(2)}, u32[]{:S(2)}) collective-permute-start(f32[3,32]{1,0:T(4,128)S(1)} %pad_maximum_fusion.4), channel_id=1, source_target_pairs={{0,2},{1,3},{2,0},{3,1},{4,6},{5,7},{6,4},{7,5},{8,10},{9,11},{10,... | collective-permute-start | bytes 1160 | tf_op jit(solution)/shard_map/ppermute | solution.py:38
  208.4 18.2 %collective-permute-start.23 = (s16[128,2176]{1,0:T(8,128)(2,1)}, s16[128,2176]{1,0:T(8,128)(2,1)S(1)}, u32[]{:S(2)}, u32[]{:S(2)}) collective-permute-start(s16[128,2176]{1,0:T(8,128)(2,1)} %encode.4), channel_id=1, source_target_pairs={{0,16},{8,24},{16,0},{24,8},{1,17},{9,25},{17,1},{25,9},{2,18},{10... | collective-permute-start | bytes 1671176 | tf_op jit(solution)/shard_map/ppermute | solution.py:406
  219.4 15.9 %collective-permute-start.24 = (s16[128,2176]{1,0:T(8,128)(2,1)}, s16[128,2176]{1,0:T(8,128)(2,1)S(1)}, u32[]{:S(2)}, u32[]{:S(2)}) collective-permute-start(s16[128,2176]{1,0:T(8,128)(2,1)} %encode.5), channel_id=1, source_target_pairs={{0,16},{8,24},{16,0},{24,8},{1,17},{9,25},{17,1},{25,9},{2,18},{10... | collective-permute-start | bytes 1671176 | tf_op jit(solution)/shard_map/ppermute | solution.py:406
  (32 other events, 275.0 us)

commit v4 on v3

--- a/solution.py
+++ b/solution.py
@@ -48,7 +48,7 @@
     return lax.optimization_barrier((value,) + earlier)[0]
 
 
-def gather_pieces(piece, nz, nx, first, during):
+def gather_pieces(piece, nz, nx, first):
     count = nz * nx
 
     def step(value, bits):
@@ -66,7 +66,7 @@
     for offset in range(2, nz):
         near = offset & -offset
         if (offset, 0) not in pieces:
-            before = [pieces[o, k] for o in done for k in range(1, nx)] + [during]
+            before = [pieces[o, k] for o in done for k in range(1, nx)]
             pieces[offset, 0] = step(held_after(pieces[offset - near, 0], *before), near * nx)
         for k in range(1, nx):
             ahead = (pieces[offset - 1, k],) if offset > 2 else ()
@@ -288,14 +288,14 @@
         small = small + lax.ppermute(small, "tensor", [(i, i ^ 1) for i in range(n_tensor)])
     relayed = local % 128 == 0
     if relayed:
-        whole = gather_pieces(hidden, nz, nx, small, drafts)
+        whole = gather_pieces(hidden, nz, nx, small)
     else:
         whole = {(0, 0): lax.all_gather(hidden, "tensor", axis=1, tiled=True)}
     offsets = list(whole)
     bit = 2
     while bit < n_tensor:
         if relayed and bit == 4:
-            small = held_after(small, whole[nz // 2, 0])
+            small = held_after(small, whole[nz // 2, 0], drafts)
         small = small + lax.ppermute(small, "tensor", [(i, i ^ bit) for i in range(n_tensor)])
         bit *= 2
     flat = small.reshape(-1)

time: 258 us -> 257 us (level)
    ppermute x2, waiting for transfers between devices: 21.6 us -> 14 us  [shards(): lax.ppermute(small, 'tensor', [(i, i ^ bit) for i in range(n_tensor)])]
    ppermute x7, waiting for transfers between devices: 24.9 us -> 30.5 us  [step(): return lax.ppermute(value, 'tensor', [(i, i ^ bits) for i in range(count)])]
    unnamed x56 -> x52, local copies, waits for them, and re-layouts: 6.89 us -> 6.07 us
  transfers between devices with their start and end apart: 29 -> 29, of which waited for: 12 -> 11; matrix products, arithmetic and copies ran while one was open for 9% -> 9% of each run, Pallas kernels for 38% -> 38%
where the time goes in v4:
time: 257 us; the launch traced here: 255 us
  Pallas kernels  125 us (49%)
  waiting for transfers between devices  57.1 us (22%)
  starting transfers between devices  40 us (16%)
  local copies, waits for them, and re-layouts  20.2 us (8%)
  other arithmetic  12.1 us (5%)
    pallas_call x5, Pallas kernels, head(): pl.pallas_call(head_kernel, out_shape=(half, half), grid=(width // tile,)...  78.9 us
    ppermute x7, waiting for transfers between devices, step(): return lax.ppermute(value, 'tensor', [(i, i ^ bits) for i in range(count)])  30.5 us
    ppermute x2, waiting for transfers between devices, shards(): lax.ppermute(small, 'tensor', [(i, i ^ bit) for i in range(n_tensor)])  14 us
    pallas_call x3, Pallas kernels, finish_others(): pl.pallas_call(functools.partial(finish_others_kernel, len(codeds)), out_...  13.2 us
    pallas_call x3, Pallas kernels, encode(): pl.pallas_call(encode_kernel, out_shape=jax.ShapeDtypeStruct((count, widt...  12.3 us
    ppermute x7, starting transfers between devices, step(): return lax.ppermute(value, 'tensor', [(i, i ^ bits) for i in range(count)])  11.4 us
    ppermute x6, waiting for transfers between devices, tree_merge(): other = lax.ppermute(stats, axis, [(i, i ^ bit) for i in range(count)])  10.3 us
    ppermute x6, starting transfers between devices, tree_merge(): other = lax.ppermute(stats, axis, [(i, i ^ bit) for i in range(count)])  9.72 us
  transfers between devices with their start and end apart: 29, of which 11 were waited for; matrix products, arithmetic and copies ran while one was open for 9% of the time, Pallas kernels for 38%

profile of v4, /device:TPU:0, one launch (start us, length us, event | category | flops | bytes accessed | tf_op | source)
XLA Modules:
  0.0 255.4 jit_solution(3122952801969321211)
XLA Ops:
  0.6 4.1 %collective-permute-start.2 = (bf16[640,512]{1,0:T(8,128)(2,1)}, bf16[640,512]{1,0:T(8,128)(2,1)S(1)}, u32[]{:S(2)}, u32[]{:S(2)}) collective-permute-start(bf16[640,512]{1,0:T(8,128)(2,1)} %refs_0_.1), channel_id=1, source_target_pairs={{0,4},{1,5},{2,6},{3,7},{4,0},{5,1},{6,2},{7,3},{8,12},{9,13},{10,... | collective-permute-start | bytes 1966088 | tf_op jit(solution)/shard_map/ppermute | solution.py:55
  17.4 6.4 %select_drafts.1 = f32[8,4,8192]{2,1,0:T(4,128)} custom-call(s32[4]{0:T(128)} %dynamic_slice.4.at, f32[20,65536]{1,0:T(8,128)} %drafts.1), custom_call_target="tpu_custom_call" | custom-call | flops 1024 | bytes 1024 | tf_op jit(solution)/shard_map/select_drafts/pallas_call | solution.py:247
  23.7 10.7 %collective-permute-done.1 = f32[40,128]{1,0:T(8,128)S(1)} collective-permute-done((f32[40,128]{1,0:T(8,128)S(1)}, f32[40,128]{1,0:T(8,128)S(1)}, u32[]{:S(2)}, u32[]{:S(2)}) %collective-permute-start.1) | collective-permute-done | bytes 20512 | tf_op jit(solution)/shard_map/ppermute | solution.py:299
  36.0 3.2 %collective-permute-done.3 = f32[40,128]{1,0:T(8,128)S(1)} collective-permute-done((f32[40,128]{1,0:T(8,128)S(1)}, f32[40,128]{1,0:T(8,128)S(1)}, u32[]{:S(2)}, u32[]{:S(2)}) %collective-permute-start.3) | collective-permute-done | bytes 20512 | tf_op jit(solution)/shard_map/ppermute | solution.py:299
  45.4 11.6 %collective-permute-done.8.refs_4_ = bf16[640,512]{1,0:T(8,128)(2,1)S(1)} collective-permute-done((bf16[640,512]{1,0:T(8,128)(2,1)S(1)}, bf16[640,512]{1,0:T(8,128)(2,1)S(1)}, u32[]{:S(2)}, u32[]{:S(2)}) %collective-permute-start.8) | collective-permute-done | bytes 655392 | tf_op jit(solution)/shard_map/ppermute | solution.py:55
  59.1 8.9 %collective-permute-done.9.refs_5_ = bf16[640,512]{1,0:T(8,128)(2,1)S(1)} collective-permute-done((bf16[640,512]{1,0:T(8,128)(2,1)S(1)}, bf16[640,512]{1,0:T(8,128)(2,1)S(1)}, u32[]{:S(2)}, u32[]{:S(2)}) %collective-permute-start.9) | collective-permute-done | bytes 655392 | tf_op jit(solution)/shard_map/ppermute | solution.py:55
  71.5 10.0 %collective-permute-done.11.refs_7_ = bf16[640,512]{1,0:T(8,128)(2,1)} collective-permute-done((bf16[640,512]{1,0:T(8,128)(2,1)}, bf16[640,512]{1,0:T(8,128)(2,1)}, u32[]{:S(2)}, u32[]{:S(2)}) %collective-permute-start.11) | collective-permute-done | bytes 655392 | tf_op jit(solution)/shard_map/ppermute | solution.py:55
  81.6 9.6 %prepare.1 = (bf16[128,4096]{1,0:T(8,128)(2,1)}, bf16[512,4096]{1,0:T(8,128)(2,1)}) custom-call(s32[8]{0:T(128)} %stack.96.place, s32[640,1]{1,0:T(8,128)} %copy.66.order, f32[640,1]{1,0:T(8,128)} %bitcast.97, f32[8,512]{1,0:T(8,128)} %reshape.172.gain, bf16[640,512]{1,0:T(8,128)(2,1)} %refs_0_.1, bf16[640,512]{1,0:T(8,128)(2,1)} %copy-done.6, ...), custom_call_target="tpu_custom_call" | custom-call | flops 1024 | bytes 1024 | tf_op jit(solution)/shard_map/prepare/pallas_call | solution.py:95
  91.2 13.6 %head.5 = (f32[64,4096]{1,0:T(8,128)}, f32[64,4096]{1,0:T(8,128)}) custom-call(bf16[128,4096]{1,0:T(8,128)(2,1)} %get-tuple-element.50.x, bf16[4096,8192]{1,0:T(8,128)(2,1)} %w.9), custom_call_target="tpu_custom_call" | custom-call | flops 34359738368 | bytes 33554432 | tf_op jit(solution)/shard_map/head/pallas_call | solution.py:121
  104.8 13.6 %head.6 = (f32[64,4096]{1,0:T(8,128)}, f32[64,4096]{1,0:T(8,128)}) custom-call(bf16[128,4096]{1,0:T(8,128)(2,1)} %get-tuple-element.50.x, bf16[4096,8192]{1,0:T(8,128)(2,1)} %w.9), custom_call_target="tpu_custom_call" | custom-call | flops 34359738368 | bytes 33554432 | tf_op jit(solution)/shard_map/head/pallas_call | solution.py:121
  118.9 7.3 %all-to-all-start = ((f32[8,4,8192]{2,1,0:T(4,128)}), f32[8,4,8192]{2,1,0:T(4,128)S(1)}, u32[]{:S(2)}, u32[]{:S(2)}) async-start(f32[8,4,8192]{2,1,0:T(4,128)} %select_drafts.1), calls=%async_computation | async-start | bytes 2097152 | tf_op jit(solution)/shard_map/all_to_all | solution.py:370
  129.6 23.7 %head.7 = (f32[256,4096]{1,0:T(8,128)}, f32[256,4096]{1,0:T(8,128)}) custom-call(bf16[512,4096]{1,0:T(8,128)(2,1)} %get-tuple-element.70.x, bf16[4096,8192]{1,0:T(8,128)(2,1)} %w.9), custom_call_target="tpu_custom_call" | custom-call | flops 137438953472 | bytes 33554432 | tf_op jit(solution)/shard_map/head/pallas_call | solution.py:121
  158.7 14.0 %head.8 = (f32[256,2048]{1,0:T(8,128)}, f32[256,2048]{1,0:T(8,128)}) custom-call(bf16[512,4096]{1,0:T(8,128)(2,1)} %get-tuple-element.70.x, bf16[4096,8192]{1,0:T(8,128)(2,1)} %w.9), custom_call_target="tpu_custom_call" | custom-call | flops 68719476736 | bytes 16777216 | tf_op jit(solution)/shard_map/head/pallas_call | solution.py:121
  174.8 4.6 %encode.3 = s16[128,4224]{1,0:T(8,128)(2,1)} custom-call(f32[256,4096]{1,0:T(8,128)} %get-tuple-element.65.keep, f32[256,4096]{1,0:T(8,128)} %collective-permute-done.15.came), custom_call_target="tpu_custom_call" | custom-call | flops 1024 | bytes 1024 | tf_op jit(solution)/shard_map/encode/pallas_call | solution.py:163
  187.1 14.0 %head.9 = (f32[256,2048]{1,0:T(8,128)}, f32[256,2048]{1,0:T(8,128)}) custom-call(bf16[512,4096]{1,0:T(8,128)(2,1)} %get-tuple-element.70.x, bf16[4096,8192]{1,0:T(8,128)(2,1)} %w.9), custom_call_target="tpu_custom_call" | custom-call | flops 68719476736 | bytes 16777216 | tf_op jit(solution)/shard_map/head/pallas_call | solution.py:121
  204.0 3.8 %encode.4 = s16[128,2176]{1,0:T(8,128)(2,1)} custom-call(f32[256,2048]{1,0:T(8,128)} %get-tuple-element.72.keep, f32[256,2048]{1,0:T(8,128)} %copy-done), custom_call_target="tpu_custom_call" | custom-call | flops 1024 | bytes 1024 | tf_op jit(solution)/shard_map/encode/pallas_call | solution.py:163
  208.4 2.4 collective-permute-start.19
  214.3 3.8 %encode.5 = s16[128,2176]{1,0:T(8,128)(2,1)} custom-call(f32[256,2048]{1,0:T(8,128)} %get-tuple-element.74.keep, f32[256,2048]{1,0:T(8,128)} %copy-done.1), custom_call_target="tpu_custom_call" | custom-call | flops 1024 | bytes 1024 | tf_op jit(solution)/shard_map/encode/pallas_call | solution.py:163
  220.4 4.8 %finish_others.3 = f32[128,128]{1,0:T(8,128)} custom-call(s32[128,1]{1,0:T(8,128)} %copy.73.ids, f32[256,4096]{1,0:T(8,128)} %get-tuple-element.65.keep, f32[256,4096]{1,0:T(8,128)} %collective-permute-done.15.came, s16[128,4224]{1,0:T(8,128)(2,1)} %collective-permute-done.22.refs_0_), custom_call_target="tpu_custom_call" | custom-call | flops 1024 | bytes 1024 | tf_op jit(solution)/shard_map/finish_others/pallas_call | solution.py:226
  226.8 4.2 %finish_others.4 = f32[128,128]{1,0:T(8,128)} custom-call(s32[128,1]{1,0:T(8,128)} %copy.74.ids, f32[256,2048]{1,0:T(8,128)} %get-tuple-element.72.keep, f32[256,2048]{1,0:T(8,128)} %copy-done, s16[128,2176]{1,0:T(8,128)(2,1)} %copy-done.11), custom_call_target="tpu_custom_call" | custom-call | flops 1024 | bytes 1024 | tf_op jit(solution)/shard_map/finish_others/pallas_call | solution.py:226
  235.6 4.2 %finish_others.5 = f32[128,128]{1,0:T(8,128)} custom-call(s32[128,1]{1,0:T(8,128)} %copy.75.ids, f32[256,2048]{1,0:T(8,128)} %get-tuple-element.74.keep, f32[256,2048]{1,0:T(8,128)} %copy-done.1, s16[128,2176]{1,0:T(8,128)(2,1)} %copy-done.12), custom_call_target="tpu_custom_call" | custom-call | flops 1024 | bytes 1024 | tf_op jit(solution)/shard_map/finish_others/pallas_call | solution.py:226
  241.8 3.0 %collective-permute-done.25 = f32[3,160]{1,0:T(4,128)S(1)} collective-permute-done((f32[3,160]{1,0:T(4,128)S(1)}, f32[3,160]{1,0:T(4,128)S(1)}, u32[]{:S(2)}, u32[]{:S(2)}) %collective-permute-start.25) | collective-permute-done | bytes 1952 | tf_op jit(solution)/shard_map/ppermute | solution.py:38
  245.6 3.0 %collective-permute-done.26 = f32[3,160]{1,0:T(4,128)S(1)} collective-permute-done((f32[3,160]{1,0:T(4,128)S(1)}, f32[3,160]{1,0:T(4,128)S(1)}, u32[]{:S(2)}, u32[]{:S(2)}) %collective-permute-start.26) | collective-permute-done | bytes 1952 | tf_op jit(solution)/shard_map/ppermute | solution.py:38
  248.7 2.4 collective-permute-start.27
  (207 shorter events, 67.2 us)
Async XLA Ops:
  0.6 33.8 %collective-permute-start.2 = (bf16[640,512]{1,0:T(8,128)(2,1)}, bf16[640,512]{1,0:T(8,128)(2,1)S(1)}, u32[]{:S(2)}, u32[]{:S(2)}) collective-permute-start(bf16[640,512]{1,0:T(8,128)(2,1)} %refs_0_.1), channel_id=1, source_target_pairs={{0,4},{1,5},{2,6},{3,7},{4,0},{5,1},{6,2},{7,3},{8,12},{9,13},{10,... | collective-permute-start | bytes 1966088 | tf_op jit(solution)/shard_map/ppermute | solution.py:55
  4.7 34.5 %collective-permute-start.6 = (bf16[640,512]{1,0:T(8,128)(2,1)}, bf16[640,512]{1,0:T(8,128)(2,1)S(1)}, u32[]{:S(2)}, u32[]{:S(2)}) collective-permute-start(bf16[640,512]{1,0:T(8,128)(2,1)} %refs_0_.1), channel_id=1, source_target_pairs={{0,2},{1,3},{2,0},{3,1},{4,6},{5,7},{6,4},{7,5},{8,10},{9,11},{10,... | collective-permute-start | bytes 1966088 | tf_op jit(solution)/shard_map/ppermute | solution.py:55
  8.5 5.7 %collective-permute-start = (f32[40,128]{1,0:T(8,128)S(1)}, f32[40,128]{1,0:T(8,128)S(1)}, u32[]{:S(2)}, u32[]{:S(2)}) collective-permute-start(f32[40,128]{1,0:T(8,128)S(1)} %fusion.1), channel_id=1, source_target_pairs={{0,1},{1,0},{2,3},{3,2},{4,5},{5,4},{6,7},{7,6},{8,9},{9,8},{10,11... | collective-permute-start | bytes 61448 | tf_op jit(solution)/shard_map/ppermute | solution.py:288
  14.3 20.2 %collective-permute-start.1 = (f32[40,128]{1,0:T(8,128)S(1)}, f32[40,128]{1,0:T(8,128)S(1)}, u32[]{:S(2)}, u32[]{:S(2)}) collective-permute-start(f32[40,128]{1,0:T(8,128)S(1)} %fusion.18), channel_id=1, source_target_pairs={{0,2},{1,3},{2,0},{3,1},{4,6},{5,7},{6,4},{7,5},{8,10},{9,11},{10,... | collective-permute-start | bytes 61448 | tf_op jit(solution)/shard_map/ppermute | solution.py:299
  14.8 24.5 %collective-permute-start.7 = (bf16[640,512]{1,0:T(8,128)(2,1)}, bf16[640,512]{1,0:T(8,128)(2,1)S(1)}, u32[]{:S(2)}, u32[]{:S(2)}) collective-permute-start(bf16[640,512]{1,0:T(8,128)(2,1)} %refs_0_.1), channel_id=1, source_target_pairs={{0,1},{1,0},{2,3},{3,2},{4,5},{5,4},{6,7},{7,6},{8,9},{9,8},{10,11... | collective-permute-start | bytes 1966088 | tf_op jit(solution)/shard_map/ppermute | solution.py:55
  34.5 4.7 %collective-permute-start.3 = (f32[40,128]{1,0:T(8,128)S(1)}, f32[40,128]{1,0:T(8,128)S(1)}, u32[]{:S(2)}, u32[]{:S(2)}) collective-permute-start(f32[40,128]{1,0:T(8,128)S(1)} %fusion.23), channel_id=1, source_target_pairs={{0,4},{1,5},{2,6},{3,7},{4,0},{5,1},{6,2},{7,3},{8,12},{9,13},{10,... | collective-permute-start | bytes 61448 | tf_op jit(solution)/shard_map/ppermute | solution.py:299
  39.3 17.7 %collective-permute-start.8 = (bf16[640,512]{1,0:T(8,128)(2,1)S(1)}, bf16[640,512]{1,0:T(8,128)(2,1)S(1)}, u32[]{:S(2)}, u32[]{:S(2)}) collective-permute-start(bf16[640,512]{1,0:T(8,128)(2,1)S(1)} %collective-permute-done.6.refs_2_), channel_id=1, source_target_pairs={{0,1},{1,0},{2,3},{3,2},{4,5},{5,4},{6,7},{7,6},{8,9},{9,8},{10,11... | collective-permute-start | bytes 1966088 | tf_op jit(solution)/shard_map/ppermute | solution.py:55
  42.1 16.4 %collective-permute-start.5 = (f32[8,128]{1,0:T(8,128)S(1)}, f32[8,128]{1,0:T(8,128)S(1)}, u32[]{:S(2)}, u32[]{:S(2)}) collective-permute-start(f32[8,128]{1,0:T(8,128)S(1)} %fusion.22), channel_id=1, source_target_pairs={{0,16},{8,24},{16,0},{24,8},{1,17},{9,25},{17,1},{25,9},{2,18},{10... | collective-permute-start | bytes 12296 | tf_op jit(solution)/shard_map/ppermute | solution.py:23
  44.3 23.7 %collective-permute-start.9 = (bf16[640,512]{1,0:T(8,128)(2,1)S(1)}, bf16[640,512]{1,0:T(8,128)(2,1)S(1)}, u32[]{:S(2)}, u32[]{:S(2)}) collective-permute-start(bf16[640,512]{1,0:T(8,128)(2,1)S(1)} %collective-permute-done.2.refs_1_), channel_id=1, source_target_pairs={{0,1},{1,0},{2,3},{3,2},{4,5},{5,4},{6,7},{7,6},{8,9},{9,8},{10,11... | collective-permute-start | bytes 1966088 | tf_op jit(solution)/shard_map/ppermute | solution.py:55
  57.0 11.0 %collective-permute-start.10 = (bf16[640,512]{1,0:T(8,128)(2,1)S(1)}, bf16[640,512]{1,0:T(8,128)(2,1)}, u32[]{:S(2)}, u32[]{:S(2)}) collective-permute-start(bf16[640,512]{1,0:T(8,128)(2,1)S(1)} %collective-permute-done.2.refs_1_), channel_id=1, source_target_pairs={{0,2},{1,3},{2,0},{3,1},{4,6},{5,7},{6,4},{7,5},{8,10},{9,11},{10,... | collective-permute-start | bytes 1966088 | tf_op jit(solution)/shard_map/ppermute | solution.py:55
  68.0 13.6 %collective-permute-start.11 = (bf16[640,512]{1,0:T(8,128)(2,1)}, bf16[640,512]{1,0:T(8,128)(2,1)}, u32[]{:S(2)}, u32[]{:S(2)}) collective-permute-start(bf16[640,512]{1,0:T(8,128)(2,1)} %collective-permute-done.10.refs_6_), channel_id=1, source_target_pairs={{0,1},{1,0},{2,3},{3,2},{4,5},{5,4},{6,7},{7,6},{8,9},{9,8},{10,11... | collective-permute-start | bytes 1966088 | tf_op jit(solution)/shard_map/ppermute | solution.py:55
  104.8 21.4 %collective-permute-start.12 = (f32[64,4096]{1,0:T(8,128)}, f32[64,4096]{1,0:T(8,128)}, u32[]{:S(2)}, u32[]{:S(2)}) collective-permute-start(f32[64,4096]{1,0:T(8,128)} %get-tuple-element.54), channel_id=1, source_target_pairs={{0,8},{8,0},{16,24},{24,16},{1,9},{9,1},{17,25},{25,17},{2,10},{10... | collective-permute-start | bytes 3145736 | tf_op jit(solution)/shard_map/ppermute | solution.py:354
  118.4 34.9 %collective-permute-start.13 = (f32[64,4096]{1,0:T(8,128)}, f32[64,4096]{1,0:T(8,128)S(1)}, u32[]{:S(2)}, u32[]{:S(2)}) collective-permute-start(f32[64,4096]{1,0:T(8,128)} %get-tuple-element.58), channel_id=1, source_target_pairs={{0,8},{8,0},{16,24},{24,16},{1,9},{9,1},{17,25},{25,17},{2,10},{10... | collective-permute-start | bytes 3145736 | tf_op jit(solution)/shard_map/ppermute | solution.py:354
  118.9 35.9 %all-to-all-start = ((f32[8,4,8192]{2,1,0:T(4,128)}), f32[8,4,8192]{2,1,0:T(4,128)S(1)}, u32[]{:S(2)}, u32[]{:S(2)}) async-start(f32[8,4,8192]{2,1,0:T(4,128)} %select_drafts.1), calls=%async_computation | async-start | bytes 2097152 | tf_op jit(solution)/shard_map/all_to_all | solution.py:370
  128.1 27.6 %collective-permute-start.14 = (f32[32,4096]{1,0:T(8,128)}, f32[32,4096]{1,0:T(8,128)S(1)}, u32[]{:S(2)}, u32[]{:S(2)}) collective-permute-start(f32[32,4096]{1,0:T(8,128)} %slice_add_fusion.1), channel_id=1, source_target_pairs={{0,16},{8,24},{16,0},{24,8},{1,17},{9,25},{17,1},{25,9},{2,18},{10... | collective-permute-start | bytes 1572872 | tf_op jit(solution)/shard_map/ppermute | solution.py:382
  154.3 27.3 %collective-permute-start.16 = (f32[32,4096]{1,0:T(8,128)}, f32[32,4096]{1,0:T(8,128)}, u32[]{:S(2)}, u32[]{:S(2)}) collective-permute-start(f32[32,4096]{1,0:T(8,128)} %slice_add_fusion), channel_id=1, source_target_pairs={{0,16},{8,24},{16,0},{24,8},{1,17},{9,25},{17,1},{25,9},{2,18},{10... | collective-permute-start | bytes 1572872 | tf_op jit(solution)/shard_map/ppermute | solution.py:382
  154.8 20.0 %collective-permute-start.15 = (f32[256,4096]{1,0:T(8,128)}, f32[256,4096]{1,0:T(8,128)}, u32[]{:S(2)}, u32[]{:S(2)}) collective-permute-start(f32[256,4096]{1,0:T(8,128)} %get-tuple-element.66), channel_id=1, source_target_pairs={{0,8},{8,0},{16,24},{24,16},{1,9},{9,1},{17,25},{25,17},{2,10},{10... | collective-permute-start | bytes 12582920 | tf_op jit(solution)/shard_map/ppermute | solution.py:354
  172.7 30.0 %collective-permute-start.20 = (f32[256,2048]{1,0:T(8,128)}, f32[256,2048]{1,0:T(8,128)S(1)}, u32[]{:S(2)}, u32[]{:S(2)}) collective-permute-start(f32[256,2048]{1,0:T(8,128)} %get-tuple-element.73), channel_id=1, source_target_pairs={{0,8},{8,0},{16,24},{24,16},{1,9},{9,1},{17,25},{25,17},{2,10},{10... | collective-permute-start | bytes 6291464 | tf_op jit(solution)/shard_map/ppermute | solution.py:354
  179.4 41.0 %collective-permute-start.22 = (s16[128,4224]{1,0:T(8,128)(2,1)}, s16[128,4224]{1,0:T(8,128)(2,1)}, u32[]{:S(2)}, u32[]{:S(2)}) collective-permute-start(s16[128,4224]{1,0:T(8,128)(2,1)} %encode.3), channel_id=1, source_target_pairs={{0,16},{8,24},{16,0},{24,8},{1,17},{9,25},{17,1},{25,9},{2,18},{10... | collective-permute-start | bytes 3244040 | tf_op jit(solution)/shard_map/ppermute | solution.py:406
  185.0 16.1 %collective-permute-start.17 = (f32[3,32]{1,0:T(4,128)S(1)}, f32[3,32]{1,0:T(4,128)S(1)}, u32[]{:S(2)}, u32[]{:S(2)}) collective-permute-start(f32[3,32]{1,0:T(4,128)S(1)} %pad_maximum_fusion.3), channel_id=1, source_target_pairs={{0,1},{1,0},{2,3},{3,2},{4,5},{5,4},{6,7},{7,6},{8,9},{9,8},{10,11... | collective-permute-start | bytes 1160 | tf_op jit(solution)/shard_map/ppermute | solution.py:38
  201.1 12.0 %collective-permute-start.21 = (f32[256,2048]{1,0:T(8,128)}, f32[256,2048]{1,0:T(8,128)S(1)}, u32[]{:S(2)}, u32[]{:S(2)}) collective-permute-start(f32[256,2048]{1,0:T(8,128)} %get-tuple-element.75), channel_id=1, source_target_pairs={{0,8},{8,0},{16,24},{24,16},{1,9},{9,1},{17,25},{25,17},{2,10},{10... | collective-permute-start | bytes 6291464 | tf_op jit(solution)/shard_map/ppermute | solution.py:354
  201.1 7.2 %collective-permute-start.18 = (f32[3,32]{1,0:T(4,128)S(1)}, f32[3,32]{1,0:T(4,128)S(1)}, u32[]{:S(2)}, u32[]{:S(2)}) collective-permute-start(f32[3,32]{1,0:T(4,128)S(1)} %pad_maximum_fusion.4), channel_id=1, source_target_pairs={{0,2},{1,3},{2,0},{3,1},{4,6},{5,7},{6,4},{7,5},{8,10},{9,11},{10,... | collective-permute-start | bytes 1160 | tf_op jit(solution)/shard_map/ppermute | solution.py:38
  207.9 18.2 %collective-permute-start.23 = (s16[128,2176]{1,0:T(8,128)(2,1)}, s16[128,2176]{1,0:T(8,128)(2,1)S(1)}, u32[]{:S(2)}, u32[]{:S(2)}) collective-permute-start(s16[128,2176]{1,0:T(8,128)(2,1)} %encode.4), channel_id=1, source_target_pairs={{0,16},{8,24},{16,0},{24,8},{1,17},{9,25},{17,1},{25,9},{2,18},{10... | collective-permute-start | bytes 1671176 | tf_op jit(solution)/shard_map/ppermute | solution.py:406
  218.2 16.6 %collective-permute-start.24 = (s16[128,2176]{1,0:T(8,128)(2,1)}, s16[128,2176]{1,0:T(8,128)(2,1)S(1)}, u32[]{:S(2)}, u32[]{:S(2)}) collective-permute-start(s16[128,2176]{1,0:T(8,128)(2,1)} %encode.5), channel_id=1, source_target_pairs={{0,16},{8,24},{16,0},{24,8},{1,17},{9,25},{17,1},{25,9},{2,18},{10... | collective-permute-start | bytes 1671176 | tf_op jit(solution)/shard_map/ppermute | solution.py:406
  (30 other events, 342.5 us)

commit v5 on v4

--- a/solution.py
+++ b/solution.py
@@ -10,7 +10,7 @@
 EPS = 1e-05
 FIRST_PARTS = (2, 2)
 REST_PARTS = (2, 1, 1)
-ROWS = 32
+ROWS = 64
 TILES = 1024, 512
 VMEM_LIMIT = 56 * 1024 * 1024
 F32 = jnp.float32

time: 257 us -> 253 us (0.984)
  Pallas kernels: 125 us -> 118 us
  waiting for transfers between devices: 57.1 us -> 60.8 us
    pallas_call x3, Pallas kernels: 13.2 us -> 9.36 us  [finish_others(): pl.pallas_call(functools.partial(finish_others_kernel, len(codeds)), out_...]
    ppermute x3, waiting for transfers between devices: 1.26 us -> 4.9 us  [send_others(): far.append(lax.ppermute(coded, 'dp', y_pairs(k)))]
    pallas_call x3, Pallas kernels: 12.3 us -> 8.73 us  [encode(): pl.pallas_call(encode_kernel, out_shape=jax.ShapeDtypeStruct((count, widt...]
  transfers between devices with their start and end apart: 29 -> 29, of which waited for: 11 -> 11; matrix products, arithmetic and copies ran while one was open for 9% -> 9% of each run, Pallas kernels for 38% -> 36%
where the time goes in v5:
time: 253 us; the launch traced here: 252 us
  Pallas kernels  118 us (47%)
  waiting for transfers between devices  60.8 us (24%)
  starting transfers between devices  40 us (16%)
  local copies, waits for them, and re-layouts  20.2 us (8%)
  other arithmetic  12.1 us (5%)
    pallas_call x5, Pallas kernels, head(): pl.pallas_call(head_kernel, out_shape=(half, half), grid=(width // tile,)...  78.9 us
    ppermute x7, waiting for transfers between devices, step(): return lax.ppermute(value, 'tensor', [(i, i ^ bits) for i in range(count)])  30.5 us
    ppermute x2, waiting for transfers between devices, shards(): lax.ppermute(small, 'tensor', [(i, i ^ bit) for i in range(n_tensor)])  14 us
    ppermute x7, starting transfers between devices, step(): return lax.ppermute(value, 'tensor', [(i, i ^ bits) for i in range(count)])  11.4 us
    ppermute x6, waiting for transfers between devices, tree_merge(): other = lax.ppermute(stats, axis, [(i, i ^ bit) for i in range(count)])  10.3 us
    ppermute x6, starting transfers between devices, tree_merge(): other = lax.ppermute(stats, axis, [(i, i ^ bit) for i in range(count)])  9.72 us
    pallas_call x1, Pallas kernels, prepare(): pl.pallas_call(functools.partial(prepare_kernel, len(pieces)), out_shape=...  9.64 us
    pallas_call x3, Pallas kernels, finish_others(): pl.pallas_call(functools.partial(finish_others_kernel, len(codeds)), out_...  9.36 us
  transfers between devices with their start and end apart: 29, of which 11 were waited for; matrix products, arithmetic and copies ran while one was open for 9% of the time, Pallas kernels for 36%

profile of v5, /device:TPU:0, one launch (start us, length us, event | category | flops | bytes accessed | tf_op | source)
XLA Modules:
  0.0 251.7 jit_solution(4577391543298750849)
XLA Ops:
  0.6 4.1 %collective-permute-start.2 = (bf16[640,512]{1,0:T(8,128)(2,1)}, bf16[640,512]{1,0:T(8,128)(2,1)S(1)}, u32[]{:S(2)}, u32[]{:S(2)}) collective-permute-start(bf16[640,512]{1,0:T(8,128)(2,1)} %refs_0_.1), channel_id=1, source_target_pairs={{0,4},{1,5},{2,6},{3,7},{4,0},{5,1},{6,2},{7,3},{8,12},{9,13},{10,... | collective-permute-start | bytes 1966088 | tf_op jit(solution)/shard_map/ppermute | solution.py:55
  17.4 6.4 %select_drafts.1 = f32[8,4,8192]{2,1,0:T(4,128)} custom-call(s32[4]{0:T(128)} %dynamic_slice.4.at, f32[20,65536]{1,0:T(8,128)} %drafts.1), custom_call_target="tpu_custom_call" | custom-call | flops 1024 | bytes 1024 | tf_op jit(solution)/shard_map/select_drafts/pallas_call | solution.py:247
  23.7 10.7 %collective-permute-done.1 = f32[40,128]{1,0:T(8,128)S(1)} collective-permute-done((f32[40,128]{1,0:T(8,128)S(1)}, f32[40,128]{1,0:T(8,128)S(1)}, u32[]{:S(2)}, u32[]{:S(2)}) %collective-permute-start.1) | collective-permute-done | bytes 20512 | tf_op jit(solution)/shard_map/ppermute | solution.py:299
  36.0 3.2 %collective-permute-done.3 = f32[40,128]{1,0:T(8,128)S(1)} collective-permute-done((f32[40,128]{1,0:T(8,128)S(1)}, f32[40,128]{1,0:T(8,128)S(1)}, u32[]{:S(2)}, u32[]{:S(2)}) %collective-permute-start.3) | collective-permute-done | bytes 20512 | tf_op jit(solution)/shard_map/ppermute | solution.py:299
  45.4 11.6 %collective-permute-done.8.refs_4_ = bf16[640,512]{1,0:T(8,128)(2,1)S(1)} collective-permute-done((bf16[640,512]{1,0:T(8,128)(2,1)S(1)}, bf16[640,512]{1,0:T(8,128)(2,1)S(1)}, u32[]{:S(2)}, u32[]{:S(2)}) %collective-permute-start.8) | collective-permute-done | bytes 655392 | tf_op jit(solution)/shard_map/ppermute | solution.py:55
  59.1 8.9 %collective-permute-done.9.refs_5_ = bf16[640,512]{1,0:T(8,128)(2,1)S(1)} collective-permute-done((bf16[640,512]{1,0:T(8,128)(2,1)S(1)}, bf16[640,512]{1,0:T(8,128)(2,1)S(1)}, u32[]{:S(2)}, u32[]{:S(2)}) %collective-permute-start.9) | collective-permute-done | bytes 655392 | tf_op jit(solution)/shard_map/ppermute | solution.py:55
  71.5 10.0 %collective-permute-done.11.refs_7_ = bf16[640,512]{1,0:T(8,128)(2,1)} collective-permute-done((bf16[640,512]{1,0:T(8,128)(2,1)}, bf16[640,512]{1,0:T(8,128)(2,1)}, u32[]{:S(2)}, u32[]{:S(2)}) %collective-permute-start.11) | collective-permute-done | bytes 655392 | tf_op jit(solution)/shard_map/ppermute | solution.py:55
  81.6 9.6 %prepare.1 = (bf16[128,4096]{1,0:T(8,128)(2,1)}, bf16[512,4096]{1,0:T(8,128)(2,1)}) custom-call(s32[8]{0:T(128)} %stack.96.place, s32[640,1]{1,0:T(8,128)} %copy.66.order, f32[640,1]{1,0:T(8,128)} %bitcast.97, f32[8,512]{1,0:T(8,128)} %reshape.172.gain, bf16[640,512]{1,0:T(8,128)(2,1)} %refs_0_.1, bf16[640,512]{1,0:T(8,128)(2,1)} %copy-done.6, ...), custom_call_target="tpu_custom_call" | custom-call | flops 1024 | bytes 1024 | tf_op jit(solution)/shard_map/prepare/pallas_call | solution.py:95
  91.2 13.6 %head.5 = (f32[64,4096]{1,0:T(8,128)}, f32[64,4096]{1,0:T(8,128)}) custom-call(bf16[128,4096]{1,0:T(8,128)(2,1)} %get-tuple-element.50.x, bf16[4096,8192]{1,0:T(8,128)(2,1)} %w.9), custom_call_target="tpu_custom_call" | custom-call | flops 34359738368 | bytes 33554432 | tf_op jit(solution)/shard_map/head/pallas_call | solution.py:121
  104.8 13.6 %head.6 = (f32[64,4096]{1,0:T(8,128)}, f32[64,4096]{1,0:T(8,128)}) custom-call(bf16[128,4096]{1,0:T(8,128)(2,1)} %get-tuple-element.50.x, bf16[4096,8192]{1,0:T(8,128)(2,1)} %w.9), custom_call_target="tpu_custom_call" | custom-call | flops 34359738368 | bytes 33554432 | tf_op jit(solution)/shard_map/head/pallas_call | solution.py:121
  118.9 7.3 %all-to-all-start = ((f32[8,4,8192]{2,1,0:T(4,128)}), f32[8,4,8192]{2,1,0:T(4,128)S(1)}, u32[]{:S(2)}, u32[]{:S(2)}) async-start(f32[8,4,8192]{2,1,0:T(4,128)} %select_drafts.1), calls=%async_computation | async-start | bytes 2097152 | tf_op jit(solution)/shard_map/all_to_all | solution.py:370
  129.6 23.7 %head.7 = (f32[256,4096]{1,0:T(8,128)}, f32[256,4096]{1,0:T(8,128)}) custom-call(bf16[512,4096]{1,0:T(8,128)(2,1)} %get-tuple-element.70.x, bf16[4096,8192]{1,0:T(8,128)(2,1)} %w.9), custom_call_target="tpu_custom_call" | custom-call | flops 137438953472 | bytes 33554432 | tf_op jit(solution)/shard_map/head/pallas_call | solution.py:121
  158.7 14.0 %head.8 = (f32[256,2048]{1,0:T(8,128)}, f32[256,2048]{1,0:T(8,128)}) custom-call(bf16[512,4096]{1,0:T(8,128)(2,1)} %get-tuple-element.70.x, bf16[4096,8192]{1,0:T(8,128)(2,1)} %w.9), custom_call_target="tpu_custom_call" | custom-call | flops 68719476736 | bytes 16777216 | tf_op jit(solution)/shard_map/head/pallas_call | solution.py:121
  174.8 3.6 %encode.3 = s16[128,4224]{1,0:T(8,128)(2,1)} custom-call(f32[256,4096]{1,0:T(8,128)} %get-tuple-element.65.keep, f32[256,4096]{1,0:T(8,128)} %collective-permute-done.15.came), custom_call_target="tpu_custom_call" | custom-call | flops 1024 | bytes 1024 | tf_op jit(solution)/shard_map/encode/pallas_call | solution.py:163
  186.1 14.0 %head.9 = (f32[256,2048]{1,0:T(8,128)}, f32[256,2048]{1,0:T(8,128)}) custom-call(bf16[512,4096]{1,0:T(8,128)(2,1)} %get-tuple-element.70.x, bf16[4096,8192]{1,0:T(8,128)(2,1)} %w.9), custom_call_target="tpu_custom_call" | custom-call | flops 68719476736 | bytes 16777216 | tf_op jit(solution)/shard_map/head/pallas_call | solution.py:121
  203.0 2.6 %encode.4 = s16[128,2176]{1,0:T(8,128)(2,1)} custom-call(f32[256,2048]{1,0:T(8,128)} %get-tuple-element.72.keep, f32[256,2048]{1,0:T(8,128)} %copy-done), custom_call_target="tpu_custom_call" | custom-call | flops 1024 | bytes 1024 | tf_op jit(solution)/shard_map/encode/pallas_call | solution.py:163
  206.1 2.4 collective-permute-start.19
  212.1 2.6 %encode.5 = s16[128,2176]{1,0:T(8,128)(2,1)} custom-call(f32[256,2048]{1,0:T(8,128)} %get-tuple-element.74.keep, f32[256,2048]{1,0:T(8,128)} %copy-done.1), custom_call_target="tpu_custom_call" | custom-call | flops 1024 | bytes 1024 | tf_op jit(solution)/shard_map/encode/pallas_call | solution.py:163
  216.9 3.8 %finish_others.3 = f32[128,128]{1,0:T(8,128)} custom-call(s32[128,1]{1,0:T(8,128)} %copy.73.ids, f32[256,4096]{1,0:T(8,128)} %get-tuple-element.65.keep, f32[256,4096]{1,0:T(8,128)} %collective-permute-done.15.came, s16[128,4224]{1,0:T(8,128)(2,1)} %collective-permute-done.22.refs_0_), custom_call_target="tpu_custom_call" | custom-call | flops 1024 | bytes 1024 | tf_op jit(solution)/shard_map/finish_others/pallas_call | solution.py:226
  222.3 2.8 %finish_others.4 = f32[128,128]{1,0:T(8,128)} custom-call(s32[128,1]{1,0:T(8,128)} %copy.74.ids, f32[256,2048]{1,0:T(8,128)} %get-tuple-element.72.keep, f32[256,2048]{1,0:T(8,128)} %copy-done, s16[128,2176]{1,0:T(8,128)(2,1)} %copy-done.11), custom_call_target="tpu_custom_call" | custom-call | flops 1024 | bytes 1024 | tf_op jit(solution)/shard_map/finish_others/pallas_call | solution.py:226
  227.6 4.9 %collective-permute-done.24.refs_0_ = s16[128,2176]{1,0:T(8,128)(2,1)S(1)} collective-permute-done((s16[128,2176]{1,0:T(8,128)(2,1)}, s16[128,2176]{1,0:T(8,128)(2,1)S(1)}, u32[]{:S(2)}, u32[]{:S(2)}) %collective-permute-start.24) | collective-permute-done | bytes 557088 | tf_op jit(solution)/shard_map/ppermute | solution.py:406
  233.3 2.8 %finish_others.5 = f32[128,128]{1,0:T(8,128)} custom-call(s32[128,1]{1,0:T(8,128)} %copy.75.ids, f32[256,2048]{1,0:T(8,128)} %get-tuple-element.74.keep, f32[256,2048]{1,0:T(8,128)} %copy-done.1, s16[128,2176]{1,0:T(8,128)(2,1)} %copy-done.12), custom_call_target="tpu_custom_call" | custom-call | flops 1024 | bytes 1024 | tf_op jit(solution)/shard_map/finish_others/pallas_call | solution.py:226
  238.2 3.0 %collective-permute-done.25 = f32[3,160]{1,0:T(4,128)S(1)} collective-permute-done((f32[3,160]{1,0:T(4,128)S(1)}, f32[3,160]{1,0:T(4,128)S(1)}, u32[]{:S(2)}, u32[]{:S(2)}) %collective-permute-start.25) | collective-permute-done | bytes 1952 | tf_op jit(solution)/shard_map/ppermute | solution.py:38
  241.9 3.0 %collective-permute-done.26 = f32[3,160]{1,0:T(4,128)S(1)} collective-permute-done((f32[3,160]{1,0:T(4,128)S(1)}, f32[3,160]{1,0:T(4,128)S(1)}, u32[]{:S(2)}, u32[]{:S(2)}) %collective-permute-start.26) | collective-permute-done | bytes 1952 | tf_op jit(solution)/shard_map/ppermute | solution.py:38
  (207 shorter events, 68.4 us)
Async XLA Ops:
  0.6 33.8 %collective-permute-start.2 = (bf16[640,512]{1,0:T(8,128)(2,1)}, bf16[640,512]{1,0:T(8,128)(2,1)S(1)}, u32[]{:S(2)}, u32[]{:S(2)}) collective-permute-start(bf16[640,512]{1,0:T(8,128)(2,1)} %refs_0_.1), channel_id=1, source_target_pairs={{0,4},{1,5},{2,6},{3,7},{4,0},{5,1},{6,2},{7,3},{8,12},{9,13},{10,... | collective-permute-start | bytes 1966088 | tf_op jit(solution)/shard_map/ppermute | solution.py:55
  4.7 34.5 %collective-permute-start.6 = (bf16[640,512]{1,0:T(8,128)(2,1)}, bf16[640,512]{1,0:T(8,128)(2,1)S(1)}, u32[]{:S(2)}, u32[]{:S(2)}) collective-permute-start(bf16[640,512]{1,0:T(8,128)(2,1)} %refs_0_.1), channel_id=1, source_target_pairs={{0,2},{1,3},{2,0},{3,1},{4,6},{5,7},{6,4},{7,5},{8,10},{9,11},{10,... | collective-permute-start | bytes 1966088 | tf_op jit(solution)/shard_map/ppermute | solution.py:55
  8.5 5.7 %collective-permute-start = (f32[40,128]{1,0:T(8,128)S(1)}, f32[40,128]{1,0:T(8,128)S(1)}, u32[]{:S(2)}, u32[]{:S(2)}) collective-permute-start(f32[40,128]{1,0:T(8,128)S(1)} %fusion.1), channel_id=1, source_target_pairs={{0,1},{1,0},{2,3},{3,2},{4,5},{5,4},{6,7},{7,6},{8,9},{9,8},{10,11... | collective-permute-start | bytes 61448 | tf_op jit(solution)/shard_map/ppermute | solution.py:288
  14.3 20.2 %collective-permute-start.1 = (f32[40,128]{1,0:T(8,128)S(1)}, f32[40,128]{1,0:T(8,128)S(1)}, u32[]{:S(2)}, u32[]{:S(2)}) collective-permute-start(f32[40,128]{1,0:T(8,128)S(1)} %fusion.18), channel_id=1, source_target_pairs={{0,2},{1,3},{2,0},{3,1},{4,6},{5,7},{6,4},{7,5},{8,10},{9,11},{10,... | collective-permute-start | bytes 61448 | tf_op jit(solution)/shard_map/ppermute | solution.py:299
  14.8 24.5 %collective-permute-start.7 = (bf16[640,512]{1,0:T(8,128)(2,1)}, bf16[640,512]{1,0:T(8,128)(2,1)S(1)}, u32[]{:S(2)}, u32[]{:S(2)}) collective-permute-start(bf16[640,512]{1,0:T(8,128)(2,1)} %refs_0_.1), channel_id=1, source_target_pairs={{0,1},{1,0},{2,3},{3,2},{4,5},{5,4},{6,7},{7,6},{8,9},{9,8},{10,11... | collective-permute-start | bytes 1966088 | tf_op jit(solution)/shard_map/ppermute | solution.py:55
  34.5 4.7 %collective-permute-start.3 = (f32[40,128]{1,0:T(8,128)S(1)}, f32[40,128]{1,0:T(8,128)S(1)}, u32[]{:S(2)}, u32[]{:S(2)}) collective-permute-start(f32[40,128]{1,0:T(8,128)S(1)} %fusion.23), channel_id=1, source_target_pairs={{0,4},{1,5},{2,6},{3,7},{4,0},{5,1},{6,2},{7,3},{8,12},{9,13},{10,... | collective-permute-start | bytes 61448 | tf_op jit(solution)/shard_map/ppermute | solution.py:299
  39.3 17.7 %collective-permute-start.8 = (bf16[640,512]{1,0:T(8,128)(2,1)S(1)}, bf16[640,512]{1,0:T(8,128)(2,1)S(1)}, u32[]{:S(2)}, u32[]{:S(2)}) collective-permute-start(bf16[640,512]{1,0:T(8,128)(2,1)S(1)} %collective-permute-done.6.refs_2_), channel_id=1, source_target_pairs={{0,1},{1,0},{2,3},{3,2},{4,5},{5,4},{6,7},{7,6},{8,9},{9,8},{10,11... | collective-permute-start | bytes 1966088 | tf_op jit(solution)/shard_map/ppermute | solution.py:55
  42.1 16.4 %collective-permute-start.5 = (f32[8,128]{1,0:T(8,128)S(1)}, f32[8,128]{1,0:T(8,128)S(1)}, u32[]{:S(2)}, u32[]{:S(2)}) collective-permute-start(f32[8,128]{1,0:T(8,128)S(1)} %fusion.22), channel_id=1, source_target_pairs={{0,16},{8,24},{16,0},{24,8},{1,17},{9,25},{17,1},{25,9},{2,18},{10... | collective-permute-start | bytes 12296 | tf_op jit(solution)/shard_map/ppermute | solution.py:23
  44.3 23.7 %collective-permute-start.9 = (bf16[640,512]{1,0:T(8,128)(2,1)S(1)}, bf16[640,512]{1,0:T(8,128)(2,1)S(1)}, u32[]{:S(2)}, u32[]{:S(2)}) collective-permute-start(bf16[640,512]{1,0:T(8,128)(2,1)S(1)} %collective-permute-done.2.refs_1_), channel_id=1, source_target_pairs={{0,1},{1,0},{2,3},{3,2},{4,5},{5,4},{6,7},{7,6},{8,9},{9,8},{10,11... | collective-permute-start | bytes 1966088 | tf_op jit(solution)/shard_map/ppermute | solution.py:55
  57.0 11.0 %collective-permute-start.10 = (bf16[640,512]{1,0:T(8,128)(2,1)S(1)}, bf16[640,512]{1,0:T(8,128)(2,1)}, u32[]{:S(2)}, u32[]{:S(2)}) collective-permute-start(bf16[640,512]{1,0:T(8,128)(2,1)S(1)} %collective-permute-done.2.refs_1_), channel_id=1, source_target_pairs={{0,2},{1,3},{2,0},{3,1},{4,6},{5,7},{6,4},{7,5},{8,10},{9,11},{10,... | collective-permute-start | bytes 1966088 | tf_op jit(solution)/shard_map/ppermute | solution.py:55
  68.0 13.6 %collective-permute-start.11 = (bf16[640,512]{1,0:T(8,128)(2,1)}, bf16[640,512]{1,0:T(8,128)(2,1)}, u32[]{:S(2)}, u32[]{:S(2)}) collective-permute-start(bf16[640,512]{1,0:T(8,128)(2,1)} %collective-permute-done.10.refs_6_), channel_id=1, source_target_pairs={{0,1},{1,0},{2,3},{3,2},{4,5},{5,4},{6,7},{7,6},{8,9},{9,8},{10,11... | collective-permute-start | bytes 1966088 | tf_op jit(solution)/shard_map/ppermute | solution.py:55
  104.8 21.4 %collective-permute-start.12 = (f32[64,4096]{1,0:T(8,128)}, f32[64,4096]{1,0:T(8,128)}, u32[]{:S(2)}, u32[]{:S(2)}) collective-permute-start(f32[64,4096]{1,0:T(8,128)} %get-tuple-element.54), channel_id=1, source_target_pairs={{0,8},{8,0},{16,24},{24,16},{1,9},{9,1},{17,25},{25,17},{2,10},{10... | collective-permute-start | bytes 3145736 | tf_op jit(solution)/shard_map/ppermute | solution.py:354
  118.4 34.9 %collective-permute-start.13 = (f32[64,4096]{1,0:T(8,128)}, f32[64,4096]{1,0:T(8,128)S(1)}, u32[]{:S(2)}, u32[]{:S(2)}) collective-permute-start(f32[64,4096]{1,0:T(8,128)} %get-tuple-element.58), channel_id=1, source_target_pairs={{0,8},{8,0},{16,24},{24,16},{1,9},{9,1},{17,25},{25,17},{2,10},{10... | collective-permute-start | bytes 3145736 | tf_op jit(solution)/shard_map/ppermute | solution.py:354
  118.9 35.9 %all-to-all-start = ((f32[8,4,8192]{2,1,0:T(4,128)}), f32[8,4,8192]{2,1,0:T(4,128)S(1)}, u32[]{:S(2)}, u32[]{:S(2)}) async-start(f32[8,4,8192]{2,1,0:T(4,128)} %select_drafts.1), calls=%async_computation | async-start | bytes 2097152 | tf_op jit(solution)/shard_map/all_to_all | solution.py:370
  128.1 27.6 %collective-permute-start.14 = (f32[32,4096]{1,0:T(8,128)}, f32[32,4096]{1,0:T(8,128)S(1)}, u32[]{:S(2)}, u32[]{:S(2)}) collective-permute-start(f32[32,4096]{1,0:T(8,128)} %slice_add_fusion.1), channel_id=1, source_target_pairs={{0,16},{8,24},{16,0},{24,8},{1,17},{9,25},{17,1},{25,9},{2,18},{10... | collective-permute-start | bytes 1572872 | tf_op jit(solution)/shard_map/ppermute | solution.py:382
  154.3 26.3 %collective-permute-start.16 = (f32[32,4096]{1,0:T(8,128)}, f32[32,4096]{1,0:T(8,128)}, u32[]{:S(2)}, u32[]{:S(2)}) collective-permute-start(f32[32,4096]{1,0:T(8,128)} %slice_add_fusion), channel_id=1, source_target_pairs={{0,16},{8,24},{16,0},{24,8},{1,17},{9,25},{17,1},{25,9},{2,18},{10... | collective-permute-start | bytes 1572872 | tf_op jit(solution)/shard_map/ppermute | solution.py:382
  154.8 20.0 %collective-permute-start.15 = (f32[256,4096]{1,0:T(8,128)}, f32[256,4096]{1,0:T(8,128)}, u32[]{:S(2)}, u32[]{:S(2)}) collective-permute-start(f32[256,4096]{1,0:T(8,128)} %get-tuple-element.66), channel_id=1, source_target_pairs={{0,8},{8,0},{16,24},{24,16},{1,9},{9,1},{17,25},{25,17},{2,10},{10... | collective-permute-start | bytes 12582920 | tf_op jit(solution)/shard_map/ppermute | solution.py:354
  172.7 28.9 %collective-permute-start.20 = (f32[256,2048]{1,0:T(8,128)}, f32[256,2048]{1,0:T(8,128)S(1)}, u32[]{:S(2)}, u32[]{:S(2)}) collective-permute-start(f32[256,2048]{1,0:T(8,128)} %get-tuple-element.73), channel_id=1, source_target_pairs={{0,8},{8,0},{16,24},{24,16},{1,9},{9,1},{17,25},{25,17},{2,10},{10... | collective-permute-start | bytes 6291464 | tf_op jit(solution)/shard_map/ppermute | solution.py:354
  178.4 38.5 %collective-permute-start.22 = (s16[128,4224]{1,0:T(8,128)(2,1)}, s16[128,4224]{1,0:T(8,128)(2,1)}, u32[]{:S(2)}, u32[]{:S(2)}) collective-permute-start(s16[128,4224]{1,0:T(8,128)(2,1)} %encode.3), channel_id=1, source_target_pairs={{0,16},{8,24},{16,0},{24,8},{1,17},{9,25},{17,1},{25,9},{2,18},{10... | collective-permute-start | bytes 3244040 | tf_op jit(solution)/shard_map/ppermute | solution.py:406
  184.0 16.1 %collective-permute-start.17 = (f32[3,32]{1,0:T(4,128)S(1)}, f32[3,32]{1,0:T(4,128)S(1)}, u32[]{:S(2)}, u32[]{:S(2)}) collective-permute-start(f32[3,32]{1,0:T(4,128)S(1)} %pad_maximum_fusion.3), channel_id=1, source_target_pairs={{0,1},{1,0},{2,3},{3,2},{4,5},{5,4},{6,7},{7,6},{8,9},{9,8},{10,11... | collective-permute-start | bytes 1160 | tf_op jit(solution)/shard_map/ppermute | solution.py:38
  200.0 10.7 %collective-permute-start.21 = (f32[256,2048]{1,0:T(8,128)}, f32[256,2048]{1,0:T(8,128)S(1)}, u32[]{:S(2)}, u32[]{:S(2)}) collective-permute-start(f32[256,2048]{1,0:T(8,128)} %get-tuple-element.75), channel_id=1, source_target_pairs={{0,8},{8,0},{16,24},{24,16},{1,9},{9,1},{17,25},{25,17},{2,10},{10... | collective-permute-start | bytes 6291464 | tf_op jit(solution)/shard_map/ppermute | solution.py:354
  200.1 6.0 %collective-permute-start.18 = (f32[3,32]{1,0:T(4,128)S(1)}, f32[3,32]{1,0:T(4,128)S(1)}, u32[]{:S(2)}, u32[]{:S(2)}) collective-permute-start(f32[3,32]{1,0:T(4,128)S(1)} %pad_maximum_fusion.4), channel_id=1, source_target_pairs={{0,2},{1,3},{2,0},{3,1},{4,6},{5,7},{6,4},{7,5},{8,10},{9,11},{10,... | collective-permute-start | bytes 1160 | tf_op jit(solution)/shard_map/ppermute | solution.py:38
  205.6 15.9 %collective-permute-start.23 = (s16[128,2176]{1,0:T(8,128)(2,1)}, s16[128,2176]{1,0:T(8,128)(2,1)S(1)}, u32[]{:S(2)}, u32[]{:S(2)}) collective-permute-start(s16[128,2176]{1,0:T(8,128)(2,1)} %encode.4), channel_id=1, source_target_pairs={{0,16},{8,24},{16,0},{24,8},{1,17},{9,25},{17,1},{25,9},{2,18},{10... | collective-permute-start | bytes 1671176 | tf_op jit(solution)/shard_map/ppermute | solution.py:406
  214.6 17.8 %collective-permute-start.24 = (s16[128,2176]{1,0:T(8,128)(2,1)}, s16[128,2176]{1,0:T(8,128)(2,1)S(1)}, u32[]{:S(2)}, u32[]{:S(2)}) collective-permute-start(s16[128,2176]{1,0:T(8,128)(2,1)} %encode.5), channel_id=1, source_target_pairs={{0,16},{8,24},{16,0},{24,8},{1,17},{9,25},{17,1},{25,9},{2,18},{10... | collective-permute-start | bytes 1671176 | tf_op jit(solution)/shard_map/ppermute | solution.py:406
  (30 other events, 334.0 us)
